TPU v7x, 32 devices: a whole 2x2x4 slice. The times are simulated.
32 devices in a mesh: aux: 4 (over z), ao: 8 (over y, x, core).
Axes of the slice: x: 2, y: 2, z: 4, core: 2. Of those that a mesh axis runs over, the one named last changes fastest.
Arguments:
- three_center: bfloat16 [512, 3, 3072], P('aux', None, 'ao'), may hold values from -6 to 6
- occ_green: bfloat16 [2, 3, 3], replicated, may hold values from -3.5 to 3.5
- virt_band: bfloat16 [2, 3072, 384], P(None, 'ao'), may hold values from -0.3125 to 0.3125
- tile_mask: int32 [4, 24], P('aux', 'ao'), may hold values 0 or 1
Outputs:
- polar: float32 [2, 512, 512], P(None, 'aux', 'ao')
All inputs are finite; a program needn't handle non-finite values. No bound on the sum of `tile_mask` on one device may be relied on, other than what follows from the above.
Results may differ from a plain program's by a relative error of at most 0.0041.
Values may be sent and summed in bfloat16 or wider, within the bound.
No kernel may reach another device: no remote copies, remote signals or barrier semaphores. Data moves between devices by JAX's collectives and lax.ppermute only.
A program may use at most 64 MiB of HBM per device.

v0:
```python
import math

import jax
import jax.numpy as jnp
from jax import lax
from jax.sharding import PartitionSpec as P


def padded(x, sides, width):
    for axis, dim in sides:
        devices, length = (lax.axis_size(axis), x.shape[dim])
        up = [(i, (i + 1) % devices) for i in range(devices - 1)]
        down = [(j, i) for i, j in up]
        last = lax.slice_in_dim(x, length - width, length, axis=dim)
        first = lax.slice_in_dim(x, 0, width, axis=dim)
        before = lax.ppermute(last, axis, up)
        after = lax.ppermute(first, axis, down)
        x = jnp.concatenate([before, x, after], axis=dim)
    return x


def dress(extended, virt_band, tile):
    times, rows, window, width = extended.shape
    count = width // tile - 2
    tiled = extended.reshape(times, rows, window, count + 2, tile)
    windows = jnp.concatenate(
        [tiled[:, :, :, :-2, :], tiled[:, :, :, 1:-1, :], tiled[:, :, :, 2:, :]], axis=4
    )
    band = virt_band.reshape(times, count, tile, 3 * tile)
    dressed = jnp.einsum("tplsj,tsij->tplsi", windows, band, preferred_element_type=jnp.float32)
    return dressed.astype(jnp.bfloat16).reshape(times, rows, window * count * tile)


def body(three_center, occ_green, virt_band, tile_mask):
    aux_rows, window, ao_cols = three_center.shape
    tile = virt_band.shape[2] // 3
    mask = tile_mask.astype(jnp.bfloat16)
    screened = (
        three_center.reshape(aux_rows // tile, tile, window, ao_cols // tile, tile)
        * mask[:, None, None, :, None]
    ).reshape(aux_rows, window, ao_cols)
    product = jnp.einsum(
        "tlm,pmn->tpln", occ_green, screened, preferred_element_type=jnp.float32
    ).astype(jnp.bfloat16)
    extended = padded(product, (("ao", 3),), tile)
    dressed = dress(extended, virt_band, tile)
    factor = 1.0 / math.sqrt(window * ao_cols * lax.axis_size("ao"))
    piece = lax.all_gather(screened, "aux", axis=0, tiled=True)
    others = piece.reshape(piece.shape[0], window * ao_cols)
    partial_terms = (
        jnp.einsum("tpk,qk->tpq", dressed, others, preferred_element_type=jnp.float32) * factor
    )
    return lax.psum_scatter(partial_terms, "ao", scatter_dimension=2, tiled=True)


def solution(mesh):
    in_specs = (P("aux", None, "ao"), P(), P(None, "ao", None), P("aux", "ao"))
    out_specs = P(None, "aux", "ao")
    return jax.shard_map(body, mesh=mesh, in_specs=in_specs, out_specs=out_specs, check_vma=False)
```

profile of v0, /device:TPU:0, one launch (start us, length us, event | category | flops | bytes accessed | tf_op | source)
XLA Modules:
  0.0 86.4 jit_solution(1145314169718154440)
XLA Ops:
  6.5 0.0 copy-start
  6.5 0.0 copy-start.1
  6.5 0.0 all-gather.2.cloned.1.call-start
  6.5 1.2 %copy.11 = bf16[128,3,384]{0,2,1:T(8,128)(2,1)S(1)} copy(bf16[128,3,384]{2,0,1:T(8,128)(2,1)} %param.4) | data formatting | bytes 589824 | tf_op args[0]
  7.8 0.7 convert_bitcast_fusion
  8.4 0.1 broadcast_bitcast_fusion
  8.5 0.9 broadcast_multiply_fusion
  9.4 0.0 all-gather.2.cloned.1.call-update
  9.4 0.0 reduce-scatter.2.cloned.1.call-start
  9.5 0.1 fusion.22
  9.6 0.2 copy.21
  9.8 0.0 copy-done.1
  9.8 0.5 fusion.9
  10.4 0.2 fusion.17
  10.6 2.4 %collective-permute-start = (bf16[2,128,3,128]{3,2,0,1:T(4,128)(2,1)S(1)}, bf16[2,128,3,128]{3,2,0,1:T(4,128)(2,1)S(1)}, u32[]{:S(2)}, u32[]{:S(2)}) collective-permute-start(bf16[2,128,3,128]{3,2,0,1:T(4,128)(2,1)S(1)} %get-tuple-element.8), channel_id=1, source_target_pairs={{0,1},{1,2},{2,3},{3,4},{4,5},{5,6},{6,7},{8,9},{9,10},{10,11},{11... | collective-permute-start | bytes 589832 | tf_op jit(solution)/shard_map/ppermute | solution.py:16
  13.0 1.3 %collective-permute-start.1 = (bf16[2,128,3,128]{3,2,0,1:T(4,128)(2,1)S(1)}, bf16[2,128,3,128]{3,2,0,1:T(4,128)(2,1)S(1)}, u32[]{:S(2)}, u32[]{:S(2)}) collective-permute-start(bf16[2,128,3,128]{3,2,0,1:T(4,128)(2,1)S(1)} %get-tuple-element.9), channel_id=1, source_target_pairs={{1,0},{2,1},{3,2},{4,3},{5,4},{6,5},{7,6},{9,8},{10,9},{11,10},{12... | collective-permute-start | bytes 589832 | tf_op jit(solution)/shard_map/ppermute | solution.py:17
  14.3 0.0 collective-permute-done
  14.3 4.2 %collective-permute-done.1 = bf16[2,128,3,128]{3,2,0,1:T(4,128)(2,1)S(1)} collective-permute-done((bf16[2,128,3,128]{3,2,0,1:T(4,128)(2,1)S(1)}, bf16[2,128,3,128]{3,2,0,1:T(4,128)(2,1)S(1)}, u32[]{:S(2)}, u32[]{:S(2)}) %collective-permute-start.1) | collective-permute-done | bytes 196640 | tf_op jit(solution)/shard_map/ppermute | solution.py:17
  18.5 0.6 pad_maximum_fusion
  19.1 1.8 %copy.14 = bf16[2,128,3,640]{1,3,2,0:T(8,128)(2,1)S(1)} copy(bf16[2,128,3,640]{3,2,0,1:T(4,128)(2,1)S(1)} %pad_maximum_fusion) | data formatting | bytes 1966080 | tf_op jit(solution)/shard_map/concatenate | solution.py:18
  20.9 0.4 fusion.16
  21.3 0.3 copy.28
  21.6 0.3 copy.29
  22.0 0.3 copy.30
  22.3 0.0 copy-done
  22.3 0.7 fusion.10
  23.0 21.0 %all-gather.2.cloned.1.call-done = bf16[512,3,384]{0,2,1:T(8,128)(2,1)} async-done(((bf16[128,3,384]{0,2,1:T(8,128)(2,1)}), bf16[512,3,384]{0,2,1:T(8,128)(2,1)}) %all-gather.2.cloned.1.call-update) | async-done | bytes 1179664 | tf_op jit(solution)/shard_map/all_gather | solution.py:48
  44.0 2.7 %convolution_multiply_fusion = f32[2,128,512]{1,2,0:T(8,128)} fusion(bf16[2,128,1152]{1,2,0:T(8,128)(2,1)S(1)} %bitcast.29, bf16[512,1152,1]{0,1,2:T(8,128)(2,1)} %bitcast.30), kind=kOutput, calls=%fused_computation.11 | convolution fusion | flops 302120960 | bytes 2293760 | tf_op jit(solution)/shard_map/tpk,qk->tpq/dot_general | solution.py:51
  46.7 0.0 reduce-scatter.2.cloned.1.call-update
  46.7 32.8 %reduce-scatter.2.cloned.1.call-done = f32[2,128,64]{1,2,0:T(8,128)} async-done(((f32[2,128,512]{1,2,0:T(8,128)}), f32[2,128,64]{1,2,0:T(8,128)}) %reduce-scatter.2.cloned.1.call-update) | async-done | bytes 65552 | tf_op jit(solution)/shard_map/reduce_scatter | solution.py:53
  (1 shorter events, 0.0 us)
Async XLA Ops:
  6.5 15.7 %copy-start = (bf16[2,384,384]{2,1,0:T(8,128)(2,1)S(1)}, bf16[2,384,384]{2,1,0:T(8,128)(2,1)}, u32[]{:S(2)}) copy-start(bf16[2,384,384]{2,1,0:T(8,128)(2,1)} %param.6) | copy-start | bytes 1769476
  6.5 3.3 %copy-start.1 = (bf16[2,3,3]{2,0,1:T(2,128)(2,1)S(1)}, bf16[2,3,3]{2,0,1:T(2,128)(2,1)}, u32[]{:S(2)}) copy-start(bf16[2,3,3]{2,0,1:T(2,128)(2,1)} %param.5) | copy-start | bytes 112
  6.5 37.5 %all-gather.2.cloned.1.call-start = ((), (), s32[]{:S(2)}) async-start(), calls=%async_computation.1 | async-start | bytes 1474560 | tf_op jit(solution)/shard_map/all_gather | solution.py:48
  9.4 70.2 %reduce-scatter.2.cloned.1.call-start = ((), (), s32[]{:S(2)}) async-start(), calls=%async_computation.2 | async-start | bytes 589824 | tf_op jit(solution)/shard_map/reduce_scatter | solution.py:53
  10.6 3.7 %collective-permute-start = (bf16[2,128,3,128]{3,2,0,1:T(4,128)(2,1)S(1)}, bf16[2,128,3,128]{3,2,0,1:T(4,128)(2,1)S(1)}, u32[]{:S(2)}, u32[]{:S(2)}) collective-permute-start(bf16[2,128,3,128]{3,2,0,1:T(4,128)(2,1)S(1)} %get-tuple-element.8), channel_id=1, source_target_pairs={{0,1},{1,2},{2,3},{3,4},{4,5},{5,6},{6,7},{8,9},{9,10},{10,11},{11... | collective-permute-start | bytes 589832 | tf_op jit(solution)/shard_map/ppermute | solution.py:16
  13.0 5.5 %collective-permute-start.1 = (bf16[2,128,3,128]{3,2,0,1:T(4,128)(2,1)S(1)}, bf16[2,128,3,128]{3,2,0,1:T(4,128)(2,1)S(1)}, u32[]{:S(2)}, u32[]{:S(2)}) collective-permute-start(bf16[2,128,3,128]{3,2,0,1:T(4,128)(2,1)S(1)} %get-tuple-element.9), channel_id=1, source_target_pairs={{1,0},{2,1},{3,2},{4,3},{5,4},{6,5},{7,6},{9,8},{10,9},{11,10},{12... | collective-permute-start | bytes 589832 | tf_op jit(solution)/shard_map/ppermute | solution.py:17
Sparse Core Ops, SparseCore 0:
  9.5 34.4 all-gather.1
  47.1 32.4 reduce-scatter.1
where the time goes:
time: 86.6 us; the launch traced here: 86.4 us
  waiting for transfers between devices  58.1 us (67%)
  between operations  13.5 us (16%)
  local copies, waits for them, and re-layouts  4.93 us (6%)
  matrix products  3.91 us (5%)
  starting transfers between devices  3.71 us (4%)
  other arithmetic  2.27 us (3%)
    reduce_scatter x1, waiting for transfers between devices, body(): lax.psum_scatter(partial_terms, 'ao', scatter_dimension=2, tiled=True)  32.8 us
    all_gather x1, waiting for transfers between devices, body(): piece = lax.all_gather(screened, 'aux', axis=0, tiled=True)  21 us
    ppermute x1, waiting for transfers between devices, padded(): after = lax.ppermute(first, axis, down)  4.21 us
    dot_general x1, matrix products, body(): jnp.einsum('tpk,qk->tpq', dressed, others, preferred_element_type=jnp.flo...  2.69 us
    ppermute x1, starting transfers between devices, padded(): before = lax.ppermute(last, axis, up)  2.37 us
    unnamed x8, local copies, waits for them, and re-layouts  2.2 us
    concatenate x1, local copies, waits for them, and re-layouts, padded(): x = jnp.concatenate([before, x, after], axis=dim)  1.78 us
  transfers between devices with their start and end apart: 4, of which 3 were waited for; matrix products, arithmetic and copies ran while one was open for 6% of the time, Pallas kernels for 0%

commit v1 on v0

v1 whole, which is shorter than its diff:
```python
import functools
import math

import jax
import jax.numpy as jnp
from jax import lax
from jax.experimental import pallas as pl
from jax.experimental.pallas import tpu as pltpu
from jax.sharding import PartitionSpec as P

VMEM = pl.BlockSpec(memory_space=pltpu.VMEM)
SMEM = pl.BlockSpec(memory_space=pltpu.SMEM)
NT = (((1,), (1,)), ((), ()))


def shape(dims, dtype):
    return jax.ShapeDtypeStruct(dims, dtype)


def screen_kernel(tile, mask_ref, raw_ref, out_ref, first_ref, last_ref):
    window, rows, cols = raw_ref.shape
    count = cols // tile
    for r in range(rows // tile):
        here = pl.ds(r * tile, tile)
        for l in range(window):
            for i in range(count):
                part = pl.ds(i * tile, tile)
                keep = mask_ref[r, i].astype(jnp.float32).astype(jnp.bfloat16)
                value = raw_ref[l, here, part] * keep
                out_ref[l, here, part] = value
                if i == 0:
                    first_ref[l, here, :] = value
                if i == count - 1:
                    last_ref[l, here, :] = value


def screen(mask, raw, tile):
    window, rows, cols = raw.shape
    edge = shape((window, rows, tile), raw.dtype)
    return pl.pallas_call(
        functools.partial(screen_kernel, tile),
        out_shape=[shape((window, rows, cols), raw.dtype), edge, edge],
        in_specs=[SMEM, VMEM],
        out_specs=[VMEM] * 3,
        name="screen",
    )(mask, raw)


def dress_kernel(tile, occ_ref, own_ref, before_ref, after_ref, band_ref, out_ref):
    window, rows, cols = own_ref.shape
    times = band_ref.shape[0]
    count = cols // tile
    tiles = []
    for i in range(count + 2):
        if i == 0:
            get = lambda m: before_ref[m]
        elif i == count + 1:
            get = lambda m: after_ref[m]
        else:
            get = lambda m, i=i: own_ref[m, :, pl.ds((i - 1) * tile, tile)]
        tiles.append([get(m).astype(jnp.float32) for m in range(window)])
    for t in range(times):
        products = []
        for l in range(window):
            row = []
            for group in tiles:
                total = occ_ref[t, l, 0] * group[0]
                for m in range(1, window):
                    total = total + occ_ref[t, l, m] * group[m]
                row.append(total.astype(jnp.bfloat16))
            products.append(jnp.concatenate(row, axis=1))
        tall = jnp.concatenate(products, axis=0)
        for i in range(count):
            part = pl.ds(i * tile, tile)
            value = lax.dot_general(
                tall[:, i * tile : (i + 3) * tile],
                band_ref[t, part, :],
                NT,
                preferred_element_type=jnp.float32,
            ).astype(jnp.bfloat16)
            for l in range(window):
                out_ref[l, pl.ds(t * rows, rows), part] = value[l * rows : (l + 1) * rows]


def dress(occ, own, before, after, band, tile):
    window, rows, cols = own.shape
    times = band.shape[0]
    return pl.pallas_call(
        functools.partial(dress_kernel, tile),
        out_shape=shape((window, times * rows, cols), jnp.bfloat16),
        in_specs=[SMEM] + [VMEM] * 4,
        out_specs=VMEM,
        name="dress",
    )(occ, own, before, after, band)


def share_kernel(offsets, width, dressed_ref, *refs):
    count = len(offsets)
    blocks, earlier = refs[:count], refs[count:-2]
    keep_ref, send_ref = refs[-2:]
    window, rows, _ = blocks[0].shape
    planes = lax.axis_size("aux")
    place = lax.axis_index("aux")
    core = lax.rem(lax.axis_index("ao"), 2)
    if earlier:
        keep_ref[...] = earlier[0][...]
        send_ref[...] = earlier[1][...]
    per = rows // (2 * width)
    for offset, block in zip(offsets, blocks):
        source = place + offset

        @pl.when((source >= 0) & (source < planes))
        def _(block=block, source=source):
            total = lax.dot_general(
                block[0], dressed_ref[0], NT, preferred_element_type=jnp.float32
            )
            for l in range(1, window):
                total += lax.dot_general(
                    block[l], dressed_ref[l], NT, preferred_element_type=jnp.float32
                )
            for j in range(per):
                low = total[2 * j * width : (2 * j + 1) * width]
                high = total[(2 * j + 1) * width : (2 * j + 2) * width]
                first = core == 0
                keep_ref[source * per + j] = jnp.where(first, low, high)
                send_ref[source * per + j] = jnp.where(first, high, low).astype(jnp.bfloat16)


def share(offsets, chips, width, dressed, blocks, earlier):
    dims = (chips, width, dressed.shape[1])
    args = [dressed, *blocks, *earlier]
    return pl.pallas_call(
        functools.partial(share_kernel, offsets, width),
        out_shape=[shape(dims, jnp.float32), shape(dims, jnp.bfloat16)],
        in_specs=[VMEM] * len(args),
        out_specs=[VMEM] * 2,
        name="share",
    )(*args)


def pair_kernel(keep_ref, got_ref, own_ref, *outs):
    chip = lax.axis_index("ao") // 2
    own_ref[...] = keep_ref[chip] + got_ref[chip].astype(jnp.float32)
    for k, out in enumerate(outs):
        other = chip ^ (k + 1)
        out[...] = (keep_ref[other] + got_ref[other].astype(jnp.float32)).astype(jnp.bfloat16)


def pair(keep, got):
    chips = keep.shape[0]
    dims = keep.shape[1:]
    return pl.pallas_call(
        pair_kernel,
        out_shape=[shape(dims, jnp.float32)] + [shape(dims, jnp.bfloat16)] * (chips - 1),
        in_specs=[VMEM] * 2,
        out_specs=[VMEM] * chips,
        name="pair",
    )(keep, got)


def finish_kernel(factor, own_ref, *refs):
    others, out_ref = refs[:-1], refs[-1]
    total = own_ref[...]
    for other in others:
        total += other[...].astype(jnp.float32)
    total *= factor
    rows = out_ref.shape[2]
    for t in range(out_ref.shape[0]):
        out_ref[t] = total[:, t * rows : (t + 1) * rows]


def finish(factor, times, own, others):
    width, both = own.shape
    return pl.pallas_call(
        functools.partial(finish_kernel, factor),
        out_shape=shape((times, width, both // times), jnp.float32),
        in_specs=[VMEM] * (1 + len(others)),
        out_specs=VMEM,
        name="finish",
    )(own, *others)


def shifted(x, axis, by):
    devices = lax.axis_size(axis)
    pairs = [(i, i + by) for i in range(devices) if 0 <= i + by < devices]
    return lax.ppermute(x, axis, pairs)


def body(three_center, occ_green, virt_band, tile_mask):
    rows, window, cols = three_center.shape
    times = virt_band.shape[0]
    tile = virt_band.shape[2] // 3
    planes, blocks = lax.axis_size("aux"), lax.axis_size("ao")
    chips = blocks // 2
    width = planes * rows // blocks
    factor = 1.0 / math.sqrt(window * cols * blocks)

    own, first, last = screen(tile_mask, three_center.transpose(1, 0, 2), tile)
    held = {0: own}
    for d in range(1, planes):
        hop, part = (d + 1) // 2, d // 2
        held[d] = shifted(held[part], "aux", -hop)
        held[-d] = shifted(held[-part], "aux", hop)
        if d == 1:
            before = shifted(last, "ao", 1)
            after = shifted(first, "ao", -1)
            dressed = dress(
                occ_green.astype(jnp.float32), own, before, after, virt_band, tile
            )
    near = [d for d in (0, 1, -1) if d in held]
    far = [d for d in held if d not in near]
    sums = share(near, chips, width, dressed, [held[d] for d in near], ())
    if far:
        sums = share(far, chips, width, dressed, [held[d] for d in far], sums)
    keep, send = sums
    got = lax.ppermute(send, "ao", [(i, i ^ 1) for i in range(blocks)])
    mine, *others = pair(keep, got)
    others = [
        lax.ppermute(other, "ao", [(i, i ^ (2 * k + 2)) for i in range(blocks)])
        for k, other in enumerate(others)
    ]
    return finish(factor, times, mine, others).transpose(0, 2, 1)


def solution(mesh):
    in_specs = (P("aux", None, "ao"), P(), P(None, "ao", None), P("aux", "ao"))
    out_specs = P(None, "aux", "ao")
    return jax.shard_map(body, mesh=mesh, in_specs=in_specs, out_specs=out_specs, check_vma=False)
```

time: 86.6 us -> 56.6 us (0.65)
  waiting for transfers between devices: 58.1 us -> 11.4 us
  starting transfers between devices: 3.71 us -> 27.9 us
  Pallas kernels: 0 us -> 13.4 us
  between operations: 13.5 us -> 0.15 us
  matrix products: 3.91 us -> 0 us
  local copies, waits for them, and re-layouts: 4.93 us -> 2.72 us
  other arithmetic: 2.27 us -> 0.6 us
    reduce_scatter x1 -> x0, waiting for transfers between devices: 32.8 us -> none  [body(): lax.psum_scatter(partial_terms, 'ao', scatter_dimension=2, tiled=True)]
    ppermute x2 -> x12, starting transfers between devices: 3.66 us -> 27.9 us  [the longest x8 22.4 us: shifted(): return lax.ppermute(x, axis, pairs)]
    all_gather x1 -> x0, waiting for transfers between devices: 21 us -> none  [body(): piece = lax.all_gather(screened, 'aux', axis=0, tiled=True)]
    pallas_call x0 -> x6, Pallas kernels: none -> 13.4 us  [the longest x2 5.68 us: share(): pl.pallas_call(functools.partial(share_kernel, offsets, width), out_shape...]
    ppermute x2 -> x12, waiting for transfers between devices: 4.21 us -> 11.4 us  [the longest x8 6.61 us: shifted(): return lax.ppermute(x, axis, pairs)]
    dot_general x3 -> x0, matrix products: 3.91 us -> none  [the longest x1 2.69 us: body(): jnp.einsum('tpk,qk->tpq', dressed, others, preferred_element_type=jnp.flo...]
    concatenate x1 -> x0, local copies, waits for them, and re-layouts: 1.78 us -> none  [padded(): x = jnp.concatenate([before, x, after], axis=dim)]
    mul x3 -> x0, other arithmetic: 1.64 us -> none  [body(): three_center.reshape(aux_rows // tile, tile, window, ao_cols // tile, tile)]
  transfers between devices with their start and end apart: 4 -> 12, of which waited for: 3 -> 7; matrix products, arithmetic and copies ran while one was open for 6% -> 1% of each run, Pallas kernels for 0% -> 10%
where the time goes in v1:
time: 56.6 us; the launch traced here: 56.1 us
  starting transfers between devices  27.9 us (49%)
  Pallas kernels  13.4 us (24%)
  waiting for transfers between devices  11.4 us (20%)
  local copies, waits for them, and re-layouts  2.72 us (5%)
  other arithmetic  0.6 us (1%)
    ppermute x8, starting transfers between devices, shifted(): return lax.ppermute(x, axis, pairs)  22.4 us
    ppermute x8, waiting for transfers between devices, shifted(): return lax.ppermute(x, axis, pairs)  6.61 us
    pallas_call x2, Pallas kernels, share(): pl.pallas_call(functools.partial(share_kernel, offsets, width), out_shape...  5.68 us
    ppermute x3, waiting for transfers between devices, body(): lax.ppermute(other, 'ao', [(i, i ^ 2 * k + 2) for i in range(blocks)])  3.58 us
    ppermute x3, starting transfers between devices, body(): lax.ppermute(other, 'ao', [(i, i ^ 2 * k + 2) for i in range(blocks)])  3.5 us
    pallas_call x1, Pallas kernels, dress(): pl.pallas_call(functools.partial(dress_kernel, tile), out_shape=shape((wi...  2.78 us
    unnamed x26, local copies, waits for them, and re-layouts  2.72 us
    ppermute x1, starting transfers between devices, body(): got = lax.ppermute(send, 'ao', [(i, i ^ 1) for i in range(blocks)])  2.01 us
  transfers between devices with their start and end apart: 12, of which 7 were waited for; matrix products, arithmetic and copies ran while one was open for 1% of the time, Pallas kernels for 10%

profile of v1, /device:TPU:0, one launch (start us, length us, event | category | flops | bytes accessed | tf_op | source)
XLA Modules:
  0.0 56.1 jit_solution(15289064236789110999)
XLA Ops:
  0.0 1.8 %screen.1 = (bf16[3,128,384]{2,1,0:T(8,128)(2,1)}, bf16[3,128,128]{2,1,0:T(8,128)(2,1)}, bf16[3,128,128]{2,1,0:T(8,128)(2,1)}) custom-call(s32[1,3]{1,0:T(1,128)} %mask_ref.1, bf16[3,128,384]{2,1,0:T(8,128)(2,1)} %bitcast.2), custom_call_target="tpu_custom_call" | custom-call | tf_op jit(solution)/shard_map/screen/pallas_call | solution.py:40
  1.8 1.4 %collective-permute-start.2 = (bf16[3,128,384]{2,1,0:T(8,128)(2,1)}, bf16[3,128,384]{2,1,0:T(8,128)(2,1)S(1)}, u32[]{:S(2)}, u32[]{:S(2)}) collective-permute-start(bf16[3,128,384]{2,1,0:T(8,128)(2,1)} %get-tuple-element.16.own_ref.refs_0_), channel_id=1, source_target_pairs={{8,0},{16,8},{24,16},{9,1},{17,9},{25,17},{10,2},{18,10},{26,18},{... | collective-permute-start | bytes 884744 | tf_op jit(solution)/shard_map/ppermute | solution.py:186
  3.2 5.6 %collective-permute-start.4 = (bf16[3,128,384]{2,1,0:T(8,128)(2,1)}, bf16[3,128,384]{2,1,0:T(8,128)(2,1)S(1)}, u32[]{:S(2)}, u32[]{:S(2)}) collective-permute-start(bf16[3,128,384]{2,1,0:T(8,128)(2,1)} %get-tuple-element.16.own_ref.refs_0_), channel_id=1, source_target_pairs={{0,8},{8,16},{16,24},{1,9},{9,17},{17,25},{2,10},{10,18},{18,26},{... | collective-permute-start | bytes 884744 | tf_op jit(solution)/shard_map/ppermute | solution.py:186
  8.8 1.5 %collective-permute-start = (bf16[3,128,128]{2,1,0:T(8,128)(2,1)}, bf16[3,128,128]{2,1,0:T(8,128)(2,1)S(1)}, u32[]{:S(2)}, u32[]{:S(2)}) collective-permute-start(bf16[3,128,128]{2,1,0:T(8,128)(2,1)} %get-tuple-element.17), channel_id=1, source_target_pairs={{0,1},{1,2},{2,3},{3,4},{4,5},{5,6},{6,7},{8,9},{9,10},{10,11},{11... | collective-permute-start | bytes 294920 | tf_op jit(solution)/shard_map/ppermute | solution.py:186
  10.3 3.8 %collective-permute-done.2.refs_1_ = bf16[3,128,384]{2,1,0:T(8,128)(2,1)S(1)} collective-permute-done((bf16[3,128,384]{2,1,0:T(8,128)(2,1)}, bf16[3,128,384]{2,1,0:T(8,128)(2,1)S(1)}, u32[]{:S(2)}, u32[]{:S(2)}) %collective-permute-start.2) | collective-permute-done | bytes 294944 | tf_op jit(solution)/shard_map/ppermute | solution.py:186
  14.1 1.3 %collective-permute-start.3 = (bf16[3,128,384]{2,1,0:T(8,128)(2,1)S(1)}, bf16[3,128,384]{2,1,0:T(8,128)(2,1)S(1)}, u32[]{:S(2)}, u32[]{:S(2)}) collective-permute-start(bf16[3,128,384]{2,1,0:T(8,128)(2,1)S(1)} %collective-permute-done.2.refs_1_), channel_id=1, source_target_pairs={{8,0},{16,8},{24,16},{9,1},{17,9},{25,17},{10,2},{18,10},{26,18},{... | collective-permute-start | bytes 884744 | tf_op jit(solution)/shard_map/ppermute | solution.py:186
  15.4 4.6 %collective-permute-start.5 = (bf16[3,128,384]{2,1,0:T(8,128)(2,1)S(1)}, bf16[3,128,384]{2,1,0:T(8,128)(2,1)S(1)}, u32[]{:S(2)}, u32[]{:S(2)}) collective-permute-start(bf16[3,128,384]{2,1,0:T(8,128)(2,1)S(1)} %collective-permute-done.4.refs_2_), channel_id=1, source_target_pairs={{0,8},{8,16},{16,24},{1,9},{9,17},{17,25},{2,10},{10,18},{18,26},{... | collective-permute-start | bytes 884744 | tf_op jit(solution)/shard_map/ppermute | solution.py:186
  20.0 1.3 %collective-permute-start.6 = (bf16[3,128,384]{2,1,0:T(8,128)(2,1)S(1)}, bf16[3,128,384]{2,1,0:T(8,128)(2,1)S(1)}, u32[]{:S(2)}, u32[]{:S(2)}) collective-permute-start(bf16[3,128,384]{2,1,0:T(8,128)(2,1)S(1)} %collective-permute-done.2.refs_1_), channel_id=1, source_target_pairs={{16,0},{24,8},{17,1},{25,9},{18,2},{26,10},{19,3},{27,11},{20,4},{... | collective-permute-start | bytes 884744 | tf_op jit(solution)/shard_map/ppermute | solution.py:186
  21.3 5.5 %collective-permute-start.7 = (bf16[3,128,384]{2,1,0:T(8,128)(2,1)S(1)}, bf16[3,128,384]{2,1,0:T(8,128)(2,1)S(1)}, u32[]{:S(2)}, u32[]{:S(2)}) collective-permute-start(bf16[3,128,384]{2,1,0:T(8,128)(2,1)S(1)} %collective-permute-done.4.refs_2_), channel_id=1, source_target_pairs={{0,16},{8,24},{1,17},{9,25},{2,18},{10,26},{3,19},{11,27},{4,20},{... | collective-permute-start | bytes 884744 | tf_op jit(solution)/shard_map/ppermute | solution.py:186
  26.8 1.3 %collective-permute-start.1 = (bf16[3,128,128]{2,1,0:T(8,128)(2,1)}, bf16[3,128,128]{2,1,0:T(8,128)(2,1)S(1)}, u32[]{:S(2)}, u32[]{:S(2)}) collective-permute-start(bf16[3,128,128]{2,1,0:T(8,128)(2,1)} %get-tuple-element.18), channel_id=1, source_target_pairs={{1,0},{2,1},{3,2},{4,3},{5,4},{6,5},{7,6},{9,8},{10,9},{11,10},{12... | collective-permute-start | bytes 294920 | tf_op jit(solution)/shard_map/ppermute | solution.py:186
  28.1 0.6 %copy_convert_fusion.occ_ref = f32[2,3,3]{2,1,0:T(4,128)} fusion(bf16[2,3,3]{2,0,1:T(2,128)(2,1)S(1)} %copy-done.12), kind=kLoop, calls=%fused_computation | loop fusion | flops 18 | bytes 108 | tf_op jit(solution)/shard_map/convert_element_type | solution.py:208
  28.7 1.5 %collective-permute-done.1.after_ref = bf16[3,128,128]{2,1,0:T(8,128)(2,1)S(1)} collective-permute-done((bf16[3,128,128]{2,1,0:T(8,128)(2,1)}, bf16[3,128,128]{2,1,0:T(8,128)(2,1)S(1)}, u32[]{:S(2)}, u32[]{:S(2)}) %collective-permute-start.1) | collective-permute-done | bytes 98336 | tf_op jit(solution)/shard_map/ppermute | solution.py:186
  30.2 0.6 %copy-done.8 = bf16[3,128,128]{2,1,0:T(8,128)(2,1)} copy-done((bf16[3,128,128]{2,1,0:T(8,128)(2,1)}, bf16[3,128,128]{2,1,0:T(8,128)(2,1)S(1)}, u32[]{:S(2)}) %copy-start.8) | copy-done | bytes 98328
  30.8 2.8 %dress.1.dressed_ref = bf16[3,256,384]{2,1,0:T(8,128)(2,1)} custom-call(f32[2,3,3]{2,1,0:T(4,128)} %copy_convert_fusion.occ_ref, bf16[3,128,384]{2,1,0:T(8,128)(2,1)} %get-tuple-element.16.own_ref.refs_0_, bf16[3,128,128]{2,1,0:T(8,128)(2,1)} %copy-done.7, bf16[3,128,128]{2,1,0:T(8,128)(2,1)} %copy-done.8, bf16[2,384,384]{2,1,0:T(8,128)(2,1)} %band_ref.1), custom_call_target="tpu_custom_call" | custom-call | tf_op jit(solution)/shard_map/dress/pallas_call | solution.py:88
  33.6 2.7 %share.2 = (f32[4,64,256]{2,1,0:T(8,128)}, bf16[4,64,256]{2,1,0:T(8,128)(2,1)}) custom-call(bf16[3,256,384]{2,1,0:T(8,128)(2,1)} %dress.1.dressed_ref, bf16[3,128,384]{2,1,0:T(8,128)(2,1)} %get-tuple-element.16.own_ref.refs_0_, bf16[3,128,384]{2,1,0:T(8,128)(2,1)} %copy-done, bf16[3,128,384]{2,1,0:T(8,128)(2,1)} %copy-done.1), custom_call_target="tpu_custom_call" | custom-call | tf_op jit(solution)/shard_map/share/pallas_call | solution.py:132
  36.3 1.3 %collective-permute-done.6.refs_2_ = bf16[3,128,384]{2,1,0:T(8,128)(2,1)S(1)} collective-permute-done((bf16[3,128,384]{2,1,0:T(8,128)(2,1)S(1)}, bf16[3,128,384]{2,1,0:T(8,128)(2,1)S(1)}, u32[]{:S(2)}, u32[]{:S(2)}) %collective-permute-start.6) | collective-permute-done | bytes 294944 | tf_op jit(solution)/shard_map/ppermute | solution.py:186
  37.7 0.7 %copy-done.4 = bf16[3,128,384]{2,1,0:T(8,128)(2,1)} copy-done((bf16[3,128,384]{2,1,0:T(8,128)(2,1)}, bf16[3,128,384]{2,1,0:T(8,128)(2,1)S(1)}, u32[]{:S(2)}) %copy-start.4) | copy-done | bytes 294936
  38.4 0.1 copy-done.5
  38.5 3.0 %share.3 = (f32[4,64,256]{2,1,0:T(8,128)}, bf16[4,64,256]{2,1,0:T(8,128)(2,1)}) custom-call(bf16[3,256,384]{2,1,0:T(8,128)(2,1)} %dress.1.dressed_ref, bf16[3,128,384]{2,1,0:T(8,128)(2,1)} %copy-done.2, bf16[3,128,384]{2,1,0:T(8,128)(2,1)} %copy-done.3, bf16[3,128,384]{2,1,0:T(8,128)(2,1)} %copy-done.4, bf16[3,128,384]{2,1,0:T(8,128)(2,1)} %copy-done.5, ...), custom_call_target="tpu_custom_call" | custom-call | tf_op jit(solution)/shard_map/share/pallas_call | solution.py:132
  41.4 2.0 %collective-permute-start.8 = (bf16[4,64,256]{2,1,0:T(8,128)(2,1)}, bf16[4,64,256]{2,1,0:T(8,128)(2,1)S(1)}, u32[]{:S(2)}, u32[]{:S(2)}) collective-permute-start(bf16[4,64,256]{2,1,0:T(8,128)(2,1)} %get-tuple-element.22), channel_id=1, source_target_pairs={{0,1},{1,0},{2,3},{3,2},{4,5},{5,4},{6,7},{7,6},{8,9},{9,8},{10,11... | collective-permute-start | bytes 393224 | tf_op jit(solution)/shard_map/ppermute | solution.py:216
  43.4 1.2 %collective-permute-done.8.got_ref = bf16[4,64,256]{2,1,0:T(8,128)(2,1)S(1)} collective-permute-done((bf16[4,64,256]{2,1,0:T(8,128)(2,1)}, bf16[4,64,256]{2,1,0:T(8,128)(2,1)S(1)}, u32[]{:S(2)}, u32[]{:S(2)}) %collective-permute-start.8) | collective-permute-done | bytes 131104 | tf_op jit(solution)/shard_map/ppermute | solution.py:216
  44.6 0.7 %copy-done.6 = bf16[4,64,256]{2,1,0:T(8,128)(2,1)} copy-done((bf16[4,64,256]{2,1,0:T(8,128)(2,1)}, bf16[4,64,256]{2,1,0:T(8,128)(2,1)S(1)}, u32[]{:S(2)}) %copy-start.6) | copy-done | bytes 131096
  45.3 1.6 %pair.1 = (f32[64,256]{1,0:T(8,128)}, bf16[64,256]{1,0:T(8,128)(2,1)}, bf16[64,256]{1,0:T(8,128)(2,1)}, bf16[64,256]{1,0:T(8,128)(2,1)}) custom-call(f32[4,64,256]{2,1,0:T(8,128)} %get-tuple-element.21.keep_ref, bf16[4,64,256]{2,1,0:T(8,128)(2,1)} %copy-done.6), custom_call_target="tpu_custom_call" | custom-call | tf_op jit(solution)/shard_map/pair/pallas_call | solution.py:152
  46.9 1.5 %collective-permute-start.10 = (bf16[64,256]{1,0:T(8,128)(2,1)}, bf16[64,256]{1,0:T(8,128)(2,1)S(1)}, u32[]{:S(2)}, u32[]{:S(2)}) collective-permute-start(bf16[64,256]{1,0:T(8,128)(2,1)} %get-tuple-element.25), channel_id=1, source_target_pairs={{0,4},{1,5},{2,6},{3,7},{4,0},{5,1},{6,2},{7,3},{8,12},{9,13},{10,... | collective-permute-start | bytes 98312 | tf_op jit(solution)/shard_map/ppermute | solution.py:219
  48.5 1.4 %collective-permute-start.11 = (bf16[64,256]{1,0:T(8,128)(2,1)}, bf16[64,256]{1,0:T(8,128)(2,1)S(1)}, u32[]{:S(2)}, u32[]{:S(2)}) collective-permute-start(bf16[64,256]{1,0:T(8,128)(2,1)} %get-tuple-element.26), channel_id=1, source_target_pairs={{0,6},{1,7},{2,4},{3,5},{4,2},{5,3},{6,0},{7,1},{8,14},{9,15},{10,... | collective-permute-start | bytes 98312 | tf_op jit(solution)/shard_map/ppermute | solution.py:219
  49.9 0.5 collective-permute-start.9
  50.4 0.6 %collective-permute-done.10.refs_1_ = bf16[64,256]{1,0:T(8,128)(2,1)S(1)} collective-permute-done((bf16[64,256]{1,0:T(8,128)(2,1)}, bf16[64,256]{1,0:T(8,128)(2,1)S(1)}, u32[]{:S(2)}, u32[]{:S(2)}) %collective-permute-start.10) | collective-permute-done | bytes 32800 | tf_op jit(solution)/shard_map/ppermute | solution.py:219
  51.1 2.4 %collective-permute-done.11.refs_2_ = bf16[64,256]{1,0:T(8,128)(2,1)S(1)} collective-permute-done((bf16[64,256]{1,0:T(8,128)(2,1)}, bf16[64,256]{1,0:T(8,128)(2,1)S(1)}, u32[]{:S(2)}, u32[]{:S(2)}) %collective-permute-start.11) | collective-permute-done | bytes 32800 | tf_op jit(solution)/shard_map/ppermute | solution.py:219
  53.5 0.5 collective-permute-done.9.refs_0_
  54.0 0.1 copy-done.10
  54.1 0.5 copy-done.11
  54.6 1.5 %finish.1 = f32[2,64,128]{2,1,0:T(8,128)} custom-call(f32[64,256]{1,0:T(8,128)} %get-tuple-element.23.own_ref, bf16[64,256]{1,0:T(8,128)(2,1)} %copy-done.11, bf16[64,256]{1,0:T(8,128)(2,1)} %copy-done.9, bf16[64,256]{1,0:T(8,128)(2,1)} %copy-done.10), custom_call_target="tpu_custom_call" | custom-call | tf_op jit(solution)/shard_map/finish/pallas_call | solution.py:174
  (25 shorter events, 0.0 us)
Async XLA Ops:
  1.8 26.3 %copy-start.12 = (bf16[2,3,3]{2,0,1:T(2,128)(2,1)S(1)}, bf16[2,3,3]{2,0,1:T(2,128)(2,1)}, u32[]{:S(2)}) copy-start(bf16[2,3,3]{2,0,1:T(2,128)(2,1)} %param.5) | copy-start | bytes 112
  1.8 12.3 %collective-permute-start.2 = (bf16[3,128,384]{2,1,0:T(8,128)(2,1)}, bf16[3,128,384]{2,1,0:T(8,128)(2,1)S(1)}, u32[]{:S(2)}, u32[]{:S(2)}) collective-permute-start(bf16[3,128,384]{2,1,0:T(8,128)(2,1)} %get-tuple-element.16.own_ref.refs_0_), channel_id=1, source_target_pairs={{8,0},{16,8},{24,16},{9,1},{17,9},{25,17},{10,2},{18,10},{26,18},{... | collective-permute-start | bytes 884744 | tf_op jit(solution)/shard_map/ppermute | solution.py:186
  3.2 12.1 %collective-permute-start.4 = (bf16[3,128,384]{2,1,0:T(8,128)(2,1)}, bf16[3,128,384]{2,1,0:T(8,128)(2,1)S(1)}, u32[]{:S(2)}, u32[]{:S(2)}) collective-permute-start(bf16[3,128,384]{2,1,0:T(8,128)(2,1)} %get-tuple-element.16.own_ref.refs_0_), channel_id=1, source_target_pairs={{0,8},{8,16},{16,24},{1,9},{9,17},{17,25},{2,10},{10,18},{18,26},{... | collective-permute-start | bytes 884744 | tf_op jit(solution)/shard_map/ppermute | solution.py:186
  8.8 17.9 %collective-permute-start = (bf16[3,128,128]{2,1,0:T(8,128)(2,1)}, bf16[3,128,128]{2,1,0:T(8,128)(2,1)S(1)}, u32[]{:S(2)}, u32[]{:S(2)}) collective-permute-start(bf16[3,128,128]{2,1,0:T(8,128)(2,1)} %get-tuple-element.17), channel_id=1, source_target_pairs={{0,1},{1,2},{2,3},{3,4},{4,5},{5,6},{6,7},{8,9},{9,10},{10,11},{11... | collective-permute-start | bytes 294920 | tf_op jit(solution)/shard_map/ppermute | solution.py:186
  14.1 19.5 %copy-start = (bf16[3,128,384]{2,1,0:T(8,128)(2,1)}, bf16[3,128,384]{2,1,0:T(8,128)(2,1)S(1)}, u32[]{:S(2)}) copy-start(bf16[3,128,384]{2,1,0:T(8,128)(2,1)S(1)} %collective-permute-done.2.refs_1_) | copy-start | bytes 884740
  14.1 22.2 %collective-permute-start.3 = (bf16[3,128,384]{2,1,0:T(8,128)(2,1)S(1)}, bf16[3,128,384]{2,1,0:T(8,128)(2,1)S(1)}, u32[]{:S(2)}, u32[]{:S(2)}) collective-permute-start(bf16[3,128,384]{2,1,0:T(8,128)(2,1)S(1)} %collective-permute-done.2.refs_1_), channel_id=1, source_target_pairs={{8,0},{16,8},{24,16},{9,1},{17,9},{25,17},{10,2},{18,10},{26,18},{... | collective-permute-start | bytes 884744 | tf_op jit(solution)/shard_map/ppermute | solution.py:186
  15.4 18.2 %copy-start.1 = (bf16[3,128,384]{2,1,0:T(8,128)(2,1)}, bf16[3,128,384]{2,1,0:T(8,128)(2,1)S(1)}, u32[]{:S(2)}) copy-start(bf16[3,128,384]{2,1,0:T(8,128)(2,1)S(1)} %collective-permute-done.4.refs_2_) | copy-start | bytes 884740
  15.4 20.9 %collective-permute-start.5 = (bf16[3,128,384]{2,1,0:T(8,128)(2,1)S(1)}, bf16[3,128,384]{2,1,0:T(8,128)(2,1)S(1)}, u32[]{:S(2)}, u32[]{:S(2)}) collective-permute-start(bf16[3,128,384]{2,1,0:T(8,128)(2,1)S(1)} %collective-permute-done.4.refs_2_), channel_id=1, source_target_pairs={{0,8},{8,16},{16,24},{1,9},{9,17},{17,25},{2,10},{10,18},{18,26},{... | collective-permute-start | bytes 884744 | tf_op jit(solution)/shard_map/ppermute | solution.py:186
  20.0 17.7 %collective-permute-start.6 = (bf16[3,128,384]{2,1,0:T(8,128)(2,1)S(1)}, bf16[3,128,384]{2,1,0:T(8,128)(2,1)S(1)}, u32[]{:S(2)}, u32[]{:S(2)}) collective-permute-start(bf16[3,128,384]{2,1,0:T(8,128)(2,1)S(1)} %collective-permute-done.2.refs_1_), channel_id=1, source_target_pairs={{16,0},{24,8},{17,1},{25,9},{18,2},{26,10},{19,3},{27,11},{20,4},{... | collective-permute-start | bytes 884744 | tf_op jit(solution)/shard_map/ppermute | solution.py:186
  21.3 16.4 %collective-permute-start.7 = (bf16[3,128,384]{2,1,0:T(8,128)(2,1)S(1)}, bf16[3,128,384]{2,1,0:T(8,128)(2,1)S(1)}, u32[]{:S(2)}, u32[]{:S(2)}) collective-permute-start(bf16[3,128,384]{2,1,0:T(8,128)(2,1)S(1)} %collective-permute-done.4.refs_2_), channel_id=1, source_target_pairs={{0,16},{8,24},{1,17},{9,25},{2,18},{10,26},{3,19},{11,27},{4,20},{... | collective-permute-start | bytes 884744 | tf_op jit(solution)/shard_map/ppermute | solution.py:186
  26.8 3.4 %copy-start.7 = (bf16[3,128,128]{2,1,0:T(8,128)(2,1)}, bf16[3,128,128]{2,1,0:T(8,128)(2,1)S(1)}, u32[]{:S(2)}) copy-start(bf16[3,128,128]{2,1,0:T(8,128)(2,1)S(1)} %collective-permute-done.before_ref) | copy-start | bytes 294916
  26.8 3.4 %collective-permute-start.1 = (bf16[3,128,128]{2,1,0:T(8,128)(2,1)}, bf16[3,128,128]{2,1,0:T(8,128)(2,1)S(1)}, u32[]{:S(2)}, u32[]{:S(2)}) collective-permute-start(bf16[3,128,128]{2,1,0:T(8,128)(2,1)} %get-tuple-element.18), channel_id=1, source_target_pairs={{1,0},{2,1},{3,2},{4,3},{5,4},{6,5},{7,6},{9,8},{10,9},{11,10},{12... | collective-permute-start | bytes 294920 | tf_op jit(solution)/shard_map/ppermute | solution.py:186
  30.2 0.6 %copy-start.8 = (bf16[3,128,128]{2,1,0:T(8,128)(2,1)}, bf16[3,128,128]{2,1,0:T(8,128)(2,1)S(1)}, u32[]{:S(2)}) copy-start(bf16[3,128,128]{2,1,0:T(8,128)(2,1)S(1)} %collective-permute-done.1.after_ref) | copy-start | bytes 294916
  36.3 1.3 %copy-start.2 = (bf16[3,128,384]{2,1,0:T(8,128)(2,1)}, bf16[3,128,384]{2,1,0:T(8,128)(2,1)S(1)}, u32[]{:S(2)}) copy-start(bf16[3,128,384]{2,1,0:T(8,128)(2,1)S(1)} %collective-permute-done.3.refs_0_) | copy-start | bytes 884740
  36.3 1.3 %copy-start.3 = (bf16[3,128,384]{2,1,0:T(8,128)(2,1)}, bf16[3,128,384]{2,1,0:T(8,128)(2,1)S(1)}, u32[]{:S(2)}) copy-start(bf16[3,128,384]{2,1,0:T(8,128)(2,1)S(1)} %collective-permute-done.5.refs_1_) | copy-start | bytes 884740
  37.7 0.7 %copy-start.4 = (bf16[3,128,384]{2,1,0:T(8,128)(2,1)}, bf16[3,128,384]{2,1,0:T(8,128)(2,1)S(1)}, u32[]{:S(2)}) copy-start(bf16[3,128,384]{2,1,0:T(8,128)(2,1)S(1)} %collective-permute-done.6.refs_2_) | copy-start | bytes 884740
  37.7 0.8 %copy-start.5 = (bf16[3,128,384]{2,1,0:T(8,128)(2,1)}, bf16[3,128,384]{2,1,0:T(8,128)(2,1)S(1)}, u32[]{:S(2)}) copy-start(bf16[3,128,384]{2,1,0:T(8,128)(2,1)S(1)} %collective-permute-done.7.refs_3_) | copy-start | bytes 884740
  41.4 3.2 %collective-permute-start.8 = (bf16[4,64,256]{2,1,0:T(8,128)(2,1)}, bf16[4,64,256]{2,1,0:T(8,128)(2,1)S(1)}, u32[]{:S(2)}, u32[]{:S(2)}) collective-permute-start(bf16[4,64,256]{2,1,0:T(8,128)(2,1)} %get-tuple-element.22), channel_id=1, source_target_pairs={{0,1},{1,0},{2,3},{3,2},{4,5},{5,4},{6,7},{7,6},{8,9},{9,8},{10,11... | collective-permute-start | bytes 393224 | tf_op jit(solution)/shard_map/ppermute | solution.py:216
  44.6 0.7 %copy-start.6 = (bf16[4,64,256]{2,1,0:T(8,128)(2,1)}, bf16[4,64,256]{2,1,0:T(8,128)(2,1)S(1)}, u32[]{:S(2)}) copy-start(bf16[4,64,256]{2,1,0:T(8,128)(2,1)S(1)} %collective-permute-done.8.got_ref) | copy-start | bytes 393220
  46.9 4.1 %collective-permute-start.10 = (bf16[64,256]{1,0:T(8,128)(2,1)}, bf16[64,256]{1,0:T(8,128)(2,1)S(1)}, u32[]{:S(2)}, u32[]{:S(2)}) collective-permute-start(bf16[64,256]{1,0:T(8,128)(2,1)} %get-tuple-element.25), channel_id=1, source_target_pairs={{0,4},{1,5},{2,6},{3,7},{4,0},{5,1},{6,2},{7,3},{8,12},{9,13},{10,... | collective-permute-start | bytes 98312 | tf_op jit(solution)/shard_map/ppermute | solution.py:219
  48.5 5.0 %collective-permute-start.11 = (bf16[64,256]{1,0:T(8,128)(2,1)}, bf16[64,256]{1,0:T(8,128)(2,1)S(1)}, u32[]{:S(2)}, u32[]{:S(2)}) collective-permute-start(bf16[64,256]{1,0:T(8,128)(2,1)} %get-tuple-element.26), channel_id=1, source_target_pairs={{0,6},{1,7},{2,4},{3,5},{4,2},{5,3},{6,0},{7,1},{8,14},{9,15},{10,... | collective-permute-start | bytes 98312 | tf_op jit(solution)/shard_map/ppermute | solution.py:219
  49.9 4.1 %collective-permute-start.9 = (bf16[64,256]{1,0:T(8,128)(2,1)}, bf16[64,256]{1,0:T(8,128)(2,1)S(1)}, u32[]{:S(2)}, u32[]{:S(2)}) collective-permute-start(bf16[64,256]{1,0:T(8,128)(2,1)} %get-tuple-element.24), channel_id=1, source_target_pairs={{0,2},{1,3},{2,0},{3,1},{4,6},{5,7},{6,4},{7,5},{8,10},{9,11},{10,... | collective-permute-start | bytes 98312 | tf_op jit(solution)/shard_map/ppermute | solution.py:219
  51.1 3.0 %copy-start.9 = (bf16[64,256]{1,0:T(8,128)(2,1)}, bf16[64,256]{1,0:T(8,128)(2,1)S(1)}, u32[]{:S(2)}) copy-start(bf16[64,256]{1,0:T(8,128)(2,1)S(1)} %collective-permute-done.10.refs_1_) | copy-start | bytes 98308
  53.5 0.6 %copy-start.10 = (bf16[64,256]{1,0:T(8,128)(2,1)}, bf16[64,256]{1,0:T(8,128)(2,1)S(1)}, u32[]{:S(2)}) copy-start(bf16[64,256]{1,0:T(8,128)(2,1)S(1)} %collective-permute-done.11.refs_2_) | copy-start | bytes 98308
  54.0 0.6 %copy-start.11 = (bf16[64,256]{1,0:T(8,128)(2,1)}, bf16[64,256]{1,0:T(8,128)(2,1)S(1)}, u32[]{:S(2)}) copy-start(bf16[64,256]{1,0:T(8,128)(2,1)S(1)} %collective-permute-done.9.refs_0_) | copy-start | bytes 98308

commit v2 on v1

v2 whole, which is shorter than its diff:
```python
import functools
import math

import jax
import jax.numpy as jnp
from jax import lax
from jax.experimental import pallas as pl
from jax.experimental.pallas import tpu as pltpu
from jax.sharding import PartitionSpec as P

VMEM = pl.BlockSpec(memory_space=pltpu.VMEM)
SMEM = pl.BlockSpec(memory_space=pltpu.SMEM)
PARAMS = pltpu.CompilerParams(vmem_limit_bytes=16 * 1024 * 1024)
NT = (((1,), (1,)), ((), ()))


def shape(dims, dtype):
    return jax.ShapeDtypeStruct(dims, dtype)


def call(name, body, specs, outs, args):
    single = not isinstance(outs, (list, tuple))
    return pl.pallas_call(
        body,
        out_shape=outs,
        in_specs=specs,
        out_specs=VMEM if single else [VMEM] * len(outs),
        compiler_params=PARAMS,
        name=name,
    )(*args)


def is_even():
    return lax.rem(lax.axis_index("ao"), 2) == 0


def put_edges(even, first, last, inner_ref, outer_ref, here):
    inner_ref[here] = jnp.where(even, last, first)
    outer_ref[here] = jnp.where(even, first, last)


def screen_kernel(tile, mask_ref, raw_ref, out_ref, inner_ref, outer_ref):
    window, rows, cols = raw_ref.shape
    count = cols // tile
    even = is_even()
    for r in range(rows // tile):
        here = pl.ds(r * tile, tile)
        keep = [
            mask_ref[r, i].astype(jnp.float32).astype(jnp.bfloat16) for i in range(count)
        ]
        for l in range(window):
            values = []
            for i in range(count):
                part = pl.ds(i * tile, tile)
                values.append(raw_ref[l, here, part] * keep[i])
                out_ref[l, here, part] = values[i]
            put_edges(even, values[0], values[-1], inner_ref, outer_ref, (l, here))


def screen(mask, raw, tile):
    window, rows, cols = raw.shape
    edge = shape((window, rows, tile), raw.dtype)
    return call(
        "screen",
        functools.partial(screen_kernel, tile),
        [SMEM, VMEM],
        [shape(raw.shape, raw.dtype), edge, edge],
        (mask, raw),
    )


def edges_kernel(tile, full_ref, inner_ref, outer_ref):
    window, _, cols = full_ref.shape
    even = is_even()
    for l in range(window):
        first, last = full_ref[l, :, :tile], full_ref[l, :, cols - tile :]
        put_edges(even, first, last, inner_ref, outer_ref, (l,))


def edges(full, tile):
    window, rows, cols = full.shape
    edge = shape((window, rows, tile), full.dtype)
    return call("edges", functools.partial(edges_kernel, tile), [VMEM], [edge, edge], (full,))


def dress_kernel(tile, occ_ref, own_ref, inner_ref, outer_ref, band_ref, out_ref):
    window, rows, cols = own_ref.shape
    times = band_ref.shape[0]
    count = cols // tile
    place = lax.axis_index("ao")
    even = is_even()
    inside = ((place != 0) & (place != lax.axis_size("ao") - 1)).astype(jnp.float32)
    tiles = [[] for _ in range(count + 2)]
    for m in range(window):
        inner = inner_ref[m].astype(jnp.float32)
        outer = outer_ref[m].astype(jnp.float32) * inside
        tiles[0].append(jnp.where(even, outer, inner))
        tiles[-1].append(jnp.where(even, inner, outer))
        for i in range(count):
            tiles[i + 1].append(own_ref[m, :, pl.ds(i * tile, tile)].astype(jnp.float32))
    for t in range(times):
        products = []
        for l in range(window):
            row = []
            for group in tiles:
                total = occ_ref[t, l, 0] * group[0]
                for m in range(1, window):
                    total = total + occ_ref[t, l, m] * group[m]
                row.append(total.astype(jnp.bfloat16))
            products.append(jnp.concatenate(row, axis=1))
        tall = jnp.concatenate(products, axis=0)
        for i in range(count):
            value = lax.dot_general(
                tall[:, i * tile : (i + 3) * tile],
                band_ref[t, pl.ds(i * tile, tile), :],
                NT,
                preferred_element_type=jnp.float32,
            ).astype(jnp.bfloat16)
            for l in range(window):
                out_ref[pl.ds(t * rows, rows), pl.ds(l * cols + i * tile, tile)] = value[
                    l * rows : (l + 1) * rows
                ]


def dress(occ, own, inner, outer, band, tile):
    window, rows, cols = own.shape
    times = band.shape[0]
    return call(
        "dress",
        functools.partial(dress_kernel, tile),
        [SMEM] + [VMEM] * 4,
        shape((times * rows, window * cols), jnp.bfloat16),
        (occ, own, inner, outer, band),
    )


def share_kernel(sources, width, parts, *refs):
    count = len(sources)
    dressed, blocks = refs[:parts], refs[parts : parts + count]
    earlier = refs[parts + count : -2]
    keep_ref, send_ref = refs[-2:]
    window, rows, _ = blocks[0].shape
    planes = lax.axis_size("aux")
    place = lax.axis_index("aux")
    even = is_even()
    if earlier:
        keep_ref[...] = earlier[0][...]
        send_ref[...] = earlier[1][...]
    per = rows // (2 * width)
    for source_of, block in zip(sources, blocks):
        source = source_of(place)

        @pl.when((source >= 0) & (source < planes))
        def _(block=block, source=source):
            flat = jnp.concatenate([block[l] for l in range(window)], axis=1)
            at = 0
            for left in dressed:
                total = lax.dot_general(
                    flat, left[...], NT, preferred_element_type=jnp.float32
                )
                here = pl.ds(at, left.shape[0])
                at += left.shape[0]
                for j in range(per):
                    low = total[2 * j * width : (2 * j + 1) * width]
                    high = total[(2 * j + 1) * width : (2 * j + 2) * width]
                    row = source * per + j
                    keep_ref[row, :, here] = jnp.where(even, low, high)
                    send_ref[row, :, here] = jnp.where(even, high, low).astype(jnp.bfloat16)


def share(sources, chips, width, dressed, blocks, earlier):
    dims = (chips, width, sum(d.shape[0] for d in dressed))
    args = [*dressed, *blocks, *earlier]
    return call(
        "share",
        functools.partial(share_kernel, sources, width, len(dressed)),
        [VMEM] * len(args),
        [shape(dims, jnp.float32), shape(dims, jnp.bfloat16)],
        args,
    )


def pair_kernel(keep_ref, got_ref, own_ref, *outs):
    chip = lax.axis_index("ao") // 2
    own_ref[...] = keep_ref[chip] + got_ref[chip].astype(jnp.float32)
    for k, out in enumerate(outs):
        other = chip ^ (k + 1)
        out[...] = (keep_ref[other] + got_ref[other].astype(jnp.float32)).astype(jnp.bfloat16)


def pair(keep, got):
    chips = keep.shape[0]
    dims = keep.shape[1:]
    return call(
        "pair",
        pair_kernel,
        [VMEM] * 2,
        [shape(dims, jnp.float32)] + [shape(dims, jnp.bfloat16)] * (chips - 1),
        (keep, got),
    )


def total_kernel(factor, count, own_ref, *refs):
    others, outs = refs[:-count], refs[-count:]
    total = own_ref[...]
    for other in others:
        total += other[...].astype(jnp.float32)
    total *= factor
    times, _, rows = outs[0].shape
    for n, out in enumerate(outs):
        for t in range(times):
            at = (n * times + t) * rows
            out[t] = total[:, at : at + rows]


def total(factor, times, count, own, others):
    width, both = own.shape
    dims = (times, width, both // (times * count))
    return call(
        "total",
        functools.partial(total_kernel, factor, count),
        [VMEM] * (1 + len(others)),
        [shape(dims, jnp.float32)] * count,
        (own, *others),
    )


def choose_kernel(own_ref, got_ref, out_ref):
    place = lax.axis_index("aux")
    inner = (place == 1) | (place == 2)
    out_ref[...] = jnp.where(inner, own_ref[...], got_ref[...])


def choose(own, got):
    return call("choose", choose_kernel, [VMEM] * 2, shape(own.shape, own.dtype), (own, got))


def shifted(x, axis, by):
    devices = lax.axis_size(axis)
    pairs = [(i, i + by) for i in range(devices) if 0 <= i + by < devices]
    return lax.ppermute(x, axis, pairs)


def body(three_center, occ_green, virt_band, tile_mask):
    rows, window, cols = three_center.shape
    times = virt_band.shape[0]
    tile = virt_band.shape[2] // 3
    planes, blocks = lax.axis_size("aux"), lax.axis_size("ao")
    chips = blocks // 2
    width = planes * rows // blocks
    factor = 1.0 / math.sqrt(window * cols * blocks)
    mates = [(i, i ^ 1) for i in range(blocks)]
    nexts = [(i, (i + 1 if i % 2 else i - 1) % blocks) for i in range(blocks)]

    def halo(inner, outer):
        return lax.ppermute(inner, "ao", mates), lax.ppermute(outer, "ao", nexts)

    occ = occ_green.astype(jnp.float32)
    own, inner, outer = screen(tile_mask, three_center.transpose(1, 0, 2), tile)
    if planes == 4:
        swap = [(0, 1), (1, 0), (2, 3), (3, 2)]
        beside = lax.ppermute(own, "aux", swap)
        second = lax.ppermute(own, "aux", [(0, 2), (3, 1), (1, 0), (2, 3)])
        across = lax.ppermute(own, "aux", [(1, 2), (2, 1), (0, 0), (3, 3)])
        dressed = [
            dress(occ, own, *halo(inner, outer), virt_band, tile),
            dress(occ, beside, *halo(*edges(beside, tile)), virt_band, tile),
        ]
        near = {0: (lambda z: z, own), 1: (lambda z: z ^ 1, beside)}
        far = {2: (lambda z: 3 - z, across), 3: (lambda z: z ^ 2, second)}
    else:
        held = {0: own}
        for d in range(1, planes):
            hop, part = (d + 1) // 2, d // 2
            held[d] = shifted(held[part], "aux", -hop)
            held[-d] = shifted(held[-part], "aux", hop)
        dressed = [dress(occ, own, *halo(inner, outer), virt_band, tile)]
        plan = {d: (lambda z, d=d: z + d, block) for d, block in held.items()}
        near = {d: plan[d] for d in plan if abs(d) < 2}
        far = {d: plan[d] for d in plan if abs(d) >= 2}
    sums = ()
    for group in (near, far):
        if group:
            sources, held = zip(*group.values())
            sums = share(sources, chips, width, dressed, held, sums)
    keep, send = sums
    mine, *others = pair(keep, lax.ppermute(send, "ao", mates))
    others = [
        lax.ppermute(other, "ao", [(i, i ^ (2 * k + 2)) for i in range(blocks)])
        for k, other in enumerate(others)
    ]
    outs = total(factor, times, len(dressed), mine, others)
    if planes == 4:
        out = choose(outs[0], lax.ppermute(outs[1], "aux", swap))
    else:
        out = outs[0]
    return out.transpose(0, 2, 1)


def solution(mesh):
    in_specs = (P("aux", None, "ao"), P(), P(None, "ao", None), P("aux", "ao"))
    out_specs = P(None, "aux", "ao")
    return jax.shard_map(body, mesh=mesh, in_specs=in_specs, out_specs=out_specs, check_vma=False)
```

time: 56.6 us -> 38.9 us (0.69)
  starting transfers between devices: 27.9 us -> 19 us
  Pallas kernels: 13.4 us -> 6.11 us
  local copies, waits for them, and re-layouts: 2.72 us -> 1.69 us
  other arithmetic: 0.6 us -> 0.01 us
    ppermute x9, starting transfers between devices: 24.4 us -> 15.4 us  [the longest x4 5.44 us: halo(): return (lax.ppermute(inner, 'ao', mates), lax.ppermute(outer, 'ao', nexts))]
    pallas_call x6 -> x9, Pallas kernels: 13.4 us -> 6.11 us  [call(): pl.pallas_call(body, out_shape=outs, in_specs=specs, out_specs=VMEM if si...]
    ppermute x3, waiting for transfers between devices: 3.58 us -> 4.64 us  [body(): lax.ppermute(other, 'ao', [(i, i ^ 2 * k + 2) for i in range(blocks)])]
    unnamed x26 -> x8, local copies, waits for them, and re-layouts: 2.72 us -> 1.69 us
    convert_element_type x1, other arithmetic: 0.6 us -> 0.01 us  [body(): occ = occ_green.astype(jnp.float32)]
    ppermute x9, waiting for transfers between devices: 7.8 us -> 7.21 us  [the longest x1 2.25 us: body(): out = choose(outs[0], lax.ppermute(outs[1], 'aux', swap))]
  transfers between devices with their start and end apart: 12 -> 12, of which waited for: 7 -> 7; matrix products, arithmetic and copies ran while one was open for 1% -> 0% of each run, Pallas kernels for 10% -> 10%
where the time goes in v2:
time: 38.9 us; the launch traced here: 38.7 us
  starting transfers between devices  19 us (49%)
  waiting for transfers between devices  11.9 us (31%)
  Pallas kernels  6.11 us (16%)
  local copies, waits for them, and re-layouts  1.69 us (4%)
    pallas_call x9, Pallas kernels, call(): pl.pallas_call(body, out_shape=outs, in_specs=specs, out_specs=VMEM if si...  6.11 us
    ppermute x4, starting transfers between devices, halo(): return (lax.ppermute(inner, 'ao', mates), lax.ppermute(outer, 'ao', nexts))  5.44 us
    ppermute x3, waiting for transfers between devices, body(): lax.ppermute(other, 'ao', [(i, i ^ 2 * k + 2) for i in range(blocks)])  4.64 us
    ppermute x3, starting transfers between devices, body(): lax.ppermute(other, 'ao', [(i, i ^ 2 * k + 2) for i in range(blocks)])  3.59 us
    ppermute x1, starting transfers between devices, body(): out = choose(outs[0], lax.ppermute(outs[1], 'aux', swap))  3.51 us
    ppermute x1, starting transfers between devices, body(): beside = lax.ppermute(own, 'aux', swap)  3.09 us
    ppermute x1, starting transfers between devices, body(): second = lax.ppermute(own, 'aux', [(0, 2), (3, 1), (1, 0), (2, 3)])  2.59 us
    ppermute x1, waiting for transfers between devices, body(): out = choose(outs[0], lax.ppermute(outs[1], 'aux', swap))  2.25 us
  transfers between devices with their start and end apart: 12, of which 7 were waited for; matrix products, arithmetic and copies ran while one was open for 0% of the time, Pallas kernels for 10%

profile of v2, /device:TPU:0, one launch (start us, length us, event | category | flops | bytes accessed | tf_op | source)
XLA Modules:
  0.0 38.7 jit_solution(1741122725266774897)
XLA Ops:
  0.0 1.0 %copy-done.1 = bf16[128,3,384]{2,0,1:T(8,128)(2,1)S(1)} copy-done((bf16[128,3,384]{2,0,1:T(8,128)(2,1)S(1)}, bf16[128,3,384]{2,0,1:T(8,128)(2,1)}, u32[]{:S(2)}) %copy-start.1) | copy-done | bytes 294936
  1.0 0.7 %copy-done.2 = s32[1,3]{1,0:T(1,128)S(1)} copy-done((s32[1,3]{1,0:T(1,128)S(1)}, s32[1,3]{1,0:T(1,128)}, u32[]{:S(2)}) %copy-start.2) | copy-done | bytes 36
  1.7 0.6 %screen.1 = (bf16[3,128,384]{2,1,0:T(8,128)(2,1)S(1)}, bf16[3,128,128]{2,1,0:T(8,128)(2,1)S(1)}, bf16[3,128,128]{2,1,0:T(8,128)(2,1)S(1)}) custom-call(s32[1,3]{1,0:T(1,128)S(1)} %copy-done.2, bf16[3,128,384]{2,1,0:T(8,128)(2,1)S(1)} %bitcast.2), custom_call_target="tpu_custom_call" | custom-call | tf_op jit(solution)/shard_map/screen/pallas_call | solution.py:23
  2.3 3.1 %collective-permute-start.2 = (bf16[3,128,384]{2,1,0:T(8,128)(2,1)S(1)}, bf16[3,128,384]{2,1,0:T(8,128)(2,1)S(1)}, u32[]{:S(2)}, u32[]{:S(2)}) collective-permute-start(bf16[3,128,384]{2,1,0:T(8,128)(2,1)S(1)} %get-tuple-element.20.own_ref.refs_2_), channel_id=1, source_target_pairs={{0,8},{8,0},{16,24},{24,16},{1,9},{9,1},{17,25},{25,17},{2,10},{10... | collective-permute-start | bytes 884744 | tf_op jit(solution)/shard_map/ppermute | solution.py:262
  5.4 0.0 collective-permute-start
  5.4 2.6 %collective-permute-start.6 = (bf16[3,128,384]{2,1,0:T(8,128)(2,1)S(1)}, bf16[3,128,384]{2,1,0:T(8,128)(2,1)S(1)}, u32[]{:S(2)}, u32[]{:S(2)}) collective-permute-start(bf16[3,128,384]{2,1,0:T(8,128)(2,1)S(1)} %get-tuple-element.20.own_ref.refs_2_), channel_id=1, source_target_pairs={{0,16},{24,8},{8,0},{16,24},{1,17},{25,9},{9,1},{17,25},{2,18},{26... | collective-permute-start | bytes 884744 | tf_op jit(solution)/shard_map/ppermute | solution.py:263
  8.0 0.7 %collective-permute-start.5 = (bf16[3,128,384]{2,1,0:T(8,128)(2,1)S(1)}, bf16[3,128,384]{2,1,0:T(8,128)(2,1)S(1)}, u32[]{:S(2)}, u32[]{:S(2)}) collective-permute-start(bf16[3,128,384]{2,1,0:T(8,128)(2,1)S(1)} %get-tuple-element.20.own_ref.refs_2_), channel_id=1, source_target_pairs={{8,16},{16,8},{0,0},{24,24},{9,17},{17,9},{1,1},{25,25},{10,18},{1... | collective-permute-start | bytes 884744 | tf_op jit(solution)/shard_map/ppermute | solution.py:264
  8.7 2.3 %collective-permute-start.1 = (bf16[3,128,128]{2,1,0:T(8,128)(2,1)S(1)}, bf16[3,128,128]{2,1,0:T(8,128)(2,1)S(1)}, u32[]{:S(2)}, u32[]{:S(2)}) collective-permute-start(bf16[3,128,128]{2,1,0:T(8,128)(2,1)S(1)} %get-tuple-element.22), channel_id=1, source_target_pairs={{0,7},{1,2},{2,1},{3,4},{4,3},{5,6},{6,5},{7,0},{8,15},{9,10},{10,... | collective-permute-start | bytes 294920 | tf_op jit(solution)/shard_map/ppermute | solution.py:256
  11.0 2.2 %collective-permute-done.2.full_ref.own_ref.refs_3_ = bf16[3,128,384]{2,1,0:T(8,128)(2,1)S(1)} collective-permute-done((bf16[3,128,384]{2,1,0:T(8,128)(2,1)S(1)}, bf16[3,128,384]{2,1,0:T(8,128)(2,1)S(1)}, u32[]{:S(2)}, u32[]{:S(2)}) %collective-permute-start.2) | collective-permute-done | bytes 294944 | tf_op jit(solution)/shard_map/ppermute | solution.py:262
  13.3 0.0 copy-start.3
  13.3 0.1 collective-permute-start.3
  13.4 0.0 collective-permute-done.inner_ref
  13.4 3.0 %collective-permute-start.4 = (bf16[3,128,128]{2,1,0:T(8,128)(2,1)S(1)}, bf16[3,128,128]{2,1,0:T(8,128)(2,1)S(1)}, u32[]{:S(2)}, u32[]{:S(2)}) collective-permute-start(bf16[3,128,128]{2,1,0:T(8,128)(2,1)S(1)} %get-tuple-element.24), channel_id=1, source_target_pairs={{0,7},{1,2},{2,1},{3,4},{4,3},{5,6},{6,5},{7,0},{8,15},{9,10},{10,... | collective-permute-start | bytes 294920 | tf_op jit(solution)/shard_map/ppermute | solution.py:256
  16.4 0.0 collective-permute-done.1.outer_ref
  16.4 1.3 %dress.2.refs_0_ = bf16[256,1152]{1,0:T(8,128)(2,1)S(1)} custom-call(f32[2,3,3]{2,1,0:T(4,128)S(1)} %copy_convert_fusion.occ_ref, bf16[3,128,384]{2,1,0:T(8,128)(2,1)S(1)} %get-tuple-element.20.own_ref.refs_2_, bf16[3,128,128]{2,1,0:T(8,128)(2,1)S(1)} %collective-permute-done.inner_ref, bf16[3,128,128]{2,1,0:T(8,128)(2,1)S(1)} %collective-permute-done.1.outer_ref, ...), custom_call_target="tpu_custom_call" | custom-call | tf_op jit(solution)/shard_map/dress/pallas_call | solution.py:23
  17.7 0.0 collective-permute-done.3.inner_ref
  17.7 1.2 %collective-permute-done.4.outer_ref = bf16[3,128,128]{2,1,0:T(8,128)(2,1)S(1)} collective-permute-done((bf16[3,128,128]{2,1,0:T(8,128)(2,1)S(1)}, bf16[3,128,128]{2,1,0:T(8,128)(2,1)S(1)}, u32[]{:S(2)}, u32[]{:S(2)}) %collective-permute-start.4) | collective-permute-done | bytes 98336 | tf_op jit(solution)/shard_map/ppermute | solution.py:256
  19.0 1.3 %dress.3.refs_1_ = bf16[256,1152]{1,0:T(8,128)(2,1)S(1)} custom-call(f32[2,3,3]{2,1,0:T(4,128)S(1)} %copy_convert_fusion.occ_ref, bf16[3,128,384]{2,1,0:T(8,128)(2,1)S(1)} %collective-permute-done.2.full_ref.own_ref.refs_3_, bf16[3,128,128]{2,1,0:T(8,128)(2,1)S(1)} %collective-permute-done.3.inner_ref, ...), custom_call_target="tpu_custom_call" | custom-call | tf_op jit(solution)/shard_map/dress/pallas_call | solution.py:23
  20.3 1.0 %share.2 = (f32[4,64,512]{2,1,0:T(8,128)S(1)}, bf16[4,64,512]{2,1,0:T(8,128)(2,1)S(1)}) custom-call(bf16[256,1152]{1,0:T(8,128)(2,1)S(1)} %dress.2.refs_0_, bf16[256,1152]{1,0:T(8,128)(2,1)S(1)} %dress.3.refs_1_, bf16[3,128,384]{2,1,0:T(8,128)(2,1)S(1)} %get-tuple-element.20.own_ref.refs_2_, ...), custom_call_target="tpu_custom_call" | custom-call | tf_op jit(solution)/shard_map/share/pallas_call | solution.py:23
  21.3 0.0 collective-permute-done.6.refs_3_
  21.3 1.1 %share.3 = (f32[4,64,512]{2,1,0:T(8,128)S(1)}, bf16[4,64,512]{2,1,0:T(8,128)(2,1)S(1)}) custom-call(bf16[256,1152]{1,0:T(8,128)(2,1)S(1)} %dress.2.refs_0_, bf16[256,1152]{1,0:T(8,128)(2,1)S(1)} %dress.3.refs_1_, bf16[3,128,384]{2,1,0:T(8,128)(2,1)S(1)} %collective-permute-done.5.refs_2_, bf16[3,128,384]{2,1,0:T(8,128)(2,1)S(1)} %collective-permute-done.6.refs_3_, ...), custom_call_target="tpu_custom_call" | custom-call | tf_op jit(solution)/shard_map/share/pallas_call | solution.py:23
  22.4 0.1 collective-permute-start.7
  22.5 1.5 %collective-permute-done.7.got_ref = bf16[4,64,512]{2,1,0:T(8,128)(2,1)S(1)} collective-permute-done((bf16[4,64,512]{2,1,0:T(8,128)(2,1)S(1)}, bf16[4,64,512]{2,1,0:T(8,128)(2,1)S(1)}, u32[]{:S(2)}, u32[]{:S(2)}) %collective-permute-start.7) | collective-permute-done | bytes 262176 | tf_op jit(solution)/shard_map/ppermute | solution.py:287
  24.1 2.0 %collective-permute-start.8 = (bf16[64,512]{1,0:T(8,128)(2,1)S(1)}, bf16[64,512]{1,0:T(8,128)(2,1)S(1)}, u32[]{:S(2)}, u32[]{:S(2)}) collective-permute-start(bf16[64,512]{1,0:T(8,128)(2,1)S(1)} %get-tuple-element.30), channel_id=1, source_target_pairs={{0,2},{1,3},{2,0},{3,1},{4,6},{5,7},{6,4},{7,5},{8,10},{9,11},{10,... | collective-permute-start | bytes 196616 | tf_op jit(solution)/shard_map/ppermute | solution.py:289
  26.1 1.0 %collective-permute-start.9 = (bf16[64,512]{1,0:T(8,128)(2,1)S(1)}, bf16[64,512]{1,0:T(8,128)(2,1)S(1)}, u32[]{:S(2)}, u32[]{:S(2)}) collective-permute-start(bf16[64,512]{1,0:T(8,128)(2,1)S(1)} %get-tuple-element.31), channel_id=1, source_target_pairs={{0,4},{1,5},{2,6},{3,7},{4,0},{5,1},{6,2},{7,3},{8,12},{9,13},{10,... | collective-permute-start | bytes 196616 | tf_op jit(solution)/shard_map/ppermute | solution.py:289
  27.1 0.5 %collective-permute-start.10 = (bf16[64,512]{1,0:T(8,128)(2,1)S(1)}, bf16[64,512]{1,0:T(8,128)(2,1)S(1)}, u32[]{:S(2)}, u32[]{:S(2)}) collective-permute-start(bf16[64,512]{1,0:T(8,128)(2,1)S(1)} %get-tuple-element.32), channel_id=1, source_target_pairs={{0,6},{1,7},{2,4},{3,5},{4,2},{5,3},{6,0},{7,1},{8,14},{9,15},{10,... | collective-permute-start | bytes 196616 | tf_op jit(solution)/shard_map/ppermute | solution.py:289
  27.7 1.1 %collective-permute-done.8.refs_0_ = bf16[64,512]{1,0:T(8,128)(2,1)S(1)} collective-permute-done((bf16[64,512]{1,0:T(8,128)(2,1)S(1)}, bf16[64,512]{1,0:T(8,128)(2,1)S(1)}, u32[]{:S(2)}, u32[]{:S(2)}) %collective-permute-start.8) | collective-permute-done | bytes 65568 | tf_op jit(solution)/shard_map/ppermute | solution.py:289
  28.7 1.6 %collective-permute-done.9.refs_1_ = bf16[64,512]{1,0:T(8,128)(2,1)S(1)} collective-permute-done((bf16[64,512]{1,0:T(8,128)(2,1)S(1)}, bf16[64,512]{1,0:T(8,128)(2,1)S(1)}, u32[]{:S(2)}, u32[]{:S(2)}) %collective-permute-start.9) | collective-permute-done | bytes 65568 | tf_op jit(solution)/shard_map/ppermute | solution.py:289
  30.4 1.9 %collective-permute-done.10.refs_2_ = bf16[64,512]{1,0:T(8,128)(2,1)S(1)} collective-permute-done((bf16[64,512]{1,0:T(8,128)(2,1)S(1)}, bf16[64,512]{1,0:T(8,128)(2,1)S(1)}, u32[]{:S(2)}, u32[]{:S(2)}) %collective-permute-start.10) | collective-permute-done | bytes 65568 | tf_op jit(solution)/shard_map/ppermute | solution.py:289
  32.3 3.5 %collective-permute-start.11 = (f32[2,64,128]{2,1,0:T(8,128)S(1)}, f32[2,64,128]{2,1,0:T(8,128)S(1)}, u32[]{:S(2)}, u32[]{:S(2)}) collective-permute-start(f32[2,64,128]{2,1,0:T(8,128)S(1)} %get-tuple-element.34), channel_id=1, source_target_pairs={{0,8},{8,0},{16,24},{24,16},{1,9},{9,1},{17,25},{25,17},{2,10},{10... | collective-permute-start | bytes 196616 | tf_op jit(solution)/shard_map/ppermute | solution.py:294
  35.9 2.2 %collective-permute-done.11.got_ref = f32[2,64,128]{2,1,0:T(8,128)S(1)} collective-permute-done((f32[2,64,128]{2,1,0:T(8,128)S(1)}, f32[2,64,128]{2,1,0:T(8,128)S(1)}, u32[]{:S(2)}, u32[]{:S(2)}) %collective-permute-start.11) | collective-permute-done | bytes 65568 | tf_op jit(solution)/shard_map/ppermute | solution.py:294
  38.1 0.6 %choose.1 = f32[2,64,128]{2,1,0:T(8,128)} custom-call(f32[2,64,128]{2,1,0:T(8,128)S(1)} %get-tuple-element.33.own_ref, f32[2,64,128]{2,1,0:T(8,128)S(1)} %collective-permute-done.11.got_ref), custom_call_target="tpu_custom_call" | custom-call | tf_op jit(solution)/shard_map/choose/pallas_call | solution.py:23
  (10 shorter events, 0.1 us)
Async XLA Ops:
  0.0 16.4 %copy-start = (bf16[2,384,384]{2,1,0:T(8,128)(2,1)S(1)}, bf16[2,384,384]{2,1,0:T(8,128)(2,1)}, u32[]{:S(2)}) copy-start(bf16[2,384,384]{2,1,0:T(8,128)(2,1)} %band_ref.3) | copy-start | bytes 1769476
  0.0 1.0 %copy-start.1 = (bf16[128,3,384]{2,0,1:T(8,128)(2,1)S(1)}, bf16[128,3,384]{2,0,1:T(8,128)(2,1)}, u32[]{:S(2)}) copy-start(bf16[128,3,384]{2,0,1:T(8,128)(2,1)} %param.4) | copy-start | bytes 884740
  1.0 0.7 %copy-start.2 = (s32[1,3]{1,0:T(1,128)S(1)}, s32[1,3]{1,0:T(1,128)}, u32[]{:S(2)}) copy-start(s32[1,3]{1,0:T(1,128)} %mask_ref.1) | copy-start | bytes 40
  2.3 10.9 %collective-permute-start.2 = (bf16[3,128,384]{2,1,0:T(8,128)(2,1)S(1)}, bf16[3,128,384]{2,1,0:T(8,128)(2,1)S(1)}, u32[]{:S(2)}, u32[]{:S(2)}) collective-permute-start(bf16[3,128,384]{2,1,0:T(8,128)(2,1)S(1)} %get-tuple-element.20.own_ref.refs_2_), channel_id=1, source_target_pairs={{0,8},{8,0},{16,24},{24,16},{1,9},{9,1},{17,25},{25,17},{2,10},{10... | collective-permute-start | bytes 884744 | tf_op jit(solution)/shard_map/ppermute | solution.py:262
  5.4 8.0 %collective-permute-start = (bf16[3,128,128]{2,1,0:T(8,128)(2,1)S(1)}, bf16[3,128,128]{2,1,0:T(8,128)(2,1)S(1)}, u32[]{:S(2)}, u32[]{:S(2)}) collective-permute-start(bf16[3,128,128]{2,1,0:T(8,128)(2,1)S(1)} %get-tuple-element.21), channel_id=1, source_target_pairs={{0,1},{1,0},{2,3},{3,2},{4,5},{5,4},{6,7},{7,6},{8,9},{9,8},{10,11... | collective-permute-start | bytes 294920 | tf_op jit(solution)/shard_map/ppermute | solution.py:256
  5.4 15.9 %collective-permute-start.6 = (bf16[3,128,384]{2,1,0:T(8,128)(2,1)S(1)}, bf16[3,128,384]{2,1,0:T(8,128)(2,1)S(1)}, u32[]{:S(2)}, u32[]{:S(2)}) collective-permute-start(bf16[3,128,384]{2,1,0:T(8,128)(2,1)S(1)} %get-tuple-element.20.own_ref.refs_2_), channel_id=1, source_target_pairs={{0,16},{24,8},{8,0},{16,24},{1,17},{25,9},{9,1},{17,25},{2,18},{26... | collective-permute-start | bytes 884744 | tf_op jit(solution)/shard_map/ppermute | solution.py:263
  8.0 13.3 %collective-permute-start.5 = (bf16[3,128,384]{2,1,0:T(8,128)(2,1)S(1)}, bf16[3,128,384]{2,1,0:T(8,128)(2,1)S(1)}, u32[]{:S(2)}, u32[]{:S(2)}) collective-permute-start(bf16[3,128,384]{2,1,0:T(8,128)(2,1)S(1)} %get-tuple-element.20.own_ref.refs_2_), channel_id=1, source_target_pairs={{8,16},{16,8},{0,0},{24,24},{9,17},{17,9},{1,1},{25,25},{10,18},{1... | collective-permute-start | bytes 884744 | tf_op jit(solution)/shard_map/ppermute | solution.py:264
  8.7 7.7 %collective-permute-start.1 = (bf16[3,128,128]{2,1,0:T(8,128)(2,1)S(1)}, bf16[3,128,128]{2,1,0:T(8,128)(2,1)S(1)}, u32[]{:S(2)}, u32[]{:S(2)}) collective-permute-start(bf16[3,128,128]{2,1,0:T(8,128)(2,1)S(1)} %get-tuple-element.22), channel_id=1, source_target_pairs={{0,7},{1,2},{2,1},{3,4},{4,3},{5,6},{6,5},{7,0},{8,15},{9,10},{10,... | collective-permute-start | bytes 294920 | tf_op jit(solution)/shard_map/ppermute | solution.py:256
  13.3 3.1 %copy-start.3 = (bf16[2,3,3]{2,0,1:T(2,128)(2,1)S(1)}, bf16[2,3,3]{2,0,1:T(2,128)(2,1)}, u32[]{:S(2)}) copy-start(bf16[2,3,3]{2,0,1:T(2,128)(2,1)} %param.5) | copy-start | bytes 112
  13.3 4.4 %collective-permute-start.3 = (bf16[3,128,128]{2,1,0:T(8,128)(2,1)S(1)}, bf16[3,128,128]{2,1,0:T(8,128)(2,1)S(1)}, u32[]{:S(2)}, u32[]{:S(2)}) collective-permute-start(bf16[3,128,128]{2,1,0:T(8,128)(2,1)S(1)} %get-tuple-element.23), channel_id=1, source_target_pairs={{0,1},{1,0},{2,3},{3,2},{4,5},{5,4},{6,7},{7,6},{8,9},{9,8},{10,11... | collective-permute-start | bytes 294920 | tf_op jit(solution)/shard_map/ppermute | solution.py:256
  13.4 5.6 %collective-permute-start.4 = (bf16[3,128,128]{2,1,0:T(8,128)(2,1)S(1)}, bf16[3,128,128]{2,1,0:T(8,128)(2,1)S(1)}, u32[]{:S(2)}, u32[]{:S(2)}) collective-permute-start(bf16[3,128,128]{2,1,0:T(8,128)(2,1)S(1)} %get-tuple-element.24), channel_id=1, source_target_pairs={{0,7},{1,2},{2,1},{3,4},{4,3},{5,6},{6,5},{7,0},{8,15},{9,10},{10,... | collective-permute-start | bytes 294920 | tf_op jit(solution)/shard_map/ppermute | solution.py:256
  22.4 1.6 %collective-permute-start.7 = (bf16[4,64,512]{2,1,0:T(8,128)(2,1)S(1)}, bf16[4,64,512]{2,1,0:T(8,128)(2,1)S(1)}, u32[]{:S(2)}, u32[]{:S(2)}) collective-permute-start(bf16[4,64,512]{2,1,0:T(8,128)(2,1)S(1)} %get-tuple-element.28), channel_id=1, source_target_pairs={{0,1},{1,0},{2,3},{3,2},{4,5},{5,4},{6,7},{7,6},{8,9},{9,8},{10,11... | collective-permute-start | bytes 786440 | tf_op jit(solution)/shard_map/ppermute | solution.py:287
  24.1 4.7 %collective-permute-start.8 = (bf16[64,512]{1,0:T(8,128)(2,1)S(1)}, bf16[64,512]{1,0:T(8,128)(2,1)S(1)}, u32[]{:S(2)}, u32[]{:S(2)}) collective-permute-start(bf16[64,512]{1,0:T(8,128)(2,1)S(1)} %get-tuple-element.30), channel_id=1, source_target_pairs={{0,2},{1,3},{2,0},{3,1},{4,6},{5,7},{6,4},{7,5},{8,10},{9,11},{10,... | collective-permute-start | bytes 196616 | tf_op jit(solution)/shard_map/ppermute | solution.py:289
  26.1 4.3 %collective-permute-start.9 = (bf16[64,512]{1,0:T(8,128)(2,1)S(1)}, bf16[64,512]{1,0:T(8,128)(2,1)S(1)}, u32[]{:S(2)}, u32[]{:S(2)}) collective-permute-start(bf16[64,512]{1,0:T(8,128)(2,1)S(1)} %get-tuple-element.31), channel_id=1, source_target_pairs={{0,4},{1,5},{2,6},{3,7},{4,0},{5,1},{6,2},{7,3},{8,12},{9,13},{10,... | collective-permute-start | bytes 196616 | tf_op jit(solution)/shard_map/ppermute | solution.py:289
  27.1 5.2 %collective-permute-start.10 = (bf16[64,512]{1,0:T(8,128)(2,1)S(1)}, bf16[64,512]{1,0:T(8,128)(2,1)S(1)}, u32[]{:S(2)}, u32[]{:S(2)}) collective-permute-start(bf16[64,512]{1,0:T(8,128)(2,1)S(1)} %get-tuple-element.32), channel_id=1, source_target_pairs={{0,6},{1,7},{2,4},{3,5},{4,2},{5,3},{6,0},{7,1},{8,14},{9,15},{10,... | collective-permute-start | bytes 196616 | tf_op jit(solution)/shard_map/ppermute | solution.py:289
  32.3 5.8 %collective-permute-start.11 = (f32[2,64,128]{2,1,0:T(8,128)S(1)}, f32[2,64,128]{2,1,0:T(8,128)S(1)}, u32[]{:S(2)}, u32[]{:S(2)}) collective-permute-start(f32[2,64,128]{2,1,0:T(8,128)S(1)} %get-tuple-element.34), channel_id=1, source_target_pairs={{0,8},{8,0},{16,24},{24,16},{1,9},{9,1},{17,25},{25,17},{2,10},{10... | collective-permute-start | bytes 196616 | tf_op jit(solution)/shard_map/ppermute | solution.py:294

commit v3 on v2

--- a/solution.py
+++ b/solution.py
@@ -9,7 +9,6 @@
 from jax.sharding import PartitionSpec as P
 
 VMEM = pl.BlockSpec(memory_space=pltpu.VMEM)
-SMEM = pl.BlockSpec(memory_space=pltpu.SMEM)
 PARAMS = pltpu.CompilerParams(vmem_limit_bytes=16 * 1024 * 1024)
 NT = (((1,), (1,)), ((), ()))
 
@@ -34,56 +33,29 @@
     return lax.rem(lax.axis_index("ao"), 2) == 0
 
 
-def put_edges(even, first, last, inner_ref, outer_ref, here):
-    inner_ref[here] = jnp.where(even, last, first)
-    outer_ref[here] = jnp.where(even, first, last)
-
-
-def screen_kernel(tile, mask_ref, raw_ref, out_ref, inner_ref, outer_ref):
-    window, rows, cols = raw_ref.shape
-    count = cols // tile
-    even = is_even()
-    for r in range(rows // tile):
-        here = pl.ds(r * tile, tile)
-        keep = [
-            mask_ref[r, i].astype(jnp.float32).astype(jnp.bfloat16) for i in range(count)
-        ]
-        for l in range(window):
-            values = []
-            for i in range(count):
-                part = pl.ds(i * tile, tile)
-                values.append(raw_ref[l, here, part] * keep[i])
-                out_ref[l, here, part] = values[i]
-            put_edges(even, values[0], values[-1], inner_ref, outer_ref, (l, here))
-
-
-def screen(mask, raw, tile):
-    window, rows, cols = raw.shape
-    edge = shape((window, rows, tile), raw.dtype)
-    return call(
-        "screen",
-        functools.partial(screen_kernel, tile),
-        [SMEM, VMEM],
-        [shape(raw.shape, raw.dtype), edge, edge],
-        (mask, raw),
-    )
-
-
-def edges_kernel(tile, full_ref, inner_ref, outer_ref):
+def edge_kernel(tile, inner, full_ref, *refs):
+    out_ref = refs[-1]
     window, _, cols = full_ref.shape
-    even = is_even()
+    at_end = is_even() if inner else jnp.logical_not(is_even())
     for l in range(window):
         first, last = full_ref[l, :, :tile], full_ref[l, :, cols - tile :]
-        put_edges(even, first, last, inner_ref, outer_ref, (l,))
-
-
-def edges(full, tile):
+        out_ref[l] = jnp.where(at_end, last, first)
+
+
+def edge(inner, full, tile, after=()):
     window, rows, cols = full.shape
-    edge = shape((window, rows, tile), full.dtype)
-    return call("edges", functools.partial(edges_kernel, tile), [VMEM], [edge, edge], (full,))
-
-
-def dress_kernel(tile, occ_ref, own_ref, inner_ref, outer_ref, band_ref, out_ref):
+    return pl.pallas_call(
+        functools.partial(edge_kernel, tile, inner),
+        out_shape=shape((window, rows, tile), full.dtype),
+        in_specs=[VMEM] + [pl.BlockSpec(memory_space=pl.ANY)] * len(after),
+        out_specs=VMEM,
+        compiler_params=PARAMS,
+        name="edge",
+    )(full, *after)
+
+
+def dress_kernel(tile, occ_ref, own_ref, inner_ref, outer_ref, band_ref, *refs):
+    out_ref = refs[-1]
     window, rows, cols = own_ref.shape
     times = band_ref.shape[0]
     count = cols // tile
@@ -98,14 +70,19 @@
         tiles[-1].append(jnp.where(even, inner, outer))
         for i in range(count):
             tiles[i + 1].append(own_ref[m, :, pl.ds(i * tile, tile)].astype(jnp.float32))
+    green = [occ_ref[l].astype(jnp.float32) for l in range(window)]
     for t in range(times):
         products = []
         for l in range(window):
             row = []
+            gains = [
+                jnp.broadcast_to(green[l][t : t + 1, m : m + 1], (rows, tile))
+                for m in range(window)
+            ]
             for group in tiles:
-                total = occ_ref[t, l, 0] * group[0]
+                total = gains[0] * group[0]
                 for m in range(1, window):
-                    total = total + occ_ref[t, l, m] * group[m]
+                    total = total + gains[m] * group[m]
                 row.append(total.astype(jnp.bfloat16))
             products.append(jnp.concatenate(row, axis=1))
         tall = jnp.concatenate(products, axis=0)
@@ -122,15 +99,15 @@
                 ]
 
 
-def dress(occ, own, inner, outer, band, tile):
+def dress(occ, own, inner, outer, band, tile, after=()):
     window, rows, cols = own.shape
     times = band.shape[0]
     return call(
         "dress",
         functools.partial(dress_kernel, tile),
-        [SMEM] + [VMEM] * 4,
+        [VMEM] * 5 + [pl.BlockSpec(memory_space=pl.ANY)] * len(after),
         shape((times * rows, window * cols), jnp.bfloat16),
-        (occ, own, inner, outer, band),
+        (occ, own, inner, outer, band, *after),
     )
 
 
@@ -147,25 +124,40 @@
         keep_ref[...] = earlier[0][...]
         send_ref[...] = earlier[1][...]
     per = rows // (2 * width)
-    for source_of, block in zip(sources, blocks):
-        source = source_of(place)
-
-        @pl.when((source >= 0) & (source < planes))
-        def _(block=block, source=source):
-            flat = jnp.concatenate([block[l] for l in range(window)], axis=1)
-            at = 0
-            for left in dressed:
-                total = lax.dot_general(
-                    flat, left[...], NT, preferred_element_type=jnp.float32
+
+    def flat(block):
+        return jnp.concatenate([block[l] for l in range(window)], axis=1)
+
+    def put(total, source, here):
+        for j in range(per):
+            low = total[2 * j * width : (2 * j + 1) * width]
+            high = total[(2 * j + 1) * width : (2 * j + 2) * width]
+            row = source * per + j
+            keep_ref[row, :, here] = jnp.where(even, low, high)
+            send_ref[row, :, here] = jnp.where(even, high, low).astype(jnp.bfloat16)
+
+    at = 0
+    for left in dressed:
+        here = pl.ds(at, left.shape[0])
+        at += left.shape[0]
+        if parts > 1:
+            tall = jnp.concatenate([flat(block) for block in blocks], axis=0)
+            total = lax.dot_general(tall, left[...], NT, preferred_element_type=jnp.float32)
+            for n, source_of in enumerate(sources):
+                put(total[n * rows : (n + 1) * rows], source_of(place), here)
+            continue
+        for source_of, block in zip(sources, blocks):
+            source = source_of(place)
+
+            @pl.when((source >= 0) & (source < planes))
+            def _(block=block, source=source, left=left, here=here):
+                put(
+                    lax.dot_general(
+                        flat(block), left[...], NT, preferred_element_type=jnp.float32
+                    ),
+                    source,
+                    here,
                 )
-                here = pl.ds(at, left.shape[0])
-                at += left.shape[0]
-                for j in range(per):
-                    low = total[2 * j * width : (2 * j + 1) * width]
-                    high = total[(2 * j + 1) * width : (2 * j + 2) * width]
-                    row = source * per + j
-                    keep_ref[row, :, here] = jnp.where(even, low, high)
-                    send_ref[row, :, here] = jnp.where(even, high, low).astype(jnp.bfloat16)
 
 
 def share(sources, chips, width, dressed, blocks, earlier):
@@ -252,20 +244,25 @@
     mates = [(i, i ^ 1) for i in range(blocks)]
     nexts = [(i, (i + 1 if i % 2 else i - 1) % blocks) for i in range(blocks)]
 
-    def halo(inner, outer):
+    def halo(full):
+        inner, outer = edge(True, full, tile), edge(False, full, tile)
         return lax.ppermute(inner, "ao", mates), lax.ppermute(outer, "ao", nexts)
 
-    occ = occ_green.astype(jnp.float32)
-    own, inner, outer = screen(tile_mask, three_center.transpose(1, 0, 2), tile)
+    occ = occ_green.transpose(1, 0, 2)
+    mask = tile_mask.astype(jnp.bfloat16)[None, :, None, :, None]
+    split = (window, rows // tile, tile, cols // tile, tile)
+    own = three_center.transpose(1, 0, 2).reshape(split) * mask
+    own = own.reshape(window, rows, cols)
     if planes == 4:
         swap = [(0, 1), (1, 0), (2, 3), (3, 2)]
+        across = lax.ppermute(own, "aux", [(1, 2), (2, 1), (0, 0), (3, 3)])
         beside = lax.ppermute(own, "aux", swap)
         second = lax.ppermute(own, "aux", [(0, 2), (3, 1), (1, 0), (2, 3)])
-        across = lax.ppermute(own, "aux", [(1, 2), (2, 1), (0, 0), (3, 3)])
-        dressed = [
-            dress(occ, own, *halo(inner, outer), virt_band, tile),
-            dress(occ, beside, *halo(*edges(beside, tile)), virt_band, tile),
-        ]
+        facing = edge(False, beside, tile)
+        dressed = [dress(occ, own, *halo(own), virt_band, tile, (facing,))]
+        outer = lax.ppermute(facing, "ao", nexts)
+        inner = lax.ppermute(edge(True, beside, tile, dressed), "ao", mates)
+        dressed.append(dress(occ, beside, inner, outer, virt_band, tile))
         near = {0: (lambda z: z, own), 1: (lambda z: z ^ 1, beside)}
         far = {2: (lambda z: 3 - z, across), 3: (lambda z: z ^ 2, second)}
     else:
@@ -274,7 +271,7 @@
             hop, part = (d + 1) // 2, d // 2
             held[d] = shifted(held[part], "aux", -hop)
             held[-d] = shifted(held[-part], "aux", hop)
-        dressed = [dress(occ, own, *halo(inner, outer), virt_band, tile)]
+        dressed = [dress(occ, own, *halo(own), virt_band, tile)]
         plan = {d: (lambda z, d=d: z + d, block) for d, block in held.items()}
         near = {d: plan[d] for d in plan if abs(d) < 2}
         far = {d: plan[d] for d in plan if abs(d) >= 2}

time: 38.9 us -> 36.9 us (0.949)
  Pallas kernels: 6.11 us -> 3.55 us
  other arithmetic: 0.01 us -> 1.65 us
  local copies, waits for them, and re-layouts: 1.69 us -> 0.09 us
  waiting for transfers between devices: 11.9 us -> 12.4 us
    ppermute x4 -> x2, starting transfers between devices: 5.44 us -> 2.68 us  [halo(): return (lax.ppermute(inner, 'ao', mates), lax.ppermute(outer, 'ao', nexts))]
    pallas_call x9 -> x7, Pallas kernels: 6.11 us -> 3.43 us  [call(): pl.pallas_call(body, out_shape=outs, in_specs=specs, out_specs=VMEM if si...]
    ppermute x0 -> x2, waiting for transfers between devices: none -> 2.45 us  [the longest x1 2.45 us: body(): outer = lax.ppermute(facing, 'ao', nexts)]
    ppermute x0 -> x2, starting transfers between devices: none -> 1.75 us  [the longest x1 1.33 us: body(): inner = lax.ppermute(edge(True, beside, tile, dressed), 'ao', mates)]
    unnamed x8 -> x4, local copies, waits for them, and re-layouts: 1.69 us -> 0.01 us
    mul x0 -> x2, other arithmetic: none -> 1.65 us  [body(): own = three_center.transpose(1, 0, 2).reshape(split) * mask]
    ppermute x1, starting transfers between devices: 3.51 us -> 4.48 us  [body(): out = choose(outs[0], lax.ppermute(outs[1], 'aux', swap))]
    ppermute x3, waiting for transfers between devices: 4.64 us -> 3.88 us  [body(): lax.ppermute(other, 'ao', [(i, i ^ 2 * k + 2) for i in range(blocks)])]
  transfers between devices with their start and end apart: 12 -> 12, of which waited for: 7 -> 8; matrix products, arithmetic and copies ran while one was open for 0% -> 0% of each run, Pallas kernels for 10% -> 6%
where the time goes in v3:
time: 36.9 us; the launch traced here: 36.7 us
  starting transfers between devices  18.9 us (51%)
  waiting for transfers between devices  12.4 us (34%)
  Pallas kernels  3.55 us (10%)
  other arithmetic  1.65 us (4%)
    ppermute x1, starting transfers between devices, body(): out = choose(outs[0], lax.ppermute(outs[1], 'aux', swap))  4.48 us
    ppermute x3, waiting for transfers between devices, body(): lax.ppermute(other, 'ao', [(i, i ^ 2 * k + 2) for i in range(blocks)])  3.88 us
    ppermute x3, starting transfers between devices, body(): lax.ppermute(other, 'ao', [(i, i ^ 2 * k + 2) for i in range(blocks)])  3.55 us
    pallas_call x7, Pallas kernels, call(): pl.pallas_call(body, out_shape=outs, in_specs=specs, out_specs=VMEM if si...  3.43 us
    ppermute x1, starting transfers between devices, body(): beside = lax.ppermute(own, 'aux', swap)  3.09 us
    ppermute x2, starting transfers between devices, halo(): return (lax.ppermute(inner, 'ao', mates), lax.ppermute(outer, 'ao', nexts))  2.68 us
    ppermute x1, starting transfers between devices, body(): second = lax.ppermute(own, 'aux', [(0, 2), (3, 1), (1, 0), (2, 3)])  2.59 us
    ppermute x1, waiting for transfers between devices, body(): outer = lax.ppermute(facing, 'ao', nexts)  2.45 us
  transfers between devices with their start and end apart: 12, of which 8 were waited for; matrix products, arithmetic and copies ran while one was open for 0% of the time, Pallas kernels for 6%

profile of v3, /device:TPU:0, one launch (start us, length us, event | category | flops | bytes accessed | tf_op | source)
XLA Modules:
  0.0 36.7 jit_solution(14711761614019618353)
XLA Ops:
  0.0 0.7 %convert_bitcast_fusion = bf16[3]{0:T(256)(128)(2,1)S(1)} fusion(s32[1,3]{1,0:T(1,128)} %param.7), kind=kLoop, calls=%fused_computation.1 | loop fusion | flops 3 | bytes 18 | tf_op jit(solution)/shard_map/mul | solution.py:254
  0.7 0.1 broadcast_bitcast_fusion
  0.7 1.0 %multiply_bitcast_fusion.full_ref.own_ref.refs_2_ = bf16[3,128,384]{2,1,0:T(8,128)(2,1)S(1)} fusion(bf16[128,3,384]{2,0,1:T(8,128)(2,1)} %param.4, bf16[384]{0:T(512)(128)(2,1)S(1)} %broadcast_bitcast_fusion), kind=kLoop, calls=%fused_computation | loop fusion | flops 147456 | bytes 590592 | tf_op jit(solution)/shard_map/mul | solution.py:254
  1.7 0.0 copy-start
  1.7 3.1 %collective-permute-start.2 = (bf16[3,128,384]{2,1,0:T(8,128)(2,1)S(1)}, bf16[3,128,384]{2,1,0:T(8,128)(2,1)S(1)}, u32[]{:S(2)}, u32[]{:S(2)}) collective-permute-start(bf16[3,128,384]{2,1,0:T(8,128)(2,1)S(1)} %multiply_bitcast_fusion.full_ref.own_ref.refs_2_), channel_id=1, source_target_pairs={{0,8},{8,0},{16,24},{24,16},{1,9},{9,1},{17,25},{25,17},{2,10},{10... | collective-permute-start | bytes 884744 | tf_op jit(solution)/shard_map/ppermute | solution.py:259
  4.8 2.6 %collective-permute-start.6 = (bf16[3,128,384]{2,1,0:T(8,128)(2,1)S(1)}, bf16[3,128,384]{2,1,0:T(8,128)(2,1)S(1)}, u32[]{:S(2)}, u32[]{:S(2)}) collective-permute-start(bf16[3,128,384]{2,1,0:T(8,128)(2,1)S(1)} %multiply_bitcast_fusion.full_ref.own_ref.refs_2_), channel_id=1, source_target_pairs={{0,16},{24,8},{8,0},{16,24},{1,17},{25,9},{9,1},{17,25},{2,18},{26... | collective-permute-start | bytes 884744 | tf_op jit(solution)/shard_map/ppermute | solution.py:260
  7.4 0.7 %collective-permute-start.5 = (bf16[3,128,384]{2,1,0:T(8,128)(2,1)S(1)}, bf16[3,128,384]{2,1,0:T(8,128)(2,1)S(1)}, u32[]{:S(2)}, u32[]{:S(2)}) collective-permute-start(bf16[3,128,384]{2,1,0:T(8,128)(2,1)S(1)} %multiply_bitcast_fusion.full_ref.own_ref.refs_2_), channel_id=1, source_target_pairs={{8,16},{16,8},{0,0},{24,24},{9,17},{17,9},{1,1},{25,25},{10,18},{1... | collective-permute-start | bytes 884744 | tf_op jit(solution)/shard_map/ppermute | solution.py:258
  8.1 0.1 collective-permute-start
  8.2 2.6 %collective-permute-start.1 = (bf16[3,128,128]{2,1,0:T(8,128)(2,1)S(1)}, bf16[3,128,128]{2,1,0:T(8,128)(2,1)S(1)}, u32[]{:S(2)}, u32[]{:S(2)}) collective-permute-start(bf16[3,128,128]{2,1,0:T(8,128)(2,1)S(1)} %edge.5), channel_id=1, source_target_pairs={{0,7},{1,2},{2,1},{3,4},{4,3},{5,6},{6,5},{7,0},{8,15},{9,10},{10,... | collective-permute-start | bytes 294920 | tf_op jit(solution)/shard_map/ppermute | solution.py:249
  10.9 1.8 %collective-permute-done.2.full_ref.own_ref.refs_3_ = bf16[3,128,384]{2,1,0:T(8,128)(2,1)S(1)} collective-permute-done((bf16[3,128,384]{2,1,0:T(8,128)(2,1)S(1)}, bf16[3,128,384]{2,1,0:T(8,128)(2,1)S(1)}, u32[]{:S(2)}, u32[]{:S(2)}) %collective-permute-start.2) | collective-permute-done | bytes 294944 | tf_op jit(solution)/shard_map/ppermute | solution.py:259
  12.7 0.0 copy-start.1
  12.7 0.4 %collective-permute-start.4 = (bf16[3,128,128]{2,1,0:T(8,128)(2,1)S(1)}, bf16[3,128,128]{2,1,0:T(8,128)(2,1)S(1)}, u32[]{:S(2)}, u32[]{:S(2)}) collective-permute-start(bf16[3,128,128]{2,1,0:T(8,128)(2,1)S(1)} %edge.6.refs_0_), channel_id=1, source_target_pairs={{0,7},{1,2},{2,1},{3,4},{4,3},{5,6},{6,5},{7,0},{8,15},{9,10},{10,... | collective-permute-start | bytes 294920 | tf_op jit(solution)/shard_map/ppermute | solution.py:263
  13.1 0.0 collective-permute-done.inner_ref
  13.1 0.5 %collective-permute-done.1.outer_ref = bf16[3,128,128]{2,1,0:T(8,128)(2,1)S(1)} collective-permute-done((bf16[3,128,128]{2,1,0:T(8,128)(2,1)S(1)}, bf16[3,128,128]{2,1,0:T(8,128)(2,1)S(1)}, u32[]{:S(2)}, u32[]{:S(2)}) %collective-permute-start.1) | collective-permute-done | bytes 98336 | tf_op jit(solution)/shard_map/ppermute | solution.py:249
  13.6 0.8 %dress.2.refs_0_ = bf16[256,1152]{1,0:T(8,128)(2,1)S(1)} custom-call(bf16[3,2,3]{2,1,0:T(2,128)(2,1)S(1)} %bitcast.8, bf16[3,128,384]{2,1,0:T(8,128)(2,1)S(1)} %multiply_bitcast_fusion.full_ref.own_ref.refs_2_, bf16[3,128,128]{2,1,0:T(8,128)(2,1)S(1)} %collective-permute-done.inner_ref, bf16[3,128,128]{2,1,0:T(8,128)(2,1)S(1)} %collective-permute-done.1.outer_ref, ...), custom_call_target="tpu_custom_call" | custom-call | tf_op jit(solution)/shard_map/dress/pallas_call | solution.py:22
  14.5 1.3 %collective-permute-start.3 = (bf16[3,128,128]{2,1,0:T(8,128)(2,1)S(1)}, bf16[3,128,128]{2,1,0:T(8,128)(2,1)S(1)}, u32[]{:S(2)}, u32[]{:S(2)}) collective-permute-start(bf16[3,128,128]{2,1,0:T(8,128)(2,1)S(1)} %edge.7), channel_id=1, source_target_pairs={{0,1},{1,0},{2,3},{3,2},{4,5},{5,4},{6,7},{7,6},{8,9},{9,8},{10,11... | collective-permute-start | bytes 294920 | tf_op jit(solution)/shard_map/ppermute | solution.py:264
  15.8 2.4 %collective-permute-done.4.outer_ref = bf16[3,128,128]{2,1,0:T(8,128)(2,1)S(1)} collective-permute-done((bf16[3,128,128]{2,1,0:T(8,128)(2,1)S(1)}, bf16[3,128,128]{2,1,0:T(8,128)(2,1)S(1)}, u32[]{:S(2)}, u32[]{:S(2)}) %collective-permute-start.4) | collective-permute-done | bytes 98336 | tf_op jit(solution)/shard_map/ppermute | solution.py:263
  18.2 0.0 collective-permute-done.3.inner_ref
  18.2 0.8 %dress.3.refs_1_ = bf16[256,1152]{1,0:T(8,128)(2,1)S(1)} custom-call(bf16[3,2,3]{2,1,0:T(2,128)(2,1)S(1)} %bitcast.9, bf16[3,128,384]{2,1,0:T(8,128)(2,1)S(1)} %collective-permute-done.2.full_ref.own_ref.refs_3_, bf16[3,128,128]{2,1,0:T(8,128)(2,1)S(1)} %collective-permute-done.3.inner_ref, bf16[3,128,128]{2,1,0:T(8,128)(2,1)S(1)} %collective-permute-done.4.outer_ref, ...), custom_call_target="tpu_custom_call" | custom-call | tf_op jit(solution)/shard_map/dress/pallas_call | solution.py:22
  19.1 0.6 %share.2 = (f32[4,64,512]{2,1,0:T(8,128)S(1)}, bf16[4,64,512]{2,1,0:T(8,128)(2,1)S(1)}) custom-call(bf16[256,1152]{1,0:T(8,128)(2,1)S(1)} %dress.2.refs_0_, bf16[256,1152]{1,0:T(8,128)(2,1)S(1)} %dress.3.refs_1_, bf16[3,128,384]{2,1,0:T(8,128)(2,1)S(1)} %multiply_bitcast_fusion.full_ref.own_ref.refs_2_, ...), custom_call_target="tpu_custom_call" | custom-call | tf_op jit(solution)/shard_map/share/pallas_call | solution.py:22
  19.6 0.6 %share.3 = (f32[4,64,512]{2,1,0:T(8,128)S(1)}, bf16[4,64,512]{2,1,0:T(8,128)(2,1)S(1)}) custom-call(bf16[256,1152]{1,0:T(8,128)(2,1)S(1)} %dress.2.refs_0_, bf16[256,1152]{1,0:T(8,128)(2,1)S(1)} %dress.3.refs_1_, bf16[3,128,384]{2,1,0:T(8,128)(2,1)S(1)} %collective-permute-done.5.refs_2_, bf16[3,128,384]{2,1,0:T(8,128)(2,1)S(1)} %collective-permute-done.6.refs_3_, ...), custom_call_target="tpu_custom_call" | custom-call | tf_op jit(solution)/shard_map/share/pallas_call | solution.py:22
  20.2 0.1 collective-permute-start.7
  20.3 1.5 %collective-permute-done.7.got_ref = bf16[4,64,512]{2,1,0:T(8,128)(2,1)S(1)} collective-permute-done((bf16[4,64,512]{2,1,0:T(8,128)(2,1)S(1)}, bf16[4,64,512]{2,1,0:T(8,128)(2,1)S(1)}, u32[]{:S(2)}, u32[]{:S(2)}) %collective-permute-start.7) | collective-permute-done | bytes 262176 | tf_op jit(solution)/shard_map/ppermute | solution.py:284
  21.8 0.6 %collective-permute-start.8 = (bf16[64,512]{1,0:T(8,128)(2,1)S(1)}, bf16[64,512]{1,0:T(8,128)(2,1)S(1)}, u32[]{:S(2)}, u32[]{:S(2)}) collective-permute-start(bf16[64,512]{1,0:T(8,128)(2,1)S(1)} %get-tuple-element.20), channel_id=1, source_target_pairs={{0,2},{1,3},{2,0},{3,1},{4,6},{5,7},{6,4},{7,5},{8,10},{9,11},{10,... | collective-permute-start | bytes 196616 | tf_op jit(solution)/shard_map/ppermute | solution.py:286
  22.5 1.7 %collective-permute-start.9 = (bf16[64,512]{1,0:T(8,128)(2,1)S(1)}, bf16[64,512]{1,0:T(8,128)(2,1)S(1)}, u32[]{:S(2)}, u32[]{:S(2)}) collective-permute-start(bf16[64,512]{1,0:T(8,128)(2,1)S(1)} %get-tuple-element.21), channel_id=1, source_target_pairs={{0,4},{1,5},{2,6},{3,7},{4,0},{5,1},{6,2},{7,3},{8,12},{9,13},{10,... | collective-permute-start | bytes 196616 | tf_op jit(solution)/shard_map/ppermute | solution.py:286
  24.1 1.3 %collective-permute-start.10 = (bf16[64,512]{1,0:T(8,128)(2,1)S(1)}, bf16[64,512]{1,0:T(8,128)(2,1)S(1)}, u32[]{:S(2)}, u32[]{:S(2)}) collective-permute-start(bf16[64,512]{1,0:T(8,128)(2,1)S(1)} %get-tuple-element.22), channel_id=1, source_target_pairs={{0,6},{1,7},{2,4},{3,5},{4,2},{5,3},{6,0},{7,1},{8,14},{9,15},{10,... | collective-permute-start | bytes 196616 | tf_op jit(solution)/shard_map/ppermute | solution.py:286
  25.4 0.9 %collective-permute-done.8.refs_0_ = bf16[64,512]{1,0:T(8,128)(2,1)S(1)} collective-permute-done((bf16[64,512]{1,0:T(8,128)(2,1)S(1)}, bf16[64,512]{1,0:T(8,128)(2,1)S(1)}, u32[]{:S(2)}, u32[]{:S(2)}) %collective-permute-start.8) | collective-permute-done | bytes 65568 | tf_op jit(solution)/shard_map/ppermute | solution.py:286
  26.3 0.4 %collective-permute-done.9.refs_1_ = bf16[64,512]{1,0:T(8,128)(2,1)S(1)} collective-permute-done((bf16[64,512]{1,0:T(8,128)(2,1)S(1)}, bf16[64,512]{1,0:T(8,128)(2,1)S(1)}, u32[]{:S(2)}, u32[]{:S(2)}) %collective-permute-start.9) | collective-permute-done | bytes 65568 | tf_op jit(solution)/shard_map/ppermute | solution.py:286
  26.7 2.6 %collective-permute-done.10.refs_2_ = bf16[64,512]{1,0:T(8,128)(2,1)S(1)} collective-permute-done((bf16[64,512]{1,0:T(8,128)(2,1)S(1)}, bf16[64,512]{1,0:T(8,128)(2,1)S(1)}, u32[]{:S(2)}, u32[]{:S(2)}) %collective-permute-start.10) | collective-permute-done | bytes 65568 | tf_op jit(solution)/shard_map/ppermute | solution.py:286
  29.3 4.5 %collective-permute-start.11 = (f32[2,64,128]{2,1,0:T(8,128)S(1)}, f32[2,64,128]{2,1,0:T(8,128)S(1)}, u32[]{:S(2)}, u32[]{:S(2)}) collective-permute-start(f32[2,64,128]{2,1,0:T(8,128)S(1)} %get-tuple-element.24), channel_id=1, source_target_pairs={{0,8},{8,0},{16,24},{24,16},{1,9},{9,1},{17,25},{25,17},{2,10},{10... | collective-permute-start | bytes 196616 | tf_op jit(solution)/shard_map/ppermute | solution.py:291
  33.8 2.2 %collective-permute-done.11.got_ref = f32[2,64,128]{2,1,0:T(8,128)S(1)} collective-permute-done((f32[2,64,128]{2,1,0:T(8,128)S(1)}, f32[2,64,128]{2,1,0:T(8,128)S(1)}, u32[]{:S(2)}, u32[]{:S(2)}) %collective-permute-start.11) | collective-permute-done | bytes 65568 | tf_op jit(solution)/shard_map/ppermute | solution.py:291
  36.0 0.6 %choose.1 = f32[2,64,128]{2,1,0:T(8,128)} custom-call(f32[2,64,128]{2,1,0:T(8,128)S(1)} %get-tuple-element.23.own_ref, f32[2,64,128]{2,1,0:T(8,128)S(1)} %collective-permute-done.11.got_ref), custom_call_target="tpu_custom_call" | custom-call | tf_op jit(solution)/shard_map/choose/pallas_call | solution.py:22
  (10 shorter events, 0.2 us)
Async XLA Ops:
  1.7 11.9 %copy-start = (bf16[2,384,384]{2,1,0:T(8,128)(2,1)S(1)}, bf16[2,384,384]{2,1,0:T(8,128)(2,1)}, u32[]{:S(2)}) copy-start(bf16[2,384,384]{2,1,0:T(8,128)(2,1)} %band_ref.3) | copy-start | bytes 1769476
  1.7 10.9 %collective-permute-start.2 = (bf16[3,128,384]{2,1,0:T(8,128)(2,1)S(1)}, bf16[3,128,384]{2,1,0:T(8,128)(2,1)S(1)}, u32[]{:S(2)}, u32[]{:S(2)}) collective-permute-start(bf16[3,128,384]{2,1,0:T(8,128)(2,1)S(1)} %multiply_bitcast_fusion.full_ref.own_ref.refs_2_), channel_id=1, source_target_pairs={{0,8},{8,0},{16,24},{24,16},{1,9},{9,1},{17,25},{25,17},{2,10},{10... | collective-permute-start | bytes 884744 | tf_op jit(solution)/shard_map/ppermute | solution.py:259
  4.8 14.8 %collective-permute-start.6 = (bf16[3,128,384]{2,1,0:T(8,128)(2,1)S(1)}, bf16[3,128,384]{2,1,0:T(8,128)(2,1)S(1)}, u32[]{:S(2)}, u32[]{:S(2)}) collective-permute-start(bf16[3,128,384]{2,1,0:T(8,128)(2,1)S(1)} %multiply_bitcast_fusion.full_ref.own_ref.refs_2_), channel_id=1, source_target_pairs={{0,16},{24,8},{8,0},{16,24},{1,17},{25,9},{9,1},{17,25},{2,18},{26... | collective-permute-start | bytes 884744 | tf_op jit(solution)/shard_map/ppermute | solution.py:260
  7.4 12.2 %collective-permute-start.5 = (bf16[3,128,384]{2,1,0:T(8,128)(2,1)S(1)}, bf16[3,128,384]{2,1,0:T(8,128)(2,1)S(1)}, u32[]{:S(2)}, u32[]{:S(2)}) collective-permute-start(bf16[3,128,384]{2,1,0:T(8,128)(2,1)S(1)} %multiply_bitcast_fusion.full_ref.own_ref.refs_2_), channel_id=1, source_target_pairs={{8,16},{16,8},{0,0},{24,24},{9,17},{17,9},{1,1},{25,25},{10,18},{1... | collective-permute-start | bytes 884744 | tf_op jit(solution)/shard_map/ppermute | solution.py:258
  8.1 5.0 %collective-permute-start = (bf16[3,128,128]{2,1,0:T(8,128)(2,1)S(1)}, bf16[3,128,128]{2,1,0:T(8,128)(2,1)S(1)}, u32[]{:S(2)}, u32[]{:S(2)}) collective-permute-start(bf16[3,128,128]{2,1,0:T(8,128)(2,1)S(1)} %edge.4), channel_id=1, source_target_pairs={{0,1},{1,0},{2,3},{3,2},{4,5},{5,4},{6,7},{7,6},{8,9},{9,8},{10,11... | collective-permute-start | bytes 294920 | tf_op jit(solution)/shard_map/ppermute | solution.py:249
  8.2 5.4 %collective-permute-start.1 = (bf16[3,128,128]{2,1,0:T(8,128)(2,1)S(1)}, bf16[3,128,128]{2,1,0:T(8,128)(2,1)S(1)}, u32[]{:S(2)}, u32[]{:S(2)}) collective-permute-start(bf16[3,128,128]{2,1,0:T(8,128)(2,1)S(1)} %edge.5), channel_id=1, source_target_pairs={{0,7},{1,2},{2,1},{3,4},{4,3},{5,6},{6,5},{7,0},{8,15},{9,10},{10,... | collective-permute-start | bytes 294920 | tf_op jit(solution)/shard_map/ppermute | solution.py:249
  12.7 0.9 %copy-start.1 = (bf16[2,3,3]{2,0,1:T(2,128)(2,1)S(1)}, bf16[2,3,3]{2,0,1:T(2,128)(2,1)}, u32[]{:S(2)}) copy-start(bf16[2,3,3]{2,0,1:T(2,128)(2,1)} %param.5) | copy-start | bytes 112
  12.7 5.5 %collective-permute-start.4 = (bf16[3,128,128]{2,1,0:T(8,128)(2,1)S(1)}, bf16[3,128,128]{2,1,0:T(8,128)(2,1)S(1)}, u32[]{:S(2)}, u32[]{:S(2)}) collective-permute-start(bf16[3,128,128]{2,1,0:T(8,128)(2,1)S(1)} %edge.6.refs_0_), channel_id=1, source_target_pairs={{0,7},{1,2},{2,1},{3,4},{4,3},{5,6},{6,5},{7,0},{8,15},{9,10},{10,... | collective-permute-start | bytes 294920 | tf_op jit(solution)/shard_map/ppermute | solution.py:263
  14.5 3.8 %collective-permute-start.3 = (bf16[3,128,128]{2,1,0:T(8,128)(2,1)S(1)}, bf16[3,128,128]{2,1,0:T(8,128)(2,1)S(1)}, u32[]{:S(2)}, u32[]{:S(2)}) collective-permute-start(bf16[3,128,128]{2,1,0:T(8,128)(2,1)S(1)} %edge.7), channel_id=1, source_target_pairs={{0,1},{1,0},{2,3},{3,2},{4,5},{5,4},{6,7},{7,6},{8,9},{9,8},{10,11... | collective-permute-start | bytes 294920 | tf_op jit(solution)/shard_map/ppermute | solution.py:264
  20.2 1.6 %collective-permute-start.7 = (bf16[4,64,512]{2,1,0:T(8,128)(2,1)S(1)}, bf16[4,64,512]{2,1,0:T(8,128)(2,1)S(1)}, u32[]{:S(2)}, u32[]{:S(2)}) collective-permute-start(bf16[4,64,512]{2,1,0:T(8,128)(2,1)S(1)} %get-tuple-element.18), channel_id=1, source_target_pairs={{0,1},{1,0},{2,3},{3,2},{4,5},{5,4},{6,7},{7,6},{8,9},{9,8},{10,11... | collective-permute-start | bytes 786440 | tf_op jit(solution)/shard_map/ppermute | solution.py:284
  21.8 4.5 %collective-permute-start.8 = (bf16[64,512]{1,0:T(8,128)(2,1)S(1)}, bf16[64,512]{1,0:T(8,128)(2,1)S(1)}, u32[]{:S(2)}, u32[]{:S(2)}) collective-permute-start(bf16[64,512]{1,0:T(8,128)(2,1)S(1)} %get-tuple-element.20), channel_id=1, source_target_pairs={{0,2},{1,3},{2,0},{3,1},{4,6},{5,7},{6,4},{7,5},{8,10},{9,11},{10,... | collective-permute-start | bytes 196616 | tf_op jit(solution)/shard_map/ppermute | solution.py:286
  22.5 4.3 %collective-permute-start.9 = (bf16[64,512]{1,0:T(8,128)(2,1)S(1)}, bf16[64,512]{1,0:T(8,128)(2,1)S(1)}, u32[]{:S(2)}, u32[]{:S(2)}) collective-permute-start(bf16[64,512]{1,0:T(8,128)(2,1)S(1)} %get-tuple-element.21), channel_id=1, source_target_pairs={{0,4},{1,5},{2,6},{3,7},{4,0},{5,1},{6,2},{7,3},{8,12},{9,13},{10,... | collective-permute-start | bytes 196616 | tf_op jit(solution)/shard_map/ppermute | solution.py:286
  24.1 5.2 %collective-permute-start.10 = (bf16[64,512]{1,0:T(8,128)(2,1)S(1)}, bf16[64,512]{1,0:T(8,128)(2,1)S(1)}, u32[]{:S(2)}, u32[]{:S(2)}) collective-permute-start(bf16[64,512]{1,0:T(8,128)(2,1)S(1)} %get-tuple-element.22), channel_id=1, source_target_pairs={{0,6},{1,7},{2,4},{3,5},{4,2},{5,3},{6,0},{7,1},{8,14},{9,15},{10,... | collective-permute-start | bytes 196616 | tf_op jit(solution)/shard_map/ppermute | solution.py:286
  29.3 6.7 %collective-permute-start.11 = (f32[2,64,128]{2,1,0:T(8,128)S(1)}, f32[2,64,128]{2,1,0:T(8,128)S(1)}, u32[]{:S(2)}, u32[]{:S(2)}) collective-permute-start(f32[2,64,128]{2,1,0:T(8,128)S(1)} %get-tuple-element.24), channel_id=1, source_target_pairs={{0,8},{8,0},{16,24},{24,16},{1,9},{9,1},{17,25},{25,17},{2,10},{10... | collective-permute-start | bytes 196616 | tf_op jit(solution)/shard_map/ppermute | solution.py:291

commit v4 on v3

--- a/solution.py
+++ b/solution.py
@@ -202,7 +202,7 @@
     for n, out in enumerate(outs):
         for t in range(times):
             at = (n * times + t) * rows
-            out[t] = total[:, at : at + rows]
+            out[t] = total[:, at : at + rows].astype(out.dtype)
 
 
 def total(factor, times, count, own, others):
@@ -212,7 +212,7 @@
         "total",
         functools.partial(total_kernel, factor, count),
         [VMEM] * (1 + len(others)),
-        [shape(dims, jnp.float32)] * count,
+        [shape(dims, jnp.float32)] + [shape(dims, jnp.bfloat16)] * (count - 1),
         (own, *others),
     )
 
@@ -220,7 +220,7 @@
 def choose_kernel(own_ref, got_ref, out_ref):
     place = lax.axis_index("aux")
     inner = (place == 1) | (place == 2)
-    out_ref[...] = jnp.where(inner, own_ref[...], got_ref[...])
+    out_ref[...] = jnp.where(inner, own_ref[...], got_ref[...].astype(jnp.float32))
 
 
 def choose(own, got):
@@ -264,7 +264,7 @@
         inner = lax.ppermute(edge(True, beside, tile, dressed), "ao", mates)
         dressed.append(dress(occ, beside, inner, outer, virt_band, tile))
         near = {0: (lambda z: z, own), 1: (lambda z: z ^ 1, beside)}
-        far = {2: (lambda z: 3 - z, across), 3: (lambda z: z ^ 2, second)}
+        far = {3: (lambda z: z ^ 2, second), 2: (lambda z: 3 - z, across)}
     else:
         held = {0: own}
         for d in range(1, planes):

time: 36.9 us -> 36.2 us (0.981)
  waiting for transfers between devices: 12.4 us -> 11.7 us
    ppermute x1, starting transfers between devices: 2.59 us -> 3.88 us  [body(): second = lax.ppermute(own, 'aux', [(0, 2), (3, 1), (1, 0), (2, 3)])]
    ppermute x2, waiting for transfers between devices: 0.49 us -> 1.78 us  [halo(): return (lax.ppermute(inner, 'ao', mates), lax.ppermute(outer, 'ao', nexts))]
    ppermute x1, waiting for transfers between devices: 1.81 us -> 0.52 us  [body(): beside = lax.ppermute(own, 'aux', swap)]
    ppermute x1, starting transfers between devices: 1.33 us -> 0.35 us  [body(): inner = lax.ppermute(edge(True, beside, tile, dressed), 'ao', mates)]
where the time goes in v4:
time: 36.2 us; the launch traced here: 36 us
  starting transfers between devices  18.9 us (52%)
  waiting for transfers between devices  11.7 us (32%)
  Pallas kernels  3.54 us (10%)
  other arithmetic  1.65 us (5%)
    ppermute x1, starting transfers between devices, body(): out = choose(outs[0], lax.ppermute(outs[1], 'aux', swap))  4.16 us
    ppermute x1, starting transfers between devices, body(): second = lax.ppermute(own, 'aux', [(0, 2), (3, 1), (1, 0), (2, 3)])  3.88 us
    ppermute x3, waiting for transfers between devices, body(): lax.ppermute(other, 'ao', [(i, i ^ 2 * k + 2) for i in range(blocks)])  3.88 us
    ppermute x3, starting transfers between devices, body(): lax.ppermute(other, 'ao', [(i, i ^ 2 * k + 2) for i in range(blocks)])  3.55 us
    pallas_call x7, Pallas kernels, call(): pl.pallas_call(body, out_shape=outs, in_specs=specs, out_specs=VMEM if si...  3.42 us
    ppermute x1, starting transfers between devices, body(): beside = lax.ppermute(own, 'aux', swap)  3.09 us
    ppermute x2, starting transfers between devices, halo(): return (lax.ppermute(inner, 'ao', mates), lax.ppermute(outer, 'ao', nexts))  2.68 us
    ppermute x1, waiting for transfers between devices, body(): outer = lax.ppermute(facing, 'ao', nexts)  2.14 us
  transfers between devices with their start and end apart: 12, of which 8 were waited for; matrix products, arithmetic and copies ran while one was open for 0% of the time, Pallas kernels for 6%

profile of v4, /device:TPU:0, one launch (start us, length us, event | category | flops | bytes accessed | tf_op | source)
XLA Modules:
  0.0 36.0 jit_solution(13584582279743663254)
XLA Ops:
  0.0 0.7 %convert_bitcast_fusion = bf16[3]{0:T(256)(128)(2,1)S(1)} fusion(s32[1,3]{1,0:T(1,128)} %param.7), kind=kLoop, calls=%fused_computation.1 | loop fusion | flops 3 | bytes 18 | tf_op jit(solution)/shard_map/mul | solution.py:254
  0.7 0.1 broadcast_bitcast_fusion
  0.7 1.0 %multiply_bitcast_fusion.full_ref.own_ref.refs_2_ = bf16[3,128,384]{2,1,0:T(8,128)(2,1)S(1)} fusion(bf16[128,3,384]{2,0,1:T(8,128)(2,1)} %param.4, bf16[384]{0:T(512)(128)(2,1)S(1)} %broadcast_bitcast_fusion), kind=kLoop, calls=%fused_computation | loop fusion | flops 147456 | bytes 590592 | tf_op jit(solution)/shard_map/mul | solution.py:254
  1.7 0.0 copy-start
  1.7 3.1 %collective-permute-start.2 = (bf16[3,128,384]{2,1,0:T(8,128)(2,1)S(1)}, bf16[3,128,384]{2,1,0:T(8,128)(2,1)S(1)}, u32[]{:S(2)}, u32[]{:S(2)}) collective-permute-start(bf16[3,128,384]{2,1,0:T(8,128)(2,1)S(1)} %multiply_bitcast_fusion.full_ref.own_ref.refs_2_), channel_id=1, source_target_pairs={{0,8},{8,0},{16,24},{24,16},{1,9},{9,1},{17,25},{25,17},{2,10},{10... | collective-permute-start | bytes 884744 | tf_op jit(solution)/shard_map/ppermute | solution.py:259
  4.8 0.7 %collective-permute-start.6 = (bf16[3,128,384]{2,1,0:T(8,128)(2,1)S(1)}, bf16[3,128,384]{2,1,0:T(8,128)(2,1)S(1)}, u32[]{:S(2)}, u32[]{:S(2)}) collective-permute-start(bf16[3,128,384]{2,1,0:T(8,128)(2,1)S(1)} %multiply_bitcast_fusion.full_ref.own_ref.refs_2_), channel_id=1, source_target_pairs={{8,16},{16,8},{0,0},{24,24},{9,17},{17,9},{1,1},{25,25},{10,18},{1... | collective-permute-start | bytes 884744 | tf_op jit(solution)/shard_map/ppermute | solution.py:258
  5.5 3.9 %collective-permute-start.5 = (bf16[3,128,384]{2,1,0:T(8,128)(2,1)S(1)}, bf16[3,128,384]{2,1,0:T(8,128)(2,1)S(1)}, u32[]{:S(2)}, u32[]{:S(2)}) collective-permute-start(bf16[3,128,384]{2,1,0:T(8,128)(2,1)S(1)} %multiply_bitcast_fusion.full_ref.own_ref.refs_2_), channel_id=1, source_target_pairs={{0,16},{24,8},{8,0},{16,24},{1,17},{25,9},{9,1},{17,25},{2,18},{26... | collective-permute-start | bytes 884744 | tf_op jit(solution)/shard_map/ppermute | solution.py:260
  9.4 0.1 collective-permute-start
  9.5 2.6 %collective-permute-start.1 = (bf16[3,128,128]{2,1,0:T(8,128)(2,1)S(1)}, bf16[3,128,128]{2,1,0:T(8,128)(2,1)S(1)}, u32[]{:S(2)}, u32[]{:S(2)}) collective-permute-start(bf16[3,128,128]{2,1,0:T(8,128)(2,1)S(1)} %edge.5), channel_id=1, source_target_pairs={{0,7},{1,2},{2,1},{3,4},{4,3},{5,6},{6,5},{7,0},{8,15},{9,10},{10,... | collective-permute-start | bytes 294920 | tf_op jit(solution)/shard_map/ppermute | solution.py:249
  12.1 0.5 %collective-permute-done.2.full_ref.own_ref.refs_3_ = bf16[3,128,384]{2,1,0:T(8,128)(2,1)S(1)} collective-permute-done((bf16[3,128,384]{2,1,0:T(8,128)(2,1)S(1)}, bf16[3,128,384]{2,1,0:T(8,128)(2,1)S(1)}, u32[]{:S(2)}, u32[]{:S(2)}) %collective-permute-start.2) | collective-permute-done | bytes 294944 | tf_op jit(solution)/shard_map/ppermute | solution.py:259
  12.7 0.0 copy-start.1
  12.7 0.4 %collective-permute-start.4 = (bf16[3,128,128]{2,1,0:T(8,128)(2,1)S(1)}, bf16[3,128,128]{2,1,0:T(8,128)(2,1)S(1)}, u32[]{:S(2)}, u32[]{:S(2)}) collective-permute-start(bf16[3,128,128]{2,1,0:T(8,128)(2,1)S(1)} %edge.6.refs_0_), channel_id=1, source_target_pairs={{0,7},{1,2},{2,1},{3,4},{4,3},{5,6},{6,5},{7,0},{8,15},{9,10},{10,... | collective-permute-start | bytes 294920 | tf_op jit(solution)/shard_map/ppermute | solution.py:263
  13.1 0.0 collective-permute-done.inner_ref
  13.1 1.8 %collective-permute-done.1.outer_ref = bf16[3,128,128]{2,1,0:T(8,128)(2,1)S(1)} collective-permute-done((bf16[3,128,128]{2,1,0:T(8,128)(2,1)S(1)}, bf16[3,128,128]{2,1,0:T(8,128)(2,1)S(1)}, u32[]{:S(2)}, u32[]{:S(2)}) %collective-permute-start.1) | collective-permute-done | bytes 98336 | tf_op jit(solution)/shard_map/ppermute | solution.py:249
  14.9 0.8 %dress.2.refs_0_ = bf16[256,1152]{1,0:T(8,128)(2,1)S(1)} custom-call(bf16[3,2,3]{2,1,0:T(2,128)(2,1)S(1)} %bitcast.8, bf16[3,128,384]{2,1,0:T(8,128)(2,1)S(1)} %multiply_bitcast_fusion.full_ref.own_ref.refs_2_, bf16[3,128,128]{2,1,0:T(8,128)(2,1)S(1)} %collective-permute-done.inner_ref, bf16[3,128,128]{2,1,0:T(8,128)(2,1)S(1)} %collective-permute-done.1.outer_ref, ...), custom_call_target="tpu_custom_call" | custom-call | tf_op jit(solution)/shard_map/dress/pallas_call | solution.py:22
  15.8 0.4 collective-permute-start.3
  16.1 2.1 %collective-permute-done.4.outer_ref = bf16[3,128,128]{2,1,0:T(8,128)(2,1)S(1)} collective-permute-done((bf16[3,128,128]{2,1,0:T(8,128)(2,1)S(1)}, bf16[3,128,128]{2,1,0:T(8,128)(2,1)S(1)}, u32[]{:S(2)}, u32[]{:S(2)}) %collective-permute-start.4) | collective-permute-done | bytes 98336 | tf_op jit(solution)/shard_map/ppermute | solution.py:263
  18.2 0.0 collective-permute-done.3.inner_ref
  18.2 0.8 %dress.3.refs_1_ = bf16[256,1152]{1,0:T(8,128)(2,1)S(1)} custom-call(bf16[3,2,3]{2,1,0:T(2,128)(2,1)S(1)} %bitcast.9, bf16[3,128,384]{2,1,0:T(8,128)(2,1)S(1)} %collective-permute-done.2.full_ref.own_ref.refs_3_, bf16[3,128,128]{2,1,0:T(8,128)(2,1)S(1)} %collective-permute-done.3.inner_ref, bf16[3,128,128]{2,1,0:T(8,128)(2,1)S(1)} %collective-permute-done.4.outer_ref, ...), custom_call_target="tpu_custom_call" | custom-call | tf_op jit(solution)/shard_map/dress/pallas_call | solution.py:22
  19.1 0.6 %share.2 = (f32[4,64,512]{2,1,0:T(8,128)S(1)}, bf16[4,64,512]{2,1,0:T(8,128)(2,1)S(1)}) custom-call(bf16[256,1152]{1,0:T(8,128)(2,1)S(1)} %dress.2.refs_0_, bf16[256,1152]{1,0:T(8,128)(2,1)S(1)} %dress.3.refs_1_, bf16[3,128,384]{2,1,0:T(8,128)(2,1)S(1)} %multiply_bitcast_fusion.full_ref.own_ref.refs_2_, ...), custom_call_target="tpu_custom_call" | custom-call | tf_op jit(solution)/shard_map/share/pallas_call | solution.py:22
  19.6 0.6 %share.3 = (f32[4,64,512]{2,1,0:T(8,128)S(1)}, bf16[4,64,512]{2,1,0:T(8,128)(2,1)S(1)}) custom-call(bf16[256,1152]{1,0:T(8,128)(2,1)S(1)} %dress.2.refs_0_, bf16[256,1152]{1,0:T(8,128)(2,1)S(1)} %dress.3.refs_1_, bf16[3,128,384]{2,1,0:T(8,128)(2,1)S(1)} %collective-permute-done.5.refs_2_, bf16[3,128,384]{2,1,0:T(8,128)(2,1)S(1)} %collective-permute-done.6.refs_3_, ...), custom_call_target="tpu_custom_call" | custom-call | tf_op jit(solution)/shard_map/share/pallas_call | solution.py:22
  20.2 0.1 collective-permute-start.7
  20.3 1.5 %collective-permute-done.7.got_ref = bf16[4,64,512]{2,1,0:T(8,128)(2,1)S(1)} collective-permute-done((bf16[4,64,512]{2,1,0:T(8,128)(2,1)S(1)}, bf16[4,64,512]{2,1,0:T(8,128)(2,1)S(1)}, u32[]{:S(2)}, u32[]{:S(2)}) %collective-permute-start.7) | collective-permute-done | bytes 262176 | tf_op jit(solution)/shard_map/ppermute | solution.py:284
  21.8 0.7 %collective-permute-start.8 = (bf16[64,512]{1,0:T(8,128)(2,1)S(1)}, bf16[64,512]{1,0:T(8,128)(2,1)S(1)}, u32[]{:S(2)}, u32[]{:S(2)}) collective-permute-start(bf16[64,512]{1,0:T(8,128)(2,1)S(1)} %get-tuple-element.20), channel_id=1, source_target_pairs={{0,2},{1,3},{2,0},{3,1},{4,6},{5,7},{6,4},{7,5},{8,10},{9,11},{10,... | collective-permute-start | bytes 196616 | tf_op jit(solution)/shard_map/ppermute | solution.py:286
  22.5 1.6 %collective-permute-start.9 = (bf16[64,512]{1,0:T(8,128)(2,1)S(1)}, bf16[64,512]{1,0:T(8,128)(2,1)S(1)}, u32[]{:S(2)}, u32[]{:S(2)}) collective-permute-start(bf16[64,512]{1,0:T(8,128)(2,1)S(1)} %get-tuple-element.21), channel_id=1, source_target_pairs={{0,4},{1,5},{2,6},{3,7},{4,0},{5,1},{6,2},{7,3},{8,12},{9,13},{10,... | collective-permute-start | bytes 196616 | tf_op jit(solution)/shard_map/ppermute | solution.py:286
  24.1 1.3 %collective-permute-start.10 = (bf16[64,512]{1,0:T(8,128)(2,1)S(1)}, bf16[64,512]{1,0:T(8,128)(2,1)S(1)}, u32[]{:S(2)}, u32[]{:S(2)}) collective-permute-start(bf16[64,512]{1,0:T(8,128)(2,1)S(1)} %get-tuple-element.22), channel_id=1, source_target_pairs={{0,6},{1,7},{2,4},{3,5},{4,2},{5,3},{6,0},{7,1},{8,14},{9,15},{10,... | collective-permute-start | bytes 196616 | tf_op jit(solution)/shard_map/ppermute | solution.py:286
  25.4 0.8 %collective-permute-done.8.refs_0_ = bf16[64,512]{1,0:T(8,128)(2,1)S(1)} collective-permute-done((bf16[64,512]{1,0:T(8,128)(2,1)S(1)}, bf16[64,512]{1,0:T(8,128)(2,1)S(1)}, u32[]{:S(2)}, u32[]{:S(2)}) %collective-permute-start.8) | collective-permute-done | bytes 65568 | tf_op jit(solution)/shard_map/ppermute | solution.py:286
  26.2 0.6 %collective-permute-done.9.refs_1_ = bf16[64,512]{1,0:T(8,128)(2,1)S(1)} collective-permute-done((bf16[64,512]{1,0:T(8,128)(2,1)S(1)}, bf16[64,512]{1,0:T(8,128)(2,1)S(1)}, u32[]{:S(2)}, u32[]{:S(2)}) %collective-permute-start.9) | collective-permute-done | bytes 65568 | tf_op jit(solution)/shard_map/ppermute | solution.py:286
  26.8 2.5 %collective-permute-done.10.refs_2_ = bf16[64,512]{1,0:T(8,128)(2,1)S(1)} collective-permute-done((bf16[64,512]{1,0:T(8,128)(2,1)S(1)}, bf16[64,512]{1,0:T(8,128)(2,1)S(1)}, u32[]{:S(2)}, u32[]{:S(2)}) %collective-permute-start.10) | collective-permute-done | bytes 65568 | tf_op jit(solution)/shard_map/ppermute | solution.py:286
  29.3 4.2 %collective-permute-start.11 = (bf16[2,64,128]{2,1,0:T(8,128)(2,1)S(1)}, bf16[2,64,128]{2,1,0:T(8,128)(2,1)S(1)}, u32[]{:S(2)}, u32[]{:S(2)}) collective-permute-start(bf16[2,64,128]{2,1,0:T(8,128)(2,1)S(1)} %get-tuple-element.24), channel_id=1, source_target_pairs={{0,8},{8,0},{16,24},{24,16},{1,9},{9,1},{17,25},{25,17},{2,10},{10... | collective-permute-start | bytes 98312 | tf_op jit(solution)/shard_map/ppermute | solution.py:291
  33.5 1.9 %collective-permute-done.11.got_ref = bf16[2,64,128]{2,1,0:T(8,128)(2,1)S(1)} collective-permute-done((bf16[2,64,128]{2,1,0:T(8,128)(2,1)S(1)}, bf16[2,64,128]{2,1,0:T(8,128)(2,1)S(1)}, u32[]{:S(2)}, u32[]{:S(2)}) %collective-permute-start.11) | collective-permute-done | bytes 32800 | tf_op jit(solution)/shard_map/ppermute | solution.py:291
  35.4 0.6 %choose.1 = f32[2,64,128]{2,1,0:T(8,128)} custom-call(f32[2,64,128]{2,1,0:T(8,128)S(1)} %get-tuple-element.23.own_ref, bf16[2,64,128]{2,1,0:T(8,128)(2,1)S(1)} %collective-permute-done.11.got_ref), custom_call_target="tpu_custom_call" | custom-call | tf_op jit(solution)/shard_map/choose/pallas_call | solution.py:22
  (10 shorter events, 0.2 us)
Async XLA Ops:
  1.7 13.2 %copy-start = (bf16[2,384,384]{2,1,0:T(8,128)(2,1)S(1)}, bf16[2,384,384]{2,1,0:T(8,128)(2,1)}, u32[]{:S(2)}) copy-start(bf16[2,384,384]{2,1,0:T(8,128)(2,1)} %band_ref.3) | copy-start | bytes 1769476
  1.7 10.9 %collective-permute-start.2 = (bf16[3,128,384]{2,1,0:T(8,128)(2,1)S(1)}, bf16[3,128,384]{2,1,0:T(8,128)(2,1)S(1)}, u32[]{:S(2)}, u32[]{:S(2)}) collective-permute-start(bf16[3,128,384]{2,1,0:T(8,128)(2,1)S(1)} %multiply_bitcast_fusion.full_ref.own_ref.refs_2_), channel_id=1, source_target_pairs={{0,8},{8,0},{16,24},{24,16},{1,9},{9,1},{17,25},{25,17},{2,10},{10... | collective-permute-start | bytes 884744 | tf_op jit(solution)/shard_map/ppermute | solution.py:259
  4.8 14.8 %collective-permute-start.6 = (bf16[3,128,384]{2,1,0:T(8,128)(2,1)S(1)}, bf16[3,128,384]{2,1,0:T(8,128)(2,1)S(1)}, u32[]{:S(2)}, u32[]{:S(2)}) collective-permute-start(bf16[3,128,384]{2,1,0:T(8,128)(2,1)S(1)} %multiply_bitcast_fusion.full_ref.own_ref.refs_2_), channel_id=1, source_target_pairs={{8,16},{16,8},{0,0},{24,24},{9,17},{17,9},{1,1},{25,25},{10,18},{1... | collective-permute-start | bytes 884744 | tf_op jit(solution)/shard_map/ppermute | solution.py:258
  5.5 14.1 %collective-permute-start.5 = (bf16[3,128,384]{2,1,0:T(8,128)(2,1)S(1)}, bf16[3,128,384]{2,1,0:T(8,128)(2,1)S(1)}, u32[]{:S(2)}, u32[]{:S(2)}) collective-permute-start(bf16[3,128,384]{2,1,0:T(8,128)(2,1)S(1)} %multiply_bitcast_fusion.full_ref.own_ref.refs_2_), channel_id=1, source_target_pairs={{0,16},{24,8},{8,0},{16,24},{1,17},{25,9},{9,1},{17,25},{2,18},{26... | collective-permute-start | bytes 884744 | tf_op jit(solution)/shard_map/ppermute | solution.py:260
  9.4 3.7 %collective-permute-start = (bf16[3,128,128]{2,1,0:T(8,128)(2,1)S(1)}, bf16[3,128,128]{2,1,0:T(8,128)(2,1)S(1)}, u32[]{:S(2)}, u32[]{:S(2)}) collective-permute-start(bf16[3,128,128]{2,1,0:T(8,128)(2,1)S(1)} %edge.4), channel_id=1, source_target_pairs={{0,1},{1,0},{2,3},{3,2},{4,5},{5,4},{6,7},{7,6},{8,9},{9,8},{10,11... | collective-permute-start | bytes 294920 | tf_op jit(solution)/shard_map/ppermute | solution.py:249
  9.5 5.4 %collective-permute-start.1 = (bf16[3,128,128]{2,1,0:T(8,128)(2,1)S(1)}, bf16[3,128,128]{2,1,0:T(8,128)(2,1)S(1)}, u32[]{:S(2)}, u32[]{:S(2)}) collective-permute-start(bf16[3,128,128]{2,1,0:T(8,128)(2,1)S(1)} %edge.5), channel_id=1, source_target_pairs={{0,7},{1,2},{2,1},{3,4},{4,3},{5,6},{6,5},{7,0},{8,15},{9,10},{10,... | collective-permute-start | bytes 294920 | tf_op jit(solution)/shard_map/ppermute | solution.py:249
  12.7 2.2 %copy-start.1 = (bf16[2,3,3]{2,0,1:T(2,128)(2,1)S(1)}, bf16[2,3,3]{2,0,1:T(2,128)(2,1)}, u32[]{:S(2)}) copy-start(bf16[2,3,3]{2,0,1:T(2,128)(2,1)} %param.5) | copy-start | bytes 112
  12.7 5.5 %collective-permute-start.4 = (bf16[3,128,128]{2,1,0:T(8,128)(2,1)S(1)}, bf16[3,128,128]{2,1,0:T(8,128)(2,1)S(1)}, u32[]{:S(2)}, u32[]{:S(2)}) collective-permute-start(bf16[3,128,128]{2,1,0:T(8,128)(2,1)S(1)} %edge.6.refs_0_), channel_id=1, source_target_pairs={{0,7},{1,2},{2,1},{3,4},{4,3},{5,6},{6,5},{7,0},{8,15},{9,10},{10,... | collective-permute-start | bytes 294920 | tf_op jit(solution)/shard_map/ppermute | solution.py:263
  15.8 2.5 %collective-permute-start.3 = (bf16[3,128,128]{2,1,0:T(8,128)(2,1)S(1)}, bf16[3,128,128]{2,1,0:T(8,128)(2,1)S(1)}, u32[]{:S(2)}, u32[]{:S(2)}) collective-permute-start(bf16[3,128,128]{2,1,0:T(8,128)(2,1)S(1)} %edge.7), channel_id=1, source_target_pairs={{0,1},{1,0},{2,3},{3,2},{4,5},{5,4},{6,7},{7,6},{8,9},{9,8},{10,11... | collective-permute-start | bytes 294920 | tf_op jit(solution)/shard_map/ppermute | solution.py:264
  20.2 1.6 %collective-permute-start.7 = (bf16[4,64,512]{2,1,0:T(8,128)(2,1)S(1)}, bf16[4,64,512]{2,1,0:T(8,128)(2,1)S(1)}, u32[]{:S(2)}, u32[]{:S(2)}) collective-permute-start(bf16[4,64,512]{2,1,0:T(8,128)(2,1)S(1)} %get-tuple-element.18), channel_id=1, source_target_pairs={{0,1},{1,0},{2,3},{3,2},{4,5},{5,4},{6,7},{7,6},{8,9},{9,8},{10,11... | collective-permute-start | bytes 786440 | tf_op jit(solution)/shard_map/ppermute | solution.py:284
  21.8 4.3 %collective-permute-start.8 = (bf16[64,512]{1,0:T(8,128)(2,1)S(1)}, bf16[64,512]{1,0:T(8,128)(2,1)S(1)}, u32[]{:S(2)}, u32[]{:S(2)}) collective-permute-start(bf16[64,512]{1,0:T(8,128)(2,1)S(1)} %get-tuple-element.20), channel_id=1, source_target_pairs={{0,2},{1,3},{2,0},{3,1},{4,6},{5,7},{6,4},{7,5},{8,10},{9,11},{10,... | collective-permute-start | bytes 196616 | tf_op jit(solution)/shard_map/ppermute | solution.py:286
  22.5 4.3 %collective-permute-start.9 = (bf16[64,512]{1,0:T(8,128)(2,1)S(1)}, bf16[64,512]{1,0:T(8,128)(2,1)S(1)}, u32[]{:S(2)}, u32[]{:S(2)}) collective-permute-start(bf16[64,512]{1,0:T(8,128)(2,1)S(1)} %get-tuple-element.21), channel_id=1, source_target_pairs={{0,4},{1,5},{2,6},{3,7},{4,0},{5,1},{6,2},{7,3},{8,12},{9,13},{10,... | collective-permute-start | bytes 196616 | tf_op jit(solution)/shard_map/ppermute | solution.py:286
  24.1 5.2 %collective-permute-start.10 = (bf16[64,512]{1,0:T(8,128)(2,1)S(1)}, bf16[64,512]{1,0:T(8,128)(2,1)S(1)}, u32[]{:S(2)}, u32[]{:S(2)}) collective-permute-start(bf16[64,512]{1,0:T(8,128)(2,1)S(1)} %get-tuple-element.22), channel_id=1, source_target_pairs={{0,6},{1,7},{2,4},{3,5},{4,2},{5,3},{6,0},{7,1},{8,14},{9,15},{10,... | collective-permute-start | bytes 196616 | tf_op jit(solution)/shard_map/ppermute | solution.py:286
  29.3 6.0 %collective-permute-start.11 = (bf16[2,64,128]{2,1,0:T(8,128)(2,1)S(1)}, bf16[2,64,128]{2,1,0:T(8,128)(2,1)S(1)}, u32[]{:S(2)}, u32[]{:S(2)}) collective-permute-start(bf16[2,64,128]{2,1,0:T(8,128)(2,1)S(1)} %get-tuple-element.24), channel_id=1, source_target_pairs={{0,8},{8,0},{16,24},{24,16},{1,9},{9,1},{17,25},{25,17},{2,10},{10... | collective-permute-start | bytes 98312 | tf_op jit(solution)/shard_map/ppermute | solution.py:291

commit v5 on v4

--- a/solution.py
+++ b/solution.py
@@ -172,11 +172,15 @@
     )
 
 
+def farthest_first(chips):
+    return range(chips - 1, 0, -1)
+
+
 def pair_kernel(keep_ref, got_ref, own_ref, *outs):
     chip = lax.axis_index("ao") // 2
     own_ref[...] = keep_ref[chip] + got_ref[chip].astype(jnp.float32)
-    for k, out in enumerate(outs):
-        other = chip ^ (k + 1)
+    for k, out in zip(farthest_first(keep_ref.shape[0]), outs):
+        other = chip ^ k
         out[...] = (keep_ref[other] + got_ref[other].astype(jnp.float32)).astype(jnp.bfloat16)
 
 
@@ -283,8 +287,8 @@
     keep, send = sums
     mine, *others = pair(keep, lax.ppermute(send, "ao", mates))
     others = [
-        lax.ppermute(other, "ao", [(i, i ^ (2 * k + 2)) for i in range(blocks)])
-        for k, other in enumerate(others)
+        lax.ppermute(other, "ao", [(i, i ^ (2 * k)) for i in range(blocks)])
+        for k, other in zip(farthest_first(chips), others)
     ]
     outs = total(factor, times, len(dressed), mine, others)
     if planes == 4:

time: 36.2 us -> 35.2 us (0.972)
  waiting for transfers between devices: 11.7 us -> 11 us
    ppermute x3, waiting for transfers between devices: 3.88 us -> 3.1 us  [body(): lax.ppermute(other, 'ao', [(i, i ^ 2 * k) for i in range(blocks)])]
where the time goes in v5:
time: 35.2 us; the launch traced here: 35.1 us
  starting transfers between devices  18.7 us (53%)
  waiting for transfers between devices  11 us (31%)
  Pallas kernels  3.54 us (10%)
  other arithmetic  1.65 us (5%)
    ppermute x1, starting transfers between devices, body(): out = choose(outs[0], lax.ppermute(outs[1], 'aux', swap))  3.98 us
    ppermute x1, starting transfers between devices, body(): second = lax.ppermute(own, 'aux', [(0, 2), (3, 1), (1, 0), (2, 3)])  3.88 us
    ppermute x3, starting transfers between devices, body(): lax.ppermute(other, 'ao', [(i, i ^ 2 * k) for i in range(blocks)])  3.55 us
    pallas_call x7, Pallas kernels, call(): pl.pallas_call(body, out_shape=outs, in_specs=specs, out_specs=VMEM if si...  3.42 us
    ppermute x3, waiting for transfers between devices, body(): lax.ppermute(other, 'ao', [(i, i ^ 2 * k) for i in range(blocks)])  3.1 us
    ppermute x1, starting transfers between devices, body(): beside = lax.ppermute(own, 'aux', swap)  3.09 us
    ppermute x2, starting transfers between devices, halo(): return (lax.ppermute(inner, 'ao', mates), lax.ppermute(outer, 'ao', nexts))  2.68 us
    ppermute x1, waiting for transfers between devices, body(): outer = lax.ppermute(facing, 'ao', nexts)  2.14 us
  transfers between devices with their start and end apart: 12, of which 8 were waited for; matrix products, arithmetic and copies ran while one was open for 0% of the time, Pallas kernels for 6%

profile of v5, /device:TPU:0, one launch (start us, length us, event | category | flops | bytes accessed | tf_op | source)
XLA Modules:
  0.0 35.1 jit_solution(15834098554704476529)
XLA Ops:
  0.0 0.7 %convert_bitcast_fusion = bf16[3]{0:T(256)(128)(2,1)S(1)} fusion(s32[1,3]{1,0:T(1,128)} %param.7), kind=kLoop, calls=%fused_computation.1 | loop fusion | flops 3 | bytes 18 | tf_op jit(solution)/shard_map/mul | solution.py:258
  0.7 0.1 broadcast_bitcast_fusion
  0.7 1.0 %multiply_bitcast_fusion.full_ref.own_ref.refs_2_ = bf16[3,128,384]{2,1,0:T(8,128)(2,1)S(1)} fusion(bf16[128,3,384]{2,0,1:T(8,128)(2,1)} %param.4, bf16[384]{0:T(512)(128)(2,1)S(1)} %broadcast_bitcast_fusion), kind=kLoop, calls=%fused_computation | loop fusion | flops 147456 | bytes 590592 | tf_op jit(solution)/shard_map/mul | solution.py:258
  1.7 0.0 copy-start
  1.7 3.1 %collective-permute-start.2 = (bf16[3,128,384]{2,1,0:T(8,128)(2,1)S(1)}, bf16[3,128,384]{2,1,0:T(8,128)(2,1)S(1)}, u32[]{:S(2)}, u32[]{:S(2)}) collective-permute-start(bf16[3,128,384]{2,1,0:T(8,128)(2,1)S(1)} %multiply_bitcast_fusion.full_ref.own_ref.refs_2_), channel_id=1, source_target_pairs={{0,8},{8,0},{16,24},{24,16},{1,9},{9,1},{17,25},{25,17},{2,10},{10... | collective-permute-start | bytes 884744 | tf_op jit(solution)/shard_map/ppermute | solution.py:263
  4.8 0.7 %collective-permute-start.6 = (bf16[3,128,384]{2,1,0:T(8,128)(2,1)S(1)}, bf16[3,128,384]{2,1,0:T(8,128)(2,1)S(1)}, u32[]{:S(2)}, u32[]{:S(2)}) collective-permute-start(bf16[3,128,384]{2,1,0:T(8,128)(2,1)S(1)} %multiply_bitcast_fusion.full_ref.own_ref.refs_2_), channel_id=1, source_target_pairs={{8,16},{16,8},{0,0},{24,24},{9,17},{17,9},{1,1},{25,25},{10,18},{1... | collective-permute-start | bytes 884744 | tf_op jit(solution)/shard_map/ppermute | solution.py:262
  5.5 3.9 %collective-permute-start.5 = (bf16[3,128,384]{2,1,0:T(8,128)(2,1)S(1)}, bf16[3,128,384]{2,1,0:T(8,128)(2,1)S(1)}, u32[]{:S(2)}, u32[]{:S(2)}) collective-permute-start(bf16[3,128,384]{2,1,0:T(8,128)(2,1)S(1)} %multiply_bitcast_fusion.full_ref.own_ref.refs_2_), channel_id=1, source_target_pairs={{0,16},{24,8},{8,0},{16,24},{1,17},{25,9},{9,1},{17,25},{2,18},{26... | collective-permute-start | bytes 884744 | tf_op jit(solution)/shard_map/ppermute | solution.py:264
  9.4 0.1 collective-permute-start
  9.5 2.6 %collective-permute-start.1 = (bf16[3,128,128]{2,1,0:T(8,128)(2,1)S(1)}, bf16[3,128,128]{2,1,0:T(8,128)(2,1)S(1)}, u32[]{:S(2)}, u32[]{:S(2)}) collective-permute-start(bf16[3,128,128]{2,1,0:T(8,128)(2,1)S(1)} %edge.5), channel_id=1, source_target_pairs={{0,7},{1,2},{2,1},{3,4},{4,3},{5,6},{6,5},{7,0},{8,15},{9,10},{10,... | collective-permute-start | bytes 294920 | tf_op jit(solution)/shard_map/ppermute | solution.py:253
  12.1 0.5 %collective-permute-done.2.full_ref.own_ref.refs_3_ = bf16[3,128,384]{2,1,0:T(8,128)(2,1)S(1)} collective-permute-done((bf16[3,128,384]{2,1,0:T(8,128)(2,1)S(1)}, bf16[3,128,384]{2,1,0:T(8,128)(2,1)S(1)}, u32[]{:S(2)}, u32[]{:S(2)}) %collective-permute-start.2) | collective-permute-done | bytes 294944 | tf_op jit(solution)/shard_map/ppermute | solution.py:263
  12.7 0.0 copy-start.1
  12.7 0.4 %collective-permute-start.4 = (bf16[3,128,128]{2,1,0:T(8,128)(2,1)S(1)}, bf16[3,128,128]{2,1,0:T(8,128)(2,1)S(1)}, u32[]{:S(2)}, u32[]{:S(2)}) collective-permute-start(bf16[3,128,128]{2,1,0:T(8,128)(2,1)S(1)} %edge.6.refs_0_), channel_id=1, source_target_pairs={{0,7},{1,2},{2,1},{3,4},{4,3},{5,6},{6,5},{7,0},{8,15},{9,10},{10,... | collective-permute-start | bytes 294920 | tf_op jit(solution)/shard_map/ppermute | solution.py:267
  13.1 0.0 collective-permute-done.inner_ref
  13.1 1.8 %collective-permute-done.1.outer_ref = bf16[3,128,128]{2,1,0:T(8,128)(2,1)S(1)} collective-permute-done((bf16[3,128,128]{2,1,0:T(8,128)(2,1)S(1)}, bf16[3,128,128]{2,1,0:T(8,128)(2,1)S(1)}, u32[]{:S(2)}, u32[]{:S(2)}) %collective-permute-start.1) | collective-permute-done | bytes 98336 | tf_op jit(solution)/shard_map/ppermute | solution.py:253
  14.9 0.8 %dress.2.refs_0_ = bf16[256,1152]{1,0:T(8,128)(2,1)S(1)} custom-call(bf16[3,2,3]{2,1,0:T(2,128)(2,1)S(1)} %bitcast.8, bf16[3,128,384]{2,1,0:T(8,128)(2,1)S(1)} %multiply_bitcast_fusion.full_ref.own_ref.refs_2_, bf16[3,128,128]{2,1,0:T(8,128)(2,1)S(1)} %collective-permute-done.inner_ref, bf16[3,128,128]{2,1,0:T(8,128)(2,1)S(1)} %collective-permute-done.1.outer_ref, ...), custom_call_target="tpu_custom_call" | custom-call | tf_op jit(solution)/shard_map/dress/pallas_call | solution.py:22
  15.8 0.4 %collective-permute-start.3 = (bf16[3,128,128]{2,1,0:T(8,128)(2,1)S(1)}, bf16[3,128,128]{2,1,0:T(8,128)(2,1)S(1)}, u32[]{:S(2)}, u32[]{:S(2)}) collective-permute-start(bf16[3,128,128]{2,1,0:T(8,128)(2,1)S(1)} %edge.7), channel_id=1, source_target_pairs={{0,1},{1,0},{2,3},{3,2},{4,5},{5,4},{6,7},{7,6},{8,9},{9,8},{10,11... | collective-permute-start | bytes 294920 | tf_op jit(solution)/shard_map/ppermute | solution.py:268
  16.1 2.1 %collective-permute-done.4.outer_ref = bf16[3,128,128]{2,1,0:T(8,128)(2,1)S(1)} collective-permute-done((bf16[3,128,128]{2,1,0:T(8,128)(2,1)S(1)}, bf16[3,128,128]{2,1,0:T(8,128)(2,1)S(1)}, u32[]{:S(2)}, u32[]{:S(2)}) %collective-permute-start.4) | collective-permute-done | bytes 98336 | tf_op jit(solution)/shard_map/ppermute | solution.py:267
  18.2 0.8 %dress.3.refs_1_ = bf16[256,1152]{1,0:T(8,128)(2,1)S(1)} custom-call(bf16[3,2,3]{2,1,0:T(2,128)(2,1)S(1)} %bitcast.9, bf16[3,128,384]{2,1,0:T(8,128)(2,1)S(1)} %collective-permute-done.2.full_ref.own_ref.refs_3_, bf16[3,128,128]{2,1,0:T(8,128)(2,1)S(1)} %collective-permute-done.3.inner_ref, bf16[3,128,128]{2,1,0:T(8,128)(2,1)S(1)} %collective-permute-done.4.outer_ref, ...), custom_call_target="tpu_custom_call" | custom-call | tf_op jit(solution)/shard_map/dress/pallas_call | solution.py:22
  19.1 0.6 %share.2 = (f32[4,64,512]{2,1,0:T(8,128)S(1)}, bf16[4,64,512]{2,1,0:T(8,128)(2,1)S(1)}) custom-call(bf16[256,1152]{1,0:T(8,128)(2,1)S(1)} %dress.2.refs_0_, bf16[256,1152]{1,0:T(8,128)(2,1)S(1)} %dress.3.refs_1_, bf16[3,128,384]{2,1,0:T(8,128)(2,1)S(1)} %multiply_bitcast_fusion.full_ref.own_ref.refs_2_, ...), custom_call_target="tpu_custom_call" | custom-call | tf_op jit(solution)/shard_map/share/pallas_call | solution.py:22
  19.6 0.0 collective-permute-done.6.refs_3_
  19.6 0.6 %share.3 = (f32[4,64,512]{2,1,0:T(8,128)S(1)}, bf16[4,64,512]{2,1,0:T(8,128)(2,1)S(1)}) custom-call(bf16[256,1152]{1,0:T(8,128)(2,1)S(1)} %dress.2.refs_0_, bf16[256,1152]{1,0:T(8,128)(2,1)S(1)} %dress.3.refs_1_, bf16[3,128,384]{2,1,0:T(8,128)(2,1)S(1)} %collective-permute-done.5.refs_2_, bf16[3,128,384]{2,1,0:T(8,128)(2,1)S(1)} %collective-permute-done.6.refs_3_, ...), custom_call_target="tpu_custom_call" | custom-call | tf_op jit(solution)/shard_map/share/pallas_call | solution.py:22
  20.2 0.1 collective-permute-start.7
  20.3 1.5 %collective-permute-done.7.got_ref = bf16[4,64,512]{2,1,0:T(8,128)(2,1)S(1)} collective-permute-done((bf16[4,64,512]{2,1,0:T(8,128)(2,1)S(1)}, bf16[4,64,512]{2,1,0:T(8,128)(2,1)S(1)}, u32[]{:S(2)}, u32[]{:S(2)}) %collective-permute-start.7) | collective-permute-done | bytes 262176 | tf_op jit(solution)/shard_map/ppermute | solution.py:288
  21.8 1.7 %collective-permute-start.8 = (bf16[64,512]{1,0:T(8,128)(2,1)S(1)}, bf16[64,512]{1,0:T(8,128)(2,1)S(1)}, u32[]{:S(2)}, u32[]{:S(2)}) collective-permute-start(bf16[64,512]{1,0:T(8,128)(2,1)S(1)} %get-tuple-element.20), channel_id=1, source_target_pairs={{0,6},{1,7},{2,4},{3,5},{4,2},{5,3},{6,0},{7,1},{8,14},{9,15},{10,... | collective-permute-start | bytes 196616 | tf_op jit(solution)/shard_map/ppermute | solution.py:290
  23.6 0.4 %collective-permute-start.9 = (bf16[64,512]{1,0:T(8,128)(2,1)S(1)}, bf16[64,512]{1,0:T(8,128)(2,1)S(1)}, u32[]{:S(2)}, u32[]{:S(2)}) collective-permute-start(bf16[64,512]{1,0:T(8,128)(2,1)S(1)} %get-tuple-element.21), channel_id=1, source_target_pairs={{0,4},{1,5},{2,6},{3,7},{4,0},{5,1},{6,2},{7,3},{8,12},{9,13},{10,... | collective-permute-start | bytes 196616 | tf_op jit(solution)/shard_map/ppermute | solution.py:290
  24.0 1.4 %collective-permute-start.10 = (bf16[64,512]{1,0:T(8,128)(2,1)S(1)}, bf16[64,512]{1,0:T(8,128)(2,1)S(1)}, u32[]{:S(2)}, u32[]{:S(2)}) collective-permute-start(bf16[64,512]{1,0:T(8,128)(2,1)S(1)} %get-tuple-element.22), channel_id=1, source_target_pairs={{0,2},{1,3},{2,0},{3,1},{4,6},{5,7},{6,4},{7,5},{8,10},{9,11},{10,... | collective-permute-start | bytes 196616 | tf_op jit(solution)/shard_map/ppermute | solution.py:290
  25.4 1.7 %collective-permute-done.8.refs_0_ = bf16[64,512]{1,0:T(8,128)(2,1)S(1)} collective-permute-done((bf16[64,512]{1,0:T(8,128)(2,1)S(1)}, bf16[64,512]{1,0:T(8,128)(2,1)S(1)}, u32[]{:S(2)}, u32[]{:S(2)}) %collective-permute-start.8) | collective-permute-done | bytes 65568 | tf_op jit(solution)/shard_map/ppermute | solution.py:290
  27.1 1.2 %collective-permute-done.9.refs_1_ = bf16[64,512]{1,0:T(8,128)(2,1)S(1)} collective-permute-done((bf16[64,512]{1,0:T(8,128)(2,1)S(1)}, bf16[64,512]{1,0:T(8,128)(2,1)S(1)}, u32[]{:S(2)}, u32[]{:S(2)}) %collective-permute-start.9) | collective-permute-done | bytes 65568 | tf_op jit(solution)/shard_map/ppermute | solution.py:290
  28.3 0.1 collective-permute-done.10.refs_2_
  28.5 4.0 %collective-permute-start.11 = (bf16[2,64,128]{2,1,0:T(8,128)(2,1)S(1)}, bf16[2,64,128]{2,1,0:T(8,128)(2,1)S(1)}, u32[]{:S(2)}, u32[]{:S(2)}) collective-permute-start(bf16[2,64,128]{2,1,0:T(8,128)(2,1)S(1)} %get-tuple-element.24), channel_id=1, source_target_pairs={{0,8},{8,0},{16,24},{24,16},{1,9},{9,1},{17,25},{25,17},{2,10},{10... | collective-permute-start | bytes 98312 | tf_op jit(solution)/shard_map/ppermute | solution.py:295
  32.5 1.9 %collective-permute-done.11.got_ref = bf16[2,64,128]{2,1,0:T(8,128)(2,1)S(1)} collective-permute-done((bf16[2,64,128]{2,1,0:T(8,128)(2,1)S(1)}, bf16[2,64,128]{2,1,0:T(8,128)(2,1)S(1)}, u32[]{:S(2)}, u32[]{:S(2)}) %collective-permute-start.11) | collective-permute-done | bytes 32800 | tf_op jit(solution)/shard_map/ppermute | solution.py:295
  34.4 0.6 %choose.1 = f32[2,64,128]{2,1,0:T(8,128)} custom-call(f32[2,64,128]{2,1,0:T(8,128)S(1)} %get-tuple-element.23.own_ref, bf16[2,64,128]{2,1,0:T(8,128)(2,1)S(1)} %collective-permute-done.11.got_ref), custom_call_target="tpu_custom_call" | custom-call | tf_op jit(solution)/shard_map/choose/pallas_call | solution.py:22
  (10 shorter events, 0.2 us)
Async XLA Ops:
  1.7 13.2 %copy-start = (bf16[2,384,384]{2,1,0:T(8,128)(2,1)S(1)}, bf16[2,384,384]{2,1,0:T(8,128)(2,1)}, u32[]{:S(2)}) copy-start(bf16[2,384,384]{2,1,0:T(8,128)(2,1)} %band_ref.3) | copy-start | bytes 1769476
  1.7 10.9 %collective-permute-start.2 = (bf16[3,128,384]{2,1,0:T(8,128)(2,1)S(1)}, bf16[3,128,384]{2,1,0:T(8,128)(2,1)S(1)}, u32[]{:S(2)}, u32[]{:S(2)}) collective-permute-start(bf16[3,128,384]{2,1,0:T(8,128)(2,1)S(1)} %multiply_bitcast_fusion.full_ref.own_ref.refs_2_), channel_id=1, source_target_pairs={{0,8},{8,0},{16,24},{24,16},{1,9},{9,1},{17,25},{25,17},{2,10},{10... | collective-permute-start | bytes 884744 | tf_op jit(solution)/shard_map/ppermute | solution.py:263
  4.8 14.8 %collective-permute-start.6 = (bf16[3,128,384]{2,1,0:T(8,128)(2,1)S(1)}, bf16[3,128,384]{2,1,0:T(8,128)(2,1)S(1)}, u32[]{:S(2)}, u32[]{:S(2)}) collective-permute-start(bf16[3,128,384]{2,1,0:T(8,128)(2,1)S(1)} %multiply_bitcast_fusion.full_ref.own_ref.refs_2_), channel_id=1, source_target_pairs={{8,16},{16,8},{0,0},{24,24},{9,17},{17,9},{1,1},{25,25},{10,18},{1... | collective-permute-start | bytes 884744 | tf_op jit(solution)/shard_map/ppermute | solution.py:262
  5.5 14.1 %collective-permute-start.5 = (bf16[3,128,384]{2,1,0:T(8,128)(2,1)S(1)}, bf16[3,128,384]{2,1,0:T(8,128)(2,1)S(1)}, u32[]{:S(2)}, u32[]{:S(2)}) collective-permute-start(bf16[3,128,384]{2,1,0:T(8,128)(2,1)S(1)} %multiply_bitcast_fusion.full_ref.own_ref.refs_2_), channel_id=1, source_target_pairs={{0,16},{24,8},{8,0},{16,24},{1,17},{25,9},{9,1},{17,25},{2,18},{26... | collective-permute-start | bytes 884744 | tf_op jit(solution)/shard_map/ppermute | solution.py:264
  9.4 3.7 %collective-permute-start = (bf16[3,128,128]{2,1,0:T(8,128)(2,1)S(1)}, bf16[3,128,128]{2,1,0:T(8,128)(2,1)S(1)}, u32[]{:S(2)}, u32[]{:S(2)}) collective-permute-start(bf16[3,128,128]{2,1,0:T(8,128)(2,1)S(1)} %edge.4), channel_id=1, source_target_pairs={{0,1},{1,0},{2,3},{3,2},{4,5},{5,4},{6,7},{7,6},{8,9},{9,8},{10,11... | collective-permute-start | bytes 294920 | tf_op jit(solution)/shard_map/ppermute | solution.py:253
  9.5 5.4 %collective-permute-start.1 = (bf16[3,128,128]{2,1,0:T(8,128)(2,1)S(1)}, bf16[3,128,128]{2,1,0:T(8,128)(2,1)S(1)}, u32[]{:S(2)}, u32[]{:S(2)}) collective-permute-start(bf16[3,128,128]{2,1,0:T(8,128)(2,1)S(1)} %edge.5), channel_id=1, source_target_pairs={{0,7},{1,2},{2,1},{3,4},{4,3},{5,6},{6,5},{7,0},{8,15},{9,10},{10,... | collective-permute-start | bytes 294920 | tf_op jit(solution)/shard_map/ppermute | solution.py:253
  12.7 2.2 %copy-start.1 = (bf16[2,3,3]{2,0,1:T(2,128)(2,1)S(1)}, bf16[2,3,3]{2,0,1:T(2,128)(2,1)}, u32[]{:S(2)}) copy-start(bf16[2,3,3]{2,0,1:T(2,128)(2,1)} %param.5) | copy-start | bytes 112
  12.7 5.5 %collective-permute-start.4 = (bf16[3,128,128]{2,1,0:T(8,128)(2,1)S(1)}, bf16[3,128,128]{2,1,0:T(8,128)(2,1)S(1)}, u32[]{:S(2)}, u32[]{:S(2)}) collective-permute-start(bf16[3,128,128]{2,1,0:T(8,128)(2,1)S(1)} %edge.6.refs_0_), channel_id=1, source_target_pairs={{0,7},{1,2},{2,1},{3,4},{4,3},{5,6},{6,5},{7,0},{8,15},{9,10},{10,... | collective-permute-start | bytes 294920 | tf_op jit(solution)/shard_map/ppermute | solution.py:267
  15.8 2.5 %collective-permute-start.3 = (bf16[3,128,128]{2,1,0:T(8,128)(2,1)S(1)}, bf16[3,128,128]{2,1,0:T(8,128)(2,1)S(1)}, u32[]{:S(2)}, u32[]{:S(2)}) collective-permute-start(bf16[3,128,128]{2,1,0:T(8,128)(2,1)S(1)} %edge.7), channel_id=1, source_target_pairs={{0,1},{1,0},{2,3},{3,2},{4,5},{5,4},{6,7},{7,6},{8,9},{9,8},{10,11... | collective-permute-start | bytes 294920 | tf_op jit(solution)/shard_map/ppermute | solution.py:268
  20.2 1.6 %collective-permute-start.7 = (bf16[4,64,512]{2,1,0:T(8,128)(2,1)S(1)}, bf16[4,64,512]{2,1,0:T(8,128)(2,1)S(1)}, u32[]{:S(2)}, u32[]{:S(2)}) collective-permute-start(bf16[4,64,512]{2,1,0:T(8,128)(2,1)S(1)} %get-tuple-element.18), channel_id=1, source_target_pairs={{0,1},{1,0},{2,3},{3,2},{4,5},{5,4},{6,7},{7,6},{8,9},{9,8},{10,11... | collective-permute-start | bytes 786440 | tf_op jit(solution)/shard_map/ppermute | solution.py:288
  21.8 5.3 %collective-permute-start.8 = (bf16[64,512]{1,0:T(8,128)(2,1)S(1)}, bf16[64,512]{1,0:T(8,128)(2,1)S(1)}, u32[]{:S(2)}, u32[]{:S(2)}) collective-permute-start(bf16[64,512]{1,0:T(8,128)(2,1)S(1)} %get-tuple-element.20), channel_id=1, source_target_pairs={{0,6},{1,7},{2,4},{3,5},{4,2},{5,3},{6,0},{7,1},{8,14},{9,15},{10,... | collective-permute-start | bytes 196616 | tf_op jit(solution)/shard_map/ppermute | solution.py:290
  23.6 4.8 %collective-permute-start.9 = (bf16[64,512]{1,0:T(8,128)(2,1)S(1)}, bf16[64,512]{1,0:T(8,128)(2,1)S(1)}, u32[]{:S(2)}, u32[]{:S(2)}) collective-permute-start(bf16[64,512]{1,0:T(8,128)(2,1)S(1)} %get-tuple-element.21), channel_id=1, source_target_pairs={{0,4},{1,5},{2,6},{3,7},{4,0},{5,1},{6,2},{7,3},{8,12},{9,13},{10,... | collective-permute-start | bytes 196616 | tf_op jit(solution)/shard_map/ppermute | solution.py:290
  24.0 4.5 %collective-permute-start.10 = (bf16[64,512]{1,0:T(8,128)(2,1)S(1)}, bf16[64,512]{1,0:T(8,128)(2,1)S(1)}, u32[]{:S(2)}, u32[]{:S(2)}) collective-permute-start(bf16[64,512]{1,0:T(8,128)(2,1)S(1)} %get-tuple-element.22), channel_id=1, source_target_pairs={{0,2},{1,3},{2,0},{3,1},{4,6},{5,7},{6,4},{7,5},{8,10},{9,11},{10,... | collective-permute-start | bytes 196616 | tf_op jit(solution)/shard_map/ppermute | solution.py:290
  28.5 5.9 %collective-permute-start.11 = (bf16[2,64,128]{2,1,0:T(8,128)(2,1)S(1)}, bf16[2,64,128]{2,1,0:T(8,128)(2,1)S(1)}, u32[]{:S(2)}, u32[]{:S(2)}) collective-permute-start(bf16[2,64,128]{2,1,0:T(8,128)(2,1)S(1)} %get-tuple-element.24), channel_id=1, source_target_pairs={{0,8},{8,0},{16,24},{24,16},{1,9},{9,1},{17,25},{25,17},{2,10},{10... | collective-permute-start | bytes 98312 | tf_op jit(solution)/shard_map/ppermute | solution.py:295

commit v6 on v5

--- a/solution.py
+++ b/solution.py
@@ -176,59 +176,57 @@
     return range(chips - 1, 0, -1)
 
 
-def pair_kernel(keep_ref, got_ref, own_ref, *outs):
+def pair_kernel(parts, keep_ref, got_ref, *outs):
+    chips, _, both = keep_ref.shape
     chip = lax.axis_index("ao") // 2
-    own_ref[...] = keep_ref[chip] + got_ref[chip].astype(jnp.float32)
-    for k, out in zip(farthest_first(keep_ref.shape[0]), outs):
-        other = chip ^ k
-        out[...] = (keep_ref[other] + got_ref[other].astype(jnp.float32)).astype(jnp.bfloat16)
-
-
-def pair(keep, got):
-    chips = keep.shape[0]
-    dims = keep.shape[1:]
-    return call(
+    size = both // parts
+    for n in range(parts):
+        here = pl.ds(n * size, size)
+        for k, out in zip((0, *farthest_first(chips)), outs[n * chips : (n + 1) * chips]):
+            other = chip ^ k
+            value = keep_ref[other, :, here] + got_ref[other, :, here].astype(jnp.float32)
+            out[...] = value.astype(out.dtype)
+
+
+def pair(parts, keep, got):
+    chips, width, both = keep.shape
+    dims = (width, both // parts)
+    kinds = ([jnp.float32] + [jnp.bfloat16] * (chips - 1)) * parts
+    outs = call(
         "pair",
-        pair_kernel,
+        functools.partial(pair_kernel, parts),
         [VMEM] * 2,
-        [shape(dims, jnp.float32)] + [shape(dims, jnp.bfloat16)] * (chips - 1),
+        [shape(dims, kind) for kind in kinds],
         (keep, got),
     )
-
-
-def total_kernel(factor, count, own_ref, *refs):
-    others, outs = refs[:-count], refs[-count:]
-    total = own_ref[...]
-    for other in others:
-        total += other[...].astype(jnp.float32)
-    total *= factor
-    times, _, rows = outs[0].shape
-    for n, out in enumerate(outs):
-        for t in range(times):
-            at = (n * times + t) * rows
-            out[t] = total[:, at : at + rows].astype(out.dtype)
-
-
-def total(factor, times, count, own, others):
-    width, both = own.shape
-    dims = (times, width, both // (times * count))
+    return [outs[n * chips : (n + 1) * chips] for n in range(parts)]
+
+
+def total_kernel(factor, count, *refs):
+    terms, back, out_ref = refs[:count], refs[count:-1], refs[-1]
+    value = terms[0][...]
+    for term in terms[1:]:
+        value += term[...].astype(jnp.float32)
+    value *= factor
+    place = lax.axis_index("aux")
+    inner = (place > 0) & (place < lax.axis_size("aux") - 1)
+    times, _, rows = out_ref.shape
+    for t in range(times):
+        part = value[:, t * rows : (t + 1) * rows]
+        for ref in back:
+            part = jnp.where(inner, part, ref[t].astype(jnp.float32))
+        out_ref[t] = part.astype(out_ref.dtype)
+
+
+def total(factor, times, kind, terms, back=()):
+    width, both = terms[0].shape
     return call(
         "total",
-        functools.partial(total_kernel, factor, count),
-        [VMEM] * (1 + len(others)),
-        [shape(dims, jnp.float32)] + [shape(dims, jnp.bfloat16)] * (count - 1),
-        (own, *others),
+        functools.partial(total_kernel, factor, len(terms)),
+        [VMEM] * (len(terms) + len(back)),
+        shape((times, width, both // times), kind),
+        (*terms, *back),
     )
-
-
-def choose_kernel(own_ref, got_ref, out_ref):
-    place = lax.axis_index("aux")
-    inner = (place == 1) | (place == 2)
-    out_ref[...] = jnp.where(inner, own_ref[...], got_ref[...].astype(jnp.float32))
-
-
-def choose(own, got):
-    return call("choose", choose_kernel, [VMEM] * 2, shape(own.shape, own.dtype), (own, got))
 
 
 def shifted(x, axis, by):
@@ -285,16 +283,19 @@
             sources, held = zip(*group.values())
             sums = share(sources, chips, width, dressed, held, sums)
     keep, send = sums
-    mine, *others = pair(keep, lax.ppermute(send, "ao", mates))
-    others = [
-        lax.ppermute(other, "ao", [(i, i ^ (2 * k)) for i in range(blocks)])
-        for k, other in zip(farthest_first(chips), others)
+    def exchanged(terms):
+        others = [
+            lax.ppermute(other, "ao", [(i, i ^ (2 * k)) for i in range(blocks)])
+            for k, other in zip(farthest_first(chips), terms[1:])
+        ]
+        return [terms[0], *others]
+
+    groups = pair(len(dressed), keep, lax.ppermute(send, "ao", mates))
+    back = [
+        lax.ppermute(total(factor, times, jnp.bfloat16, exchanged(terms)), "aux", swap)
+        for terms in groups[1:]
     ]
-    outs = total(factor, times, len(dressed), mine, others)
-    if planes == 4:
-        out = choose(outs[0], lax.ppermute(outs[1], "aux", swap))
-    else:
-        out = outs[0]
+    out = total(factor, times, jnp.float32, exchanged(groups[0]), back)
     return out.transpose(0, 2, 1)
 
 

time: 35.2 us -> 35 us (level)
  waiting for transfers between devices: 11 us -> 7.86 us
  starting transfers between devices: 18.7 us -> 21.6 us
    ppermute x5 -> x8, waiting for transfers between devices: 6.51 us -> 3.42 us  [the longest x1 1.88 us: body(): lax.ppermute(total(factor, times, jnp.bfloat16, exchanged(terms)), 'aux',...]
    ppermute x5 -> x8, starting transfers between devices: 7.61 us -> 10.5 us  [the longest x6 7.04 us: exchanged(): lax.ppermute(other, 'ao', [(i, i ^ 2 * k) for i in range(blocks)])]
  transfers between devices with their start and end apart: 12 -> 15, of which waited for: 8 -> 5; matrix products, arithmetic and copies ran while one was open for 0% -> 0% of each run, Pallas kernels for 6% -> 7%
where the time goes in v6:
time: 35 us; the launch traced here: 34.9 us
  starting transfers between devices  21.6 us (62%)
  waiting for transfers between devices  7.86 us (22%)
  Pallas kernels  3.54 us (10%)
  other arithmetic  1.65 us (5%)
    ppermute x6, starting transfers between devices, exchanged(): lax.ppermute(other, 'ao', [(i, i ^ 2 * k) for i in range(blocks)])  7.04 us
    ppermute x1, starting transfers between devices, body(): second = lax.ppermute(own, 'aux', [(0, 2), (3, 1), (1, 0), (2, 3)])  3.88 us
    pallas_call x7, Pallas kernels, call(): pl.pallas_call(body, out_shape=outs, in_specs=specs, out_specs=VMEM if si...  3.42 us
    ppermute x1, starting transfers between devices, body(): lax.ppermute(total(factor, times, jnp.bfloat16, exchanged(terms)), 'aux',...  3.4 us
    ppermute x1, starting transfers between devices, body(): beside = lax.ppermute(own, 'aux', swap)  3.09 us
    ppermute x2, starting transfers between devices, halo(): return (lax.ppermute(inner, 'ao', mates), lax.ppermute(outer, 'ao', nexts))  2.68 us
    ppermute x1, waiting for transfers between devices, body(): outer = lax.ppermute(facing, 'ao', nexts)  2.14 us
    ppermute x1, waiting for transfers between devices, body(): lax.ppermute(total(factor, times, jnp.bfloat16, exchanged(terms)), 'aux',...  1.88 us
  transfers between devices with their start and end apart: 15, of which 5 were waited for; matrix products, arithmetic and copies ran while one was open for 0% of the time, Pallas kernels for 7%

profile of v6, /device:TPU:0, one launch (start us, length us, event | category | flops | bytes accessed | tf_op | source)
XLA Modules:
  0.0 34.9 jit_solution(9256478905672576935)
XLA Ops:
  0.0 0.7 %convert_bitcast_fusion = bf16[3]{0:T(256)(128)(2,1)S(1)} fusion(s32[1,3]{1,0:T(1,128)} %param.7), kind=kLoop, calls=%fused_computation.1 | loop fusion | flops 3 | bytes 18 | tf_op jit(solution)/shard_map/mul | solution.py:256
  0.7 0.1 broadcast_bitcast_fusion
  0.7 1.0 %multiply_bitcast_fusion.full_ref.own_ref.refs_2_ = bf16[3,128,384]{2,1,0:T(8,128)(2,1)S(1)} fusion(bf16[128,3,384]{2,0,1:T(8,128)(2,1)} %param.4, bf16[384]{0:T(512)(128)(2,1)S(1)} %broadcast_bitcast_fusion), kind=kLoop, calls=%fused_computation | loop fusion | flops 147456 | bytes 590592 | tf_op jit(solution)/shard_map/mul | solution.py:256
  1.7 0.0 copy-start
  1.7 3.1 %collective-permute-start.2 = (bf16[3,128,384]{2,1,0:T(8,128)(2,1)S(1)}, bf16[3,128,384]{2,1,0:T(8,128)(2,1)S(1)}, u32[]{:S(2)}, u32[]{:S(2)}) collective-permute-start(bf16[3,128,384]{2,1,0:T(8,128)(2,1)S(1)} %multiply_bitcast_fusion.full_ref.own_ref.refs_2_), channel_id=1, source_target_pairs={{0,8},{8,0},{16,24},{24,16},{1,9},{9,1},{17,25},{25,17},{2,10},{10... | collective-permute-start | bytes 884744 | tf_op jit(solution)/shard_map/ppermute | solution.py:261
  4.8 0.7 %collective-permute-start.6 = (bf16[3,128,384]{2,1,0:T(8,128)(2,1)S(1)}, bf16[3,128,384]{2,1,0:T(8,128)(2,1)S(1)}, u32[]{:S(2)}, u32[]{:S(2)}) collective-permute-start(bf16[3,128,384]{2,1,0:T(8,128)(2,1)S(1)} %multiply_bitcast_fusion.full_ref.own_ref.refs_2_), channel_id=1, source_target_pairs={{8,16},{16,8},{0,0},{24,24},{9,17},{17,9},{1,1},{25,25},{10,18},{1... | collective-permute-start | bytes 884744 | tf_op jit(solution)/shard_map/ppermute | solution.py:260
  5.5 3.9 %collective-permute-start.5 = (bf16[3,128,384]{2,1,0:T(8,128)(2,1)S(1)}, bf16[3,128,384]{2,1,0:T(8,128)(2,1)S(1)}, u32[]{:S(2)}, u32[]{:S(2)}) collective-permute-start(bf16[3,128,384]{2,1,0:T(8,128)(2,1)S(1)} %multiply_bitcast_fusion.full_ref.own_ref.refs_2_), channel_id=1, source_target_pairs={{0,16},{24,8},{8,0},{16,24},{1,17},{25,9},{9,1},{17,25},{2,18},{26... | collective-permute-start | bytes 884744 | tf_op jit(solution)/shard_map/ppermute | solution.py:262
  9.4 0.1 collective-permute-start
  9.5 2.6 %collective-permute-start.1 = (bf16[3,128,128]{2,1,0:T(8,128)(2,1)S(1)}, bf16[3,128,128]{2,1,0:T(8,128)(2,1)S(1)}, u32[]{:S(2)}, u32[]{:S(2)}) collective-permute-start(bf16[3,128,128]{2,1,0:T(8,128)(2,1)S(1)} %edge.5), channel_id=1, source_target_pairs={{0,7},{1,2},{2,1},{3,4},{4,3},{5,6},{6,5},{7,0},{8,15},{9,10},{10,... | collective-permute-start | bytes 294920 | tf_op jit(solution)/shard_map/ppermute | solution.py:251
  12.1 0.5 %collective-permute-done.2.full_ref.own_ref.refs_3_ = bf16[3,128,384]{2,1,0:T(8,128)(2,1)S(1)} collective-permute-done((bf16[3,128,384]{2,1,0:T(8,128)(2,1)S(1)}, bf16[3,128,384]{2,1,0:T(8,128)(2,1)S(1)}, u32[]{:S(2)}, u32[]{:S(2)}) %collective-permute-start.2) | collective-permute-done | bytes 294944 | tf_op jit(solution)/shard_map/ppermute | solution.py:261
  12.7 0.0 copy-start.1
  12.7 0.4 %collective-permute-start.4 = (bf16[3,128,128]{2,1,0:T(8,128)(2,1)S(1)}, bf16[3,128,128]{2,1,0:T(8,128)(2,1)S(1)}, u32[]{:S(2)}, u32[]{:S(2)}) collective-permute-start(bf16[3,128,128]{2,1,0:T(8,128)(2,1)S(1)} %edge.6.refs_0_), channel_id=1, source_target_pairs={{0,7},{1,2},{2,1},{3,4},{4,3},{5,6},{6,5},{7,0},{8,15},{9,10},{10,... | collective-permute-start | bytes 294920 | tf_op jit(solution)/shard_map/ppermute | solution.py:265
  13.1 1.8 %collective-permute-done.1.outer_ref = bf16[3,128,128]{2,1,0:T(8,128)(2,1)S(1)} collective-permute-done((bf16[3,128,128]{2,1,0:T(8,128)(2,1)S(1)}, bf16[3,128,128]{2,1,0:T(8,128)(2,1)S(1)}, u32[]{:S(2)}, u32[]{:S(2)}) %collective-permute-start.1) | collective-permute-done | bytes 98336 | tf_op jit(solution)/shard_map/ppermute | solution.py:251
  14.9 0.8 %dress.2.refs_0_ = bf16[256,1152]{1,0:T(8,128)(2,1)S(1)} custom-call(bf16[3,2,3]{2,1,0:T(2,128)(2,1)S(1)} %bitcast.8, bf16[3,128,384]{2,1,0:T(8,128)(2,1)S(1)} %multiply_bitcast_fusion.full_ref.own_ref.refs_2_, bf16[3,128,128]{2,1,0:T(8,128)(2,1)S(1)} %collective-permute-done.inner_ref, bf16[3,128,128]{2,1,0:T(8,128)(2,1)S(1)} %collective-permute-done.1.outer_ref, ...), custom_call_target="tpu_custom_call" | custom-call | tf_op jit(solution)/shard_map/dress/pallas_call | solution.py:22
  15.8 0.4 %collective-permute-start.3 = (bf16[3,128,128]{2,1,0:T(8,128)(2,1)S(1)}, bf16[3,128,128]{2,1,0:T(8,128)(2,1)S(1)}, u32[]{:S(2)}, u32[]{:S(2)}) collective-permute-start(bf16[3,128,128]{2,1,0:T(8,128)(2,1)S(1)} %edge.7), channel_id=1, source_target_pairs={{0,1},{1,0},{2,3},{3,2},{4,5},{5,4},{6,7},{7,6},{8,9},{9,8},{10,11... | collective-permute-start | bytes 294920 | tf_op jit(solution)/shard_map/ppermute | solution.py:266
  16.1 2.1 %collective-permute-done.4.outer_ref = bf16[3,128,128]{2,1,0:T(8,128)(2,1)S(1)} collective-permute-done((bf16[3,128,128]{2,1,0:T(8,128)(2,1)S(1)}, bf16[3,128,128]{2,1,0:T(8,128)(2,1)S(1)}, u32[]{:S(2)}, u32[]{:S(2)}) %collective-permute-start.4) | collective-permute-done | bytes 98336 | tf_op jit(solution)/shard_map/ppermute | solution.py:265
  18.2 0.0 collective-permute-done.3.inner_ref
  18.2 0.8 %dress.3.refs_1_ = bf16[256,1152]{1,0:T(8,128)(2,1)S(1)} custom-call(bf16[3,2,3]{2,1,0:T(2,128)(2,1)S(1)} %bitcast.9, bf16[3,128,384]{2,1,0:T(8,128)(2,1)S(1)} %collective-permute-done.2.full_ref.own_ref.refs_3_, bf16[3,128,128]{2,1,0:T(8,128)(2,1)S(1)} %collective-permute-done.3.inner_ref, bf16[3,128,128]{2,1,0:T(8,128)(2,1)S(1)} %collective-permute-done.4.outer_ref, ...), custom_call_target="tpu_custom_call" | custom-call | tf_op jit(solution)/shard_map/dress/pallas_call | solution.py:22
  19.1 0.6 %share.2 = (f32[4,64,512]{2,1,0:T(8,128)S(1)}, bf16[4,64,512]{2,1,0:T(8,128)(2,1)S(1)}) custom-call(bf16[256,1152]{1,0:T(8,128)(2,1)S(1)} %dress.2.refs_0_, bf16[256,1152]{1,0:T(8,128)(2,1)S(1)} %dress.3.refs_1_, bf16[3,128,384]{2,1,0:T(8,128)(2,1)S(1)} %multiply_bitcast_fusion.full_ref.own_ref.refs_2_, ...), custom_call_target="tpu_custom_call" | custom-call | tf_op jit(solution)/shard_map/share/pallas_call | solution.py:22
  19.6 0.0 collective-permute-done.6.refs_3_
  19.6 0.6 %share.3 = (f32[4,64,512]{2,1,0:T(8,128)S(1)}, bf16[4,64,512]{2,1,0:T(8,128)(2,1)S(1)}) custom-call(bf16[256,1152]{1,0:T(8,128)(2,1)S(1)} %dress.2.refs_0_, bf16[256,1152]{1,0:T(8,128)(2,1)S(1)} %dress.3.refs_1_, bf16[3,128,384]{2,1,0:T(8,128)(2,1)S(1)} %collective-permute-done.5.refs_2_, bf16[3,128,384]{2,1,0:T(8,128)(2,1)S(1)} %collective-permute-done.6.refs_3_, ...), custom_call_target="tpu_custom_call" | custom-call | tf_op jit(solution)/shard_map/share/pallas_call | solution.py:22
  20.2 0.1 collective-permute-start.7
  20.3 1.5 %collective-permute-done.7.got_ref = bf16[4,64,512]{2,1,0:T(8,128)(2,1)S(1)} collective-permute-done((bf16[4,64,512]{2,1,0:T(8,128)(2,1)S(1)}, bf16[4,64,512]{2,1,0:T(8,128)(2,1)S(1)}, u32[]{:S(2)}, u32[]{:S(2)}) %collective-permute-start.7) | collective-permute-done | bytes 262176 | tf_op jit(solution)/shard_map/ppermute | solution.py:293
  21.8 1.7 %collective-permute-start.11 = (bf16[64,256]{1,0:T(8,128)(2,1)S(1)}, bf16[64,256]{1,0:T(8,128)(2,1)S(1)}, u32[]{:S(2)}, u32[]{:S(2)}) collective-permute-start(bf16[64,256]{1,0:T(8,128)(2,1)S(1)} %get-tuple-element.26), channel_id=1, source_target_pairs={{0,6},{1,7},{2,4},{3,5},{4,2},{5,3},{6,0},{7,1},{8,14},{9,15},{10,... | collective-permute-start | bytes 98312 | tf_op jit(solution)/shard_map/ppermute | solution.py:288
  23.6 0.4 %collective-permute-start.12 = (bf16[64,256]{1,0:T(8,128)(2,1)S(1)}, bf16[64,256]{1,0:T(8,128)(2,1)S(1)}, u32[]{:S(2)}, u32[]{:S(2)}) collective-permute-start(bf16[64,256]{1,0:T(8,128)(2,1)S(1)} %get-tuple-element.27), channel_id=1, source_target_pairs={{0,4},{1,5},{2,6},{3,7},{4,0},{5,1},{6,2},{7,3},{8,12},{9,13},{10,... | collective-permute-start | bytes 98312 | tf_op jit(solution)/shard_map/ppermute | solution.py:288
  24.0 1.4 %collective-permute-start.13 = (bf16[64,256]{1,0:T(8,128)(2,1)S(1)}, bf16[64,256]{1,0:T(8,128)(2,1)S(1)}, u32[]{:S(2)}, u32[]{:S(2)}) collective-permute-start(bf16[64,256]{1,0:T(8,128)(2,1)S(1)} %get-tuple-element.28), channel_id=1, source_target_pairs={{0,2},{1,3},{2,0},{3,1},{4,6},{5,7},{6,4},{7,5},{8,10},{9,11},{10,... | collective-permute-start | bytes 98312 | tf_op jit(solution)/shard_map/ppermute | solution.py:288
  25.4 1.6 %collective-permute-start.8 = (bf16[64,256]{1,0:T(8,128)(2,1)S(1)}, bf16[64,256]{1,0:T(8,128)(2,1)S(1)}, u32[]{:S(2)}, u32[]{:S(2)}) collective-permute-start(bf16[64,256]{1,0:T(8,128)(2,1)S(1)} %get-tuple-element.22), channel_id=1, source_target_pairs={{0,6},{1,7},{2,4},{3,5},{4,2},{5,3},{6,0},{7,1},{8,14},{9,15},{10,... | collective-permute-start | bytes 98312 | tf_op jit(solution)/shard_map/ppermute | solution.py:288
  27.0 0.4 %collective-permute-start.9 = (bf16[64,256]{1,0:T(8,128)(2,1)S(1)}, bf16[64,256]{1,0:T(8,128)(2,1)S(1)}, u32[]{:S(2)}, u32[]{:S(2)}) collective-permute-start(bf16[64,256]{1,0:T(8,128)(2,1)S(1)} %get-tuple-element.23), channel_id=1, source_target_pairs={{0,4},{1,5},{2,6},{3,7},{4,0},{5,1},{6,2},{7,3},{8,12},{9,13},{10,... | collective-permute-start | bytes 98312 | tf_op jit(solution)/shard_map/ppermute | solution.py:288
  27.5 1.4 %collective-permute-start.10 = (bf16[64,256]{1,0:T(8,128)(2,1)S(1)}, bf16[64,256]{1,0:T(8,128)(2,1)S(1)}, u32[]{:S(2)}, u32[]{:S(2)}) collective-permute-start(bf16[64,256]{1,0:T(8,128)(2,1)S(1)} %get-tuple-element.24), channel_id=1, source_target_pairs={{0,2},{1,3},{2,0},{3,1},{4,6},{5,7},{6,4},{7,5},{8,10},{9,11},{10,... | collective-permute-start | bytes 98312 | tf_op jit(solution)/shard_map/ppermute | solution.py:288
  28.9 3.4 %collective-permute-start.14 = (bf16[2,64,128]{2,1,0:T(8,128)(2,1)S(1)}, bf16[2,64,128]{2,1,0:T(8,128)(2,1)S(1)}, u32[]{:S(2)}, u32[]{:S(2)}) collective-permute-start(bf16[2,64,128]{2,1,0:T(8,128)(2,1)S(1)} %total.2), channel_id=1, source_target_pairs={{0,8},{8,0},{16,24},{24,16},{1,9},{9,1},{17,25},{25,17},{2,10},{10... | collective-permute-start | bytes 98312 | tf_op jit(solution)/shard_map/ppermute | solution.py:295
  32.3 1.9 %collective-permute-done.14.refs_4_ = bf16[2,64,128]{2,1,0:T(8,128)(2,1)S(1)} collective-permute-done((bf16[2,64,128]{2,1,0:T(8,128)(2,1)S(1)}, bf16[2,64,128]{2,1,0:T(8,128)(2,1)S(1)}, u32[]{:S(2)}, u32[]{:S(2)}) %collective-permute-start.14) | collective-permute-done | bytes 32800 | tf_op jit(solution)/shard_map/ppermute | solution.py:295
  34.2 0.7 %total.3 = f32[2,64,128]{2,1,0:T(8,128)} custom-call(f32[64,256]{1,0:T(8,128)S(1)} %get-tuple-element.21.refs_0_, bf16[64,256]{1,0:T(8,128)(2,1)S(1)} %collective-permute-done.8.refs_1_, bf16[64,256]{1,0:T(8,128)(2,1)S(1)} %collective-permute-done.9.refs_2_, bf16[64,256]{1,0:T(8,128)(2,1)S(1)} %collective-permute-done.10.refs_3_, ...), custom_call_target="tpu_custom_call" | custom-call | tf_op jit(solution)/shard_map/total/pallas_call | solution.py:22
  (16 shorter events, 0.2 us)
Async XLA Ops:
  1.7 13.2 %copy-start = (bf16[2,384,384]{2,1,0:T(8,128)(2,1)S(1)}, bf16[2,384,384]{2,1,0:T(8,128)(2,1)}, u32[]{:S(2)}) copy-start(bf16[2,384,384]{2,1,0:T(8,128)(2,1)} %band_ref.3) | copy-start | bytes 1769476
  1.7 10.9 %collective-permute-start.2 = (bf16[3,128,384]{2,1,0:T(8,128)(2,1)S(1)}, bf16[3,128,384]{2,1,0:T(8,128)(2,1)S(1)}, u32[]{:S(2)}, u32[]{:S(2)}) collective-permute-start(bf16[3,128,384]{2,1,0:T(8,128)(2,1)S(1)} %multiply_bitcast_fusion.full_ref.own_ref.refs_2_), channel_id=1, source_target_pairs={{0,8},{8,0},{16,24},{24,16},{1,9},{9,1},{17,25},{25,17},{2,10},{10... | collective-permute-start | bytes 884744 | tf_op jit(solution)/shard_map/ppermute | solution.py:261
  4.8 14.8 %collective-permute-start.6 = (bf16[3,128,384]{2,1,0:T(8,128)(2,1)S(1)}, bf16[3,128,384]{2,1,0:T(8,128)(2,1)S(1)}, u32[]{:S(2)}, u32[]{:S(2)}) collective-permute-start(bf16[3,128,384]{2,1,0:T(8,128)(2,1)S(1)} %multiply_bitcast_fusion.full_ref.own_ref.refs_2_), channel_id=1, source_target_pairs={{8,16},{16,8},{0,0},{24,24},{9,17},{17,9},{1,1},{25,25},{10,18},{1... | collective-permute-start | bytes 884744 | tf_op jit(solution)/shard_map/ppermute | solution.py:260
  5.5 14.1 %collective-permute-start.5 = (bf16[3,128,384]{2,1,0:T(8,128)(2,1)S(1)}, bf16[3,128,384]{2,1,0:T(8,128)(2,1)S(1)}, u32[]{:S(2)}, u32[]{:S(2)}) collective-permute-start(bf16[3,128,384]{2,1,0:T(8,128)(2,1)S(1)} %multiply_bitcast_fusion.full_ref.own_ref.refs_2_), channel_id=1, source_target_pairs={{0,16},{24,8},{8,0},{16,24},{1,17},{25,9},{9,1},{17,25},{2,18},{26... | collective-permute-start | bytes 884744 | tf_op jit(solution)/shard_map/ppermute | solution.py:262
  9.4 3.7 %collective-permute-start = (bf16[3,128,128]{2,1,0:T(8,128)(2,1)S(1)}, bf16[3,128,128]{2,1,0:T(8,128)(2,1)S(1)}, u32[]{:S(2)}, u32[]{:S(2)}) collective-permute-start(bf16[3,128,128]{2,1,0:T(8,128)(2,1)S(1)} %edge.4), channel_id=1, source_target_pairs={{0,1},{1,0},{2,3},{3,2},{4,5},{5,4},{6,7},{7,6},{8,9},{9,8},{10,11... | collective-permute-start | bytes 294920 | tf_op jit(solution)/shard_map/ppermute | solution.py:251
  9.5 5.4 %collective-permute-start.1 = (bf16[3,128,128]{2,1,0:T(8,128)(2,1)S(1)}, bf16[3,128,128]{2,1,0:T(8,128)(2,1)S(1)}, u32[]{:S(2)}, u32[]{:S(2)}) collective-permute-start(bf16[3,128,128]{2,1,0:T(8,128)(2,1)S(1)} %edge.5), channel_id=1, source_target_pairs={{0,7},{1,2},{2,1},{3,4},{4,3},{5,6},{6,5},{7,0},{8,15},{9,10},{10,... | collective-permute-start | bytes 294920 | tf_op jit(solution)/shard_map/ppermute | solution.py:251
  12.7 2.2 %copy-start.1 = (bf16[2,3,3]{2,0,1:T(2,128)(2,1)S(1)}, bf16[2,3,3]{2,0,1:T(2,128)(2,1)}, u32[]{:S(2)}) copy-start(bf16[2,3,3]{2,0,1:T(2,128)(2,1)} %param.5) | copy-start | bytes 112
  12.7 5.5 %collective-permute-start.4 = (bf16[3,128,128]{2,1,0:T(8,128)(2,1)S(1)}, bf16[3,128,128]{2,1,0:T(8,128)(2,1)S(1)}, u32[]{:S(2)}, u32[]{:S(2)}) collective-permute-start(bf16[3,128,128]{2,1,0:T(8,128)(2,1)S(1)} %edge.6.refs_0_), channel_id=1, source_target_pairs={{0,7},{1,2},{2,1},{3,4},{4,3},{5,6},{6,5},{7,0},{8,15},{9,10},{10,... | collective-permute-start | bytes 294920 | tf_op jit(solution)/shard_map/ppermute | solution.py:265
  15.8 2.5 %collective-permute-start.3 = (bf16[3,128,128]{2,1,0:T(8,128)(2,1)S(1)}, bf16[3,128,128]{2,1,0:T(8,128)(2,1)S(1)}, u32[]{:S(2)}, u32[]{:S(2)}) collective-permute-start(bf16[3,128,128]{2,1,0:T(8,128)(2,1)S(1)} %edge.7), channel_id=1, source_target_pairs={{0,1},{1,0},{2,3},{3,2},{4,5},{5,4},{6,7},{7,6},{8,9},{9,8},{10,11... | collective-permute-start | bytes 294920 | tf_op jit(solution)/shard_map/ppermute | solution.py:266
  20.2 1.6 %collective-permute-start.7 = (bf16[4,64,512]{2,1,0:T(8,128)(2,1)S(1)}, bf16[4,64,512]{2,1,0:T(8,128)(2,1)S(1)}, u32[]{:S(2)}, u32[]{:S(2)}) collective-permute-start(bf16[4,64,512]{2,1,0:T(8,128)(2,1)S(1)} %get-tuple-element.20), channel_id=1, source_target_pairs={{0,1},{1,0},{2,3},{3,2},{4,5},{5,4},{6,7},{7,6},{8,9},{9,8},{10,11... | collective-permute-start | bytes 786440 | tf_op jit(solution)/shard_map/ppermute | solution.py:293
  21.8 5.6 %collective-permute-start.11 = (bf16[64,256]{1,0:T(8,128)(2,1)S(1)}, bf16[64,256]{1,0:T(8,128)(2,1)S(1)}, u32[]{:S(2)}, u32[]{:S(2)}) collective-permute-start(bf16[64,256]{1,0:T(8,128)(2,1)S(1)} %get-tuple-element.26), channel_id=1, source_target_pairs={{0,6},{1,7},{2,4},{3,5},{4,2},{5,3},{6,0},{7,1},{8,14},{9,15},{10,... | collective-permute-start | bytes 98312 | tf_op jit(solution)/shard_map/ppermute | solution.py:288
  23.6 5.3 %collective-permute-start.12 = (bf16[64,256]{1,0:T(8,128)(2,1)S(1)}, bf16[64,256]{1,0:T(8,128)(2,1)S(1)}, u32[]{:S(2)}, u32[]{:S(2)}) collective-permute-start(bf16[64,256]{1,0:T(8,128)(2,1)S(1)} %get-tuple-element.27), channel_id=1, source_target_pairs={{0,4},{1,5},{2,6},{3,7},{4,0},{5,1},{6,2},{7,3},{8,12},{9,13},{10,... | collective-permute-start | bytes 98312 | tf_op jit(solution)/shard_map/ppermute | solution.py:288
  24.0 4.9 %collective-permute-start.13 = (bf16[64,256]{1,0:T(8,128)(2,1)S(1)}, bf16[64,256]{1,0:T(8,128)(2,1)S(1)}, u32[]{:S(2)}, u32[]{:S(2)}) collective-permute-start(bf16[64,256]{1,0:T(8,128)(2,1)S(1)} %get-tuple-element.28), channel_id=1, source_target_pairs={{0,2},{1,3},{2,0},{3,1},{4,6},{5,7},{6,4},{7,5},{8,10},{9,11},{10,... | collective-permute-start | bytes 98312 | tf_op jit(solution)/shard_map/ppermute | solution.py:288
  25.4 6.9 %collective-permute-start.8 = (bf16[64,256]{1,0:T(8,128)(2,1)S(1)}, bf16[64,256]{1,0:T(8,128)(2,1)S(1)}, u32[]{:S(2)}, u32[]{:S(2)}) collective-permute-start(bf16[64,256]{1,0:T(8,128)(2,1)S(1)} %get-tuple-element.22), channel_id=1, source_target_pairs={{0,6},{1,7},{2,4},{3,5},{4,2},{5,3},{6,0},{7,1},{8,14},{9,15},{10,... | collective-permute-start | bytes 98312 | tf_op jit(solution)/shard_map/ppermute | solution.py:288
  27.0 5.3 %collective-permute-start.9 = (bf16[64,256]{1,0:T(8,128)(2,1)S(1)}, bf16[64,256]{1,0:T(8,128)(2,1)S(1)}, u32[]{:S(2)}, u32[]{:S(2)}) collective-permute-start(bf16[64,256]{1,0:T(8,128)(2,1)S(1)} %get-tuple-element.23), channel_id=1, source_target_pairs={{0,4},{1,5},{2,6},{3,7},{4,0},{5,1},{6,2},{7,3},{8,12},{9,13},{10,... | collective-permute-start | bytes 98312 | tf_op jit(solution)/shard_map/ppermute | solution.py:288
  27.5 4.8 %collective-permute-start.10 = (bf16[64,256]{1,0:T(8,128)(2,1)S(1)}, bf16[64,256]{1,0:T(8,128)(2,1)S(1)}, u32[]{:S(2)}, u32[]{:S(2)}) collective-permute-start(bf16[64,256]{1,0:T(8,128)(2,1)S(1)} %get-tuple-element.24), channel_id=1, source_target_pairs={{0,2},{1,3},{2,0},{3,1},{4,6},{5,7},{6,4},{7,5},{8,10},{9,11},{10,... | collective-permute-start | bytes 98312 | tf_op jit(solution)/shard_map/ppermute | solution.py:288
  28.9 5.3 %collective-permute-start.14 = (bf16[2,64,128]{2,1,0:T(8,128)(2,1)S(1)}, bf16[2,64,128]{2,1,0:T(8,128)(2,1)S(1)}, u32[]{:S(2)}, u32[]{:S(2)}) collective-permute-start(bf16[2,64,128]{2,1,0:T(8,128)(2,1)S(1)} %total.2), channel_id=1, source_target_pairs={{0,8},{8,0},{16,24},{24,16},{1,9},{9,1},{17,25},{25,17},{2,10},{10... | collective-permute-start | bytes 98312 | tf_op jit(solution)/shard_map/ppermute | solution.py:295
